TPU v7x, 512 devices: a whole 4x4x16 slice. The times are simulated.
512 devices in a mesh: inst: 64 (over x, y, z_hi, core), tensor: 8 (over z_lo).
Axes of the slice: x: 4, y: 4, z: 16 (z_hi: 2, z_lo: 8; z = z_hi * 8 + z_lo), core: 2. Of those that a mesh axis runs over, the one named last changes fastest.
Arguments:
- hidden_rows: bfloat16 [32768, 8192], P('inst', 'tensor'), may hold values from -50 to 50
- kv_weight: bfloat16 [8192, 2048], P('tensor'), may hold values from -0.0625 to 0.0625
- norm_gain: float32 [8192], P('tensor'), may hold values from 0.5 to 2
- resident_cache: bfloat16 [2048, 16384], P('tensor', 'inst'), may hold values from -12 to 12
- queries: bfloat16 [2, 1024, 8192], P(None, 'inst', 'tensor'), may hold values from -160 to 160
- fresh_hidden: bfloat16 [2, 1024, 8192], P(None, 'inst', 'tensor'), may hold values from -50 to 50
- move_dest: int32 [2048], P('inst'), may hold values from 0 to 63, as said below
- move_len: int32 [2048], P('inst'), may hold values from 1 to 16
- resident_len: int32 [1024], P('inst'), may hold values from 1 to 16
- decode_ids: int32 [1024], P('inst'), may hold values from 0 to 47, as said below
Outputs:
- rebuilt: bfloat16 [2048, 32768], P('tensor', 'inst')
- attended: bfloat16 [2, 1024, 8192], P(None, 'inst', 'tensor')
Inputs may be any that keep to these rules, and one draw needn't show every extreme that they name: `move_dest`: each instance sends its 32 requests to 32 different instances, never to itself, and receives exactly 32 requests, each from a different instance. `decode_ids`: the 16 entries of one instance are different; 0 to 15 name its staying requests, 16 + a its arrived request a.
All inputs are finite; a program needn't handle non-finite values.
Results may differ from a plain program's by a relative error of at most 0.019.
Values may be sent and summed in bfloat16 or wider, within the bound.
No kernel may reach another device: no remote copies, remote signals or barrier semaphores. Data moves between devices by JAX's collectives and lax.ppermute only.
A program may use at most 64 MiB of HBM per device.

v0:
```python
import jax
import jax.numpy as jnp
from jax import lax
from jax.sharding import PartitionSpec as P

D = 8192
GROUP = 8
HD = 128
STEPS = 2


def project(source_rows, kv_weight, norm_gain):
    widened = source_rows.astype(jnp.float32)
    squares = lax.psum(jnp.sum(widened * widened, axis=1), "tensor")
    scaled = (widened * norm_gain).astype(jnp.bfloat16)
    summed = lax.psum_scatter(
        lax.dot_general(
            kv_weight, scaled, (((0,), (1,)), ((), ())), preferred_element_type=jnp.float32
        ).astype(jnp.bfloat16),
        "tensor",
        scatter_dimension=0,
        tiled=True,
    ).astype(jnp.float32)
    return (summed * lax.rsqrt(squares / D + 1e-06)[None, :]).astype(jnp.bfloat16)


def fresh_partial(fresh_rows, kv_weight, norm_gain):
    widened = fresh_rows.astype(jnp.float32)
    scaled = (widened * norm_gain).astype(jnp.bfloat16)
    return (
        jnp.dot(scaled, kv_weight, preferred_element_type=jnp.float32),
        jnp.sum(widened * widened, axis=1),
    )


def fresh_finish(partial_value, squares, owned):
    offset = lax.axis_index("tensor") * owned
    picked = lax.dynamic_slice_in_dim(partial_value, offset, owned, 1)
    return (picked * lax.rsqrt(squares / D + 1e-06)[:, None]).astype(jnp.bfloat16)


def arrivals(arrived_len, requests):
    senders = arrived_len.shape[0]
    living = (arrived_len > 0).astype(jnp.int32)
    ranking = jnp.cumsum(living) - 1
    picked = living[None, :] * (
        ranking[None, :] == jnp.arange(requests, dtype=jnp.int32)[:, None]
    ).astype(jnp.int32)
    source = jnp.sum(picked * jnp.arange(senders, dtype=jnp.int32)[None, :], axis=1)
    return (source, jnp.sum(picked * arrived_len[None, :], axis=1))


def attend(query_step, cache_keys, cache_values, fresh_keys, fresh_values, valid):
    scale = 1.0 / HD**0.5
    cached = (
        jnp.einsum("bhgd,hdbp->bhgp", query_step, cache_keys, preferred_element_type=jnp.float32)
        * scale
    )
    recent = (
        jnp.einsum("bhgd,tbhd->bhgt", query_step, fresh_keys, preferred_element_type=jnp.float32)
        * scale
    )
    masking = valid[:, None, None, :]
    cached = jnp.where(masking, cached, -1e30)
    highest = jnp.maximum(jnp.max(cached, axis=-1), jnp.max(recent, axis=-1))
    cached_exp = jnp.where(masking, jnp.exp(cached - highest[..., None]), 0.0)
    recent_exp = jnp.exp(recent - highest[..., None])
    denominator = jnp.sum(cached_exp, axis=-1) + jnp.sum(recent_exp, axis=-1)
    cached_prob = (cached_exp / denominator[..., None]).astype(jnp.bfloat16)
    recent_prob = (recent_exp / denominator[..., None]).astype(jnp.bfloat16)
    output = jnp.einsum(
        "bhgp,hdbp->bhgd", cached_prob, cache_values, preferred_element_type=jnp.float32
    )
    output = output + jnp.einsum(
        "bhgt,tbhd->bhgd", recent_prob, fresh_values, preferred_element_type=jnp.float32
    )
    return output.astype(jnp.bfloat16).reshape(query_step.shape[0], -1)


def shards(
    hidden_rows,
    kv_weight,
    norm_gain,
    resident_cache,
    queries,
    fresh_hidden,
    move_dest,
    move_len,
    resident_len,
    decode_ids,
):
    requests = move_dest.shape[0]
    context = hidden_rows.shape[0] // requests
    instances = lax.axis_size("inst")
    owned = kv_weight.shape[1] // lax.axis_size("tensor")
    heads_here = owned // (2 * HD)
    batch_rows = decode_ids.shape[0]
    nothing = jnp.zeros((), jnp.bfloat16)
    targets = jnp.arange(instances, dtype=jnp.int32)
    matched = (move_dest[None, :] == targets[:, None]).astype(jnp.int32)
    chosen = jnp.sum(matched * jnp.arange(requests, dtype=jnp.int32)[None, :], axis=1)
    sent_len = jnp.sum(matched * move_len[None, :], axis=1)
    sending = (sent_len > 0)[:, None, None]
    blocks = hidden_rows.reshape(requests, context, -1)
    outgoing = jnp.where(sending, jnp.take(blocks, chosen, axis=0), nothing)
    arrived, arrived_len = (
        lax.all_to_all(outgoing, "inst", split_axis=0, concat_axis=0, tiled=True),
        lax.all_to_all(sent_len, "inst", split_axis=0, concat_axis=0, tiled=True),
    )
    source, kept_len = arrivals(arrived_len, requests)
    gathered_rows = jnp.take(arrived, source, axis=0).reshape(requests * context, -1)
    rebuilt = project(gathered_rows, kv_weight, norm_gain)
    keeping = (jnp.arange(context, dtype=jnp.int32)[None, :] < kept_len[:, None]).reshape(1, -1)
    rebuilt = jnp.where(keeping, rebuilt, nothing)
    fresh_list = []
    for step in range(STEPS):
        partial_value, squares = fresh_partial(fresh_hidden[step], kv_weight, norm_gain)
        partial_value, squares = lax.psum((partial_value, squares), "tensor")
        fresh_list.append(fresh_finish(partial_value, squares, owned))
    fresh_kv = jnp.stack(fresh_list)
    fresh_kv = fresh_kv.reshape(STEPS, batch_rows, heads_here, 2, HD)
    combined = jnp.concatenate([resident_cache, rebuilt], axis=1)
    lengths = jnp.concatenate([resident_len, kept_len])
    positions = (
        decode_ids[:, None] * context + jnp.arange(context, dtype=jnp.int32)[None, :]
    ).reshape(-1)
    gathered = jnp.take(combined, positions, axis=1).reshape(heads_here, 2, HD, batch_rows, context)
    valid = jnp.arange(context, dtype=jnp.int32)[None, :] < jnp.take(lengths, decode_ids)[:, None]
    query_heads = queries.reshape(STEPS, batch_rows, heads_here, GROUP, HD)
    outputs = []
    for step in range(STEPS):
        outputs.append(
            attend(
                query_heads[step],
                gathered[:, 0],
                gathered[:, 1],
                fresh_kv[: step + 1, :, :, 0],
                fresh_kv[: step + 1, :, :, 1],
                valid,
            )
        )
    return (rebuilt, jnp.stack(outputs))


def solution(mesh):
    in_specs = (
        P("inst", "tensor"),
        P("tensor", None),
        P("tensor"),
        P("tensor", "inst"),
        P(None, "inst", "tensor"),
        P(None, "inst", "tensor"),
        P("inst"),
        P("inst"),
        P("inst"),
        P("inst"),
    )
    out_specs = (P("tensor", "inst"), P(None, "inst", "tensor"))
    return jax.shard_map(shards, mesh=mesh, in_specs=in_specs, out_specs=out_specs, check_vma=False)
```

profile of v0, /device:TPU:2, one launch (start us, length us, event | category | flops | bytes accessed | tf_op | source)
XLA Modules:
  0.0 298.0 jit_solution(8934084800445112663)
XLA Ops:
  7.2 0.8 select_reduce_fusion.1
  8.0 0.7 copy.40
  8.7 21.3 %all-to-all-start = ((s32[64,1,1]{2,1,0:T(1,128)}), s32[64,1,1]{2,1,0:T(1,128)S(1)}, u32[]{:S(2)}, u32[]{:S(2)}) async-start(s32[64,1,1]{2,1,0:T(1,128)} %copy.40), calls=%async_computation | async-start | bytes 65536 | tf_op jit(solution)/shard_map/all_to_all | solution.py:108
  30.1 0.7 gather_fusion
  30.8 1.6 select_select_fusion
  32.4 13.3 %all-to-all-done = s32[64,1,1]{2,1,0:T(1,128)S(1)} async-done(((s32[64,1,1]{2,1,0:T(1,128)}), s32[64,1,1]{2,1,0:T(1,128)S(1)}, u32[]{:S(2)}, u32[]{:S(2)}) %all-to-all-start) | async-done | bytes 288 | tf_op jit(solution)/shard_map/all_to_all | solution.py:108
  45.7 6.5 %all-to-all-start.1 = ((bf16[64,16,1024]{2,1,0:T(8,128)(2,1)}), bf16[64,16,1024]{2,1,0:T(8,128)(2,1)}, u32[]{:S(2)}, u32[]{:S(2)}) async-start(bf16[64,16,1024]{2,1,0:T(8,128)(2,1)} %select_select_fusion), calls=%async_computation.1 | async-start | bytes 4194304 | tf_op jit(solution)/shard_map/all_to_all | solution.py:107
  52.3 3.7 %fusion.19 = f32[16,2048]{1,0:T(8,128)} fusion(bf16[1024,2048]{1,0:T(8,128)(2,1)} %param.11, f32[1024]{0:T(1024)S(1)} %copy-done.5, bf16[2,16,1024]{2,1,0:T(8,128)(2,1)S(1)} %copy-done.2), kind=kOutput, calls=%fused_computation.47 | convolution fusion | flops 67158016 | bytes 4362240 | tf_op jit(solution)/shard_map/dot_general | solution.py:31
  55.9 1.3 fusion.17
  57.5 1.2 reduce.14
  59.1 46.7 %all-to-all-done.1 = bf16[64,16,1024]{2,1,0:T(8,128)(2,1)} async-done(((bf16[64,16,1024]{2,1,0:T(8,128)(2,1)}), bf16[64,16,1024]{2,1,0:T(8,128)(2,1)}, u32[]{:S(2)}, u32[]{:S(2)}) %all-to-all-start.1) | async-done | bytes 2097184 | tf_op jit(solution)/shard_map/all_to_all | solution.py:107
  105.8 2.2 gather_fusion.1
  108.2 5.9 %fusion = bf16[2048,512]{0,1:T(8,128)(2,1)} fusion(bf16[1024,2048]{1,0:T(8,128)(2,1)} %param.11, bf16[512,1024]{1,0:T(8,128)(2,1)S(1)} %bitcast_select_fusion, f32[1024]{0:T(1024)S(1)} %copy-done.5), kind=kOutput, calls=%fused_computation.5 | convolution fusion | flops 2150105088 | bytes 7344128 | tf_op jit(solution)/shard_map/dot_general | solution.py:17
  114.2 0.9 copy-done.3
  115.6 0.7 gather_fusion.2
  117.0 80.5 %all-reduce = (f32[512]{0:T(512)S(1)}, f32[16]{0:T(128)S(1)}, f32[16]{0:T(128)S(1)}) all-reduce(f32[512]{0:T(512)S(1)} %reduce_sum.107, f32[16]{0:T(128)S(1)} %get-tuple-element.13, f32[16]{0:T(128)S(1)} %get-tuple-element.12), channel_id=1, replica_groups=mesh['inst'=64,'tensor'=8] {'tensor'}, use_global_device_ids=true, to_apply=%region_7.8 | all-reduce | flops 544 | bytes 4352 | tf_op jit(solution)/shard_map/psum | solution.py:14
  197.6 18.1 %all-reduce.4.cloned.1.call-done = (f32[16,2048]{1,0:T(8,128)}, f32[16,2048]{1,0:T(8,128)}) async-done(((f32[16,2048]{1,0:T(8,128)}, f32[16,2048]{1,0:T(8,128)}), (f32[16,2048]{1,0:T(8,128)}, f32[16,2048]{1,0:T(8,128)})) %all-reduce.4.cloned.1.call-update) | async-done | bytes 262160 | tf_op jit(solution)/shard_map/psum | solution.py:118
  215.6 0.8 multiply_convert_fusion.4
  216.5 0.8 multiply_convert_fusion.3
  217.7 68.0 %reduce-scatter.2.cloned.1.call-done = bf16[256,512]{0,1:T(8,128)(2,1)} async-done(((bf16[2048,512]{0,1:T(8,128)(2,1)}), bf16[256,512]{0,1:T(8,128)(2,1)}) %reduce-scatter.2.cloned.1.call-update) | async-done | bytes 262160 | tf_op jit(solution)/shard_map/reduce_scatter | solution.py:16
  285.7 1.1 fusion.9
  286.9 0.8 copy.47
  287.7 1.2 gather_fusion.3
  290.5 0.6 pad_maximum_fusion.1
  (78 shorter events, 4.2 us)
Async XLA Ops:
  7.2 22.9 %copy-start = (bf16[512,1024]{1,0:T(8,128)(2,1)S(1)}, bf16[512,1024]{1,0:T(8,128)(2,1)}, u32[]{:S(2)}) copy-start(bf16[512,1024]{1,0:T(8,128)(2,1)} %param.10) | copy-start | bytes 3145732
  8.7 37.0 %all-to-all-start = ((s32[64,1,1]{2,1,0:T(1,128)}), s32[64,1,1]{2,1,0:T(1,128)S(1)}, u32[]{:S(2)}, u32[]{:S(2)}) async-start(s32[64,1,1]{2,1,0:T(1,128)} %copy.40), calls=%async_computation | async-start | bytes 65536 | tf_op jit(solution)/shard_map/all_to_all | solution.py:108
  32.4 19.8 %copy-start.2 = (bf16[2,16,1024]{2,1,0:T(8,128)(2,1)S(1)}, bf16[2,16,1024]{2,1,0:T(8,128)(2,1)}, u32[]{:S(2)}) copy-start(bf16[2,16,1024]{2,1,0:T(8,128)(2,1)} %param.15) | copy-start | bytes 196612
  32.4 19.9 %copy-start.5 = (f32[1024]{0:T(1024)S(1)}, f32[1024]{0:T(1024)}, u32[]{:S(2)}) copy-start(f32[1024]{0:T(1024)} %param.12) | copy-start | bytes 12292
  45.7 60.1 %all-to-all-start.1 = ((bf16[64,16,1024]{2,1,0:T(8,128)(2,1)}), bf16[64,16,1024]{2,1,0:T(8,128)(2,1)}, u32[]{:S(2)}, u32[]{:S(2)}) async-start(bf16[64,16,1024]{2,1,0:T(8,128)(2,1)} %select_select_fusion), calls=%async_computation.1 | async-start | bytes 4194304 | tf_op jit(solution)/shard_map/all_to_all | solution.py:107
  52.2 163.5 %all-reduce.4.cloned.1.call-start = ((), (), s32[]{:S(2)}) async-start(), calls=%async_computation.4 | async-start | bytes 524288 | tf_op jit(solution)/shard_map/psum | solution.py:118
  52.3 3.7 %copy-start.1 = (bf16[1024,2048]{1,0:T(8,128)(2,1)S(1)}, bf16[1024,2048]{1,0:T(8,128)(2,1)}, u32[]{:S(2)}) copy-start(bf16[1024,2048]{1,0:T(8,128)(2,1)} %param.11) | copy-start | bytes 12582916
  57.3 228.4 %reduce-scatter.2.cloned.1.call-start = ((), (), s32[]{:S(2)}) async-start(), calls=%async_computation.3 | async-start | bytes 2359296 | tf_op jit(solution)/shard_map/reduce_scatter | solution.py:16
  114.1 0.9 copy-start.3
  114.1 1.0 copy-start.4
  114.1 1.1 copy-start.6
  114.1 1.4 copy-start.7
Sparse Core Ops, SparseCore 0:
  57.4 158.2 all-reduce.3
  218.7 66.9 reduce-scatter.1
where the time goes:
time: 299 us; the launch traced here: 298 us
  waiting for transfers between devices  146 us (49%)
  blocking collectives  80.5 us (27%)
  starting transfers between devices  27.8 us (9%)
  between operations  14.4 us (5%)
  matrix products  12.3 us (4%)
  other arithmetic  8.96 us (3%)
  local copies, waits for them, and re-layouts  7.85 us (3%)
    psum x1, blocking collectives, project(): squares = lax.psum(jnp.sum(widened * widened, axis=1), 'tensor')  80.5 us
    reduce_scatter x1, waiting for transfers between devices, project(): lax.psum_scatter(lax.dot_general(kv_weight, scaled, (((0,), (1,)), ((), (...  68 us
    all_to_all x1, waiting for transfers between devices, shards(): lax.all_to_all(outgoing, 'inst', split_axis=0, concat_axis=0, tiled=True)  46.7 us
    all_to_all x1, starting transfers between devices, shards(): lax.all_to_all(sent_len, 'inst', split_axis=0, concat_axis=0, tiled=True)  21.3 us
    psum x1, waiting for transfers between devices, shards(): partial_value, squares = lax.psum((partial_value, squares), 'tensor')  18.1 us
    all_to_all x1, waiting for transfers between devices, shards(): lax.all_to_all(sent_len, 'inst', split_axis=0, concat_axis=0, tiled=True)  13.3 us
    all_to_all x1, starting transfers between devices, shards(): lax.all_to_all(outgoing, 'inst', split_axis=0, concat_axis=0, tiled=True)  6.48 us
  transfers between devices with their start and end apart: 4, of which 4 were waited for; matrix products, arithmetic and copies ran while one was open for 7% of the time, Pallas kernels for 0%

commit v1 on v0

--- a/solution.py
+++ b/solution.py
@@ -9,34 +9,22 @@
 STEPS = 2
 
 
-def project(source_rows, kv_weight, norm_gain):
-    widened = source_rows.astype(jnp.float32)
-    squares = lax.psum(jnp.sum(widened * widened, axis=1), "tensor")
+def partial_sums(rows, kv_weight, norm_gain):
+    widened = rows.astype(jnp.float32)
+    squares = jnp.sum(widened * widened, axis=1)
     scaled = (widened * norm_gain).astype(jnp.bfloat16)
-    summed = lax.psum_scatter(
-        lax.dot_general(
-            kv_weight, scaled, (((0,), (1,)), ((), ())), preferred_element_type=jnp.float32
-        ).astype(jnp.bfloat16),
-        "tensor",
-        scatter_dimension=0,
-        tiled=True,
-    ).astype(jnp.float32)
-    return (summed * lax.rsqrt(squares / D + 1e-06)[None, :]).astype(jnp.bfloat16)
+    partial_value = jnp.dot(scaled, kv_weight, preferred_element_type=jnp.float32)
+    return partial_value.astype(jnp.bfloat16), squares
 
 
-def fresh_partial(fresh_rows, kv_weight, norm_gain):
-    widened = fresh_rows.astype(jnp.float32)
-    scaled = (widened * norm_gain).astype(jnp.bfloat16)
-    return (
-        jnp.dot(scaled, kv_weight, preferred_element_type=jnp.float32),
-        jnp.sum(widened * widened, axis=1),
-    )
-
-
-def fresh_finish(partial_value, squares, owned):
-    offset = lax.axis_index("tensor") * owned
-    picked = lax.dynamic_slice_in_dim(partial_value, offset, owned, 1)
-    return (picked * lax.rsqrt(squares / D + 1e-06)[:, None]).astype(jnp.bfloat16)
+def sum_over_tensor(values):
+    tensors = lax.axis_size("tensor")
+    distance = 1
+    while distance < tensors:
+        pairs = [(i, i ^ distance) for i in range(tensors)]
+        values = values + lax.ppermute(values, "tensor", pairs)
+        distance *= 2
+    return values
 
 
 def arrivals(arrived_len, requests):
@@ -91,6 +79,7 @@
 ):
     requests = move_dest.shape[0]
     context = hidden_rows.shape[0] // requests
+    leaving = hidden_rows.shape[0]
     instances = lax.axis_size("inst")
     owned = kv_weight.shape[1] // lax.axis_size("tensor")
     heads_here = owned // (2 * HD)
@@ -101,24 +90,27 @@
     chosen = jnp.sum(matched * jnp.arange(requests, dtype=jnp.int32)[None, :], axis=1)
     sent_len = jnp.sum(matched * move_len[None, :], axis=1)
     sending = (sent_len > 0)[:, None, None]
-    blocks = hidden_rows.reshape(requests, context, -1)
+
+    all_rows = jnp.concatenate(
+        [hidden_rows, fresh_hidden.reshape(STEPS * batch_rows, -1)], axis=0
+    )
+    partial_value, squares = partial_sums(all_rows, kv_weight, norm_gain)
+    raw = lax.psum_scatter(partial_value, "tensor", scatter_dimension=1, tiled=True)
+    squares = sum_over_tensor(squares)
+    arrived_len = lax.all_to_all(sent_len, "inst", split_axis=0, concat_axis=0, tiled=True)
+    source, kept_len = arrivals(arrived_len, requests)
+    kv_rows = (
+        raw.astype(jnp.float32) * lax.rsqrt(squares / D + 1e-06)[:, None]
+    ).astype(jnp.bfloat16)
+    fresh_kv = kv_rows[leaving:].reshape(STEPS, batch_rows, heads_here, 2, HD)
+
+    blocks = kv_rows[:leaving].reshape(requests, context, owned)
     outgoing = jnp.where(sending, jnp.take(blocks, chosen, axis=0), nothing)
-    arrived, arrived_len = (
-        lax.all_to_all(outgoing, "inst", split_axis=0, concat_axis=0, tiled=True),
-        lax.all_to_all(sent_len, "inst", split_axis=0, concat_axis=0, tiled=True),
-    )
-    source, kept_len = arrivals(arrived_len, requests)
-    gathered_rows = jnp.take(arrived, source, axis=0).reshape(requests * context, -1)
-    rebuilt = project(gathered_rows, kv_weight, norm_gain)
-    keeping = (jnp.arange(context, dtype=jnp.int32)[None, :] < kept_len[:, None]).reshape(1, -1)
-    rebuilt = jnp.where(keeping, rebuilt, nothing)
-    fresh_list = []
-    for step in range(STEPS):
-        partial_value, squares = fresh_partial(fresh_hidden[step], kv_weight, norm_gain)
-        partial_value, squares = lax.psum((partial_value, squares), "tensor")
-        fresh_list.append(fresh_finish(partial_value, squares, owned))
-    fresh_kv = jnp.stack(fresh_list)
-    fresh_kv = fresh_kv.reshape(STEPS, batch_rows, heads_here, 2, HD)
+    arrived = lax.all_to_all(outgoing, "inst", split_axis=0, concat_axis=0, tiled=True)
+    gathered_rows = jnp.take(arrived, source, axis=0)
+    keeping = jnp.arange(context, dtype=jnp.int32)[None, :] < kept_len[:, None]
+    rebuilt = jnp.where(keeping[:, :, None], gathered_rows, nothing)
+    rebuilt = rebuilt.reshape(requests * context, owned).T
     combined = jnp.concatenate([resident_cache, rebuilt], axis=1)
     lengths = jnp.concatenate([resident_len, kept_len])
     positions = (

time: 299 us -> 150 us (0.50)
  the two profiles are of different devices: /device:TPU:2 before, /device:TPU:1 now
where the time goes in v1:
time: 150 us; the launch traced here: 149 us
  waiting for transfers between devices  62.8 us (42%)
  starting transfers between devices  52.2 us (35%)
  between operations  14.5 us (10%)
  matrix products  7.84 us (5%)
  local copies, waits for them, and re-layouts  6.31 us (4%)
  other arithmetic  5.69 us (4%)
    all_to_all x1, waiting for transfers between devices, shards(): lax.all_to_all(outgoing, 'inst', split_axis=0, concat_axis=0, tiled=True)  25.9 us
    all_to_all x1, starting transfers between devices, shards(): lax.all_to_all(sent_len, 'inst', split_axis=0, concat_axis=0, tiled=True)  20.8 us
    all_to_all x1, starting transfers between devices, shards(): lax.all_to_all(outgoing, 'inst', split_axis=0, concat_axis=0, tiled=True)  19.2 us
    all_to_all x1, waiting for transfers between devices, shards(): lax.all_to_all(sent_len, 'inst', split_axis=0, concat_axis=0, tiled=True)  16.4 us
    reduce_scatter x1, waiting for transfers between devices, shards(): lax.psum_scatter(partial_value, 'tensor', scatter_dimension=1, tiled=True)  13.9 us
    ppermute x3, starting transfers between devices, sum_over_tensor(): values = values + lax.ppermute(values, 'tensor', pairs)  12.1 us
    ppermute x3, waiting for transfers between devices, sum_over_tensor(): values = values + lax.ppermute(values, 'tensor', pairs)  6.53 us
    dot_general x1, matrix products, partial_sums(): jnp.dot(scaled, kv_weight, preferred_element_type=jnp.float32)  6.42 us
  transfers between devices with their start and end apart: 6, of which 5 were waited for; matrix products, arithmetic and copies ran while one was open for 3% of the time, Pallas kernels for 0%

profile of v1, /device:TPU:1, one launch (start us, length us, event | category | flops | bytes accessed | tf_op | source)
XLA Modules:
  0.0 149.3 jit_solution(3625024184656599679)
XLA Ops:
  7.2 6.4 %convolution_convert_fusion = bf16[544,2048]{1,0:T(8,128)(2,1)} fusion(bf16[1024,2048]{1,0:T(8,128)(2,1)} %param.11, f32[1024]{0:T(1024)} %param.12, bf16[32,1024]{1,0:T(8,128)(2,1)} %bitcast.77, bf16[512,1024]{1,0:T(8,128)(2,1)} %param.10), kind=kOutput, calls=%fused_computation.4 | convolution fusion | flops 2286157824 | bytes 7540736 | tf_op jit(solution)/shard_map/dot_general | solution.py:16
  13.7 1.1 copy-done
  14.9 0.3 fusion.1
  15.2 4.4 %collective-permute-start = (f32[544]{0:T(1024)S(1)}, f32[544]{0:T(1024)S(1)}, u32[]{:S(2)}, u32[]{:S(2)}) collective-permute-start(f32[544]{0:T(1024)S(1)} %fusion.1), channel_id=1, source_target_pairs={{0,1},{1,0},{2,3},{3,2},{4,5},{5,4},{6,7},{7,6},{8,9},{9,8},{10,11... | collective-permute-start | bytes 6536 | tf_op jit(solution)/shard_map/ppermute | solution.py:25
  19.7 0.7 copy.40
  20.4 20.8 %all-to-all-start = ((s32[64,1,1]{2,1,0:T(1,128)}), s32[64,1,1]{2,1,0:T(1,128)S(1)}, u32[]{:S(2)}, u32[]{:S(2)}) async-start(s32[64,1,1]{2,1,0:T(1,128)} %copy.40), calls=%async_computation | async-start | bytes 65536 | tf_op jit(solution)/shard_map/all_to_all | solution.py:100
  41.4 16.4 %all-to-all-done = s32[64,1,1]{2,1,0:T(1,128)S(1)} async-done(((s32[64,1,1]{2,1,0:T(1,128)}), s32[64,1,1]{2,1,0:T(1,128)S(1)}, u32[]{:S(2)}, u32[]{:S(2)}) %all-to-all-start) | async-done | bytes 288 | tf_op jit(solution)/shard_map/all_to_all | solution.py:100
  58.0 1.2 reduce.13
  59.5 3.7 %collective-permute-start.1 = (f32[544]{0:T(1024)S(1)}, f32[544]{0:T(1024)S(1)}, u32[]{:S(2)}, u32[]{:S(2)}) collective-permute-start(f32[544]{0:T(1024)S(1)} %add.145), channel_id=1, source_target_pairs={{0,2},{1,3},{2,0},{3,1},{4,6},{5,7},{6,4},{7,5},{8,10},{9,11},{10,... | collective-permute-start | bytes 6536 | tf_op jit(solution)/shard_map/ppermute | solution.py:25
  63.3 0.7 gather_fusion.2
  64.0 1.8 %collective-permute-done.1 = f32[544]{0:T(1024)S(1)} collective-permute-done((f32[544]{0:T(1024)S(1)}, f32[544]{0:T(1024)S(1)}, u32[]{:S(2)}, u32[]{:S(2)}) %collective-permute-start.1) | collective-permute-done | bytes 2208 | tf_op jit(solution)/shard_map/ppermute | solution.py:25
  65.8 4.0 %collective-permute-start.2 = (f32[544]{0:T(1024)S(1)}, f32[544]{0:T(1024)S(1)}, u32[]{:S(2)}, u32[]{:S(2)}) collective-permute-start(f32[544]{0:T(1024)S(1)} %add.146), channel_id=1, source_target_pairs={{0,4},{1,5},{2,6},{3,7},{4,0},{5,1},{6,2},{7,3},{8,12},{9,13},{10,... | collective-permute-start | bytes 6536 | tf_op jit(solution)/shard_map/ppermute | solution.py:25
  69.9 4.7 %collective-permute-done.2 = f32[544]{0:T(1024)S(1)} collective-permute-done((f32[544]{0:T(1024)S(1)}, f32[544]{0:T(1024)S(1)}, u32[]{:S(2)}, u32[]{:S(2)}) %collective-permute-start.2) | collective-permute-done | bytes 2208 | tf_op jit(solution)/shard_map/ppermute | solution.py:25
  74.6 13.9 %reduce-scatter.2.cloned.1.call-done = bf16[544,256]{1,0:T(8,128)(2,1)} async-done(((bf16[544,2048]{1,0:T(8,128)(2,1)}), bf16[544,256]{1,0:T(8,128)(2,1)}) %reduce-scatter.2.cloned.1.call-update) | async-done | bytes 278544 | tf_op jit(solution)/shard_map/reduce_scatter | solution.py:98
  88.5 1.1 multiply_convert_fusion
  89.6 0.6 gather_fusion
  90.2 1.0 select_select_fusion
  91.2 19.2 %all-to-all-start.1 = ((bf16[64,16,256]{2,1,0:T(8,128)(2,1)}), bf16[64,16,256]{2,1,0:T(8,128)(2,1)S(1)}, u32[]{:S(2)}, u32[]{:S(2)}) async-start(bf16[64,16,256]{2,1,0:T(8,128)(2,1)} %select_select_fusion), calls=%async_computation.2 | async-start | bytes 1048576 | tf_op jit(solution)/shard_map/all_to_all | solution.py:109
  111.4 25.9 %all-to-all-done.1 = bf16[64,16,256]{2,1,0:T(8,128)(2,1)S(1)} async-done(((bf16[64,16,256]{2,1,0:T(8,128)(2,1)}), bf16[64,16,256]{2,1,0:T(8,128)(2,1)S(1)}, u32[]{:S(2)}, u32[]{:S(2)}) %all-to-all-start.1) | async-done | bytes 524320 | tf_op jit(solution)/shard_map/all_to_all | solution.py:109
  137.3 0.6 gather_fusion.1
  138.1 0.8 copy.47
  139.0 1.2 gather_fusion.3
  140.5 0.2 fusion.38
  141.8 0.6 pad_maximum_fusion.3
  (74 shorter events, 3.3 us)
Async XLA Ops:
  7.2 81.3 %reduce-scatter.2.cloned.1.call-start = ((), (), s32[]{:S(2)}) async-start(), calls=%async_computation.3 | async-start | bytes 2506752 | tf_op jit(solution)/shard_map/reduce_scatter | solution.py:98
  13.6 1.2 copy-start
  13.6 1.2 copy-start.2
  13.6 5.9 %copy-start.4 = (s32[32]{0:T(128)S(1)}, s32[32]{0:T(128)}, u32[]{:S(2)}) copy-start(s32[32]{0:T(128)} %param.17) | copy-start | bytes 388
  13.6 5.9 %copy-start.5 = (s32[32]{0:T(128)S(1)}, s32[32]{0:T(128)}, u32[]{:S(2)}) copy-start(s32[32]{0:T(128)} %param.16) | copy-start | bytes 388
  13.6 27.6 %copy-start.6 = (s32[16]{0:T(128)S(1)}, s32[16]{0:T(128)}, u32[]{:S(2)}) copy-start(s32[16]{0:T(128)} %param.19) | copy-start | bytes 196
  13.7 27.6 %copy-start.3 = (bf16[2,16,1024]{2,1,0:T(8,128)(2,1)S(1)}, bf16[2,16,1024]{2,1,0:T(8,128)(2,1)}, u32[]{:S(2)}) copy-start(bf16[2,16,1024]{2,1,0:T(8,128)(2,1)} %param.14) | copy-start | bytes 196612
  13.7 27.6 %copy-start.1 = (bf16[256,256]{1,0:T(8,128)(2,1)S(1)}, bf16[256,256]{1,0:T(8,128)(2,1)}, u32[]{:S(2)}) copy-start(bf16[256,256]{1,0:T(8,128)(2,1)} %param.13) | copy-start | bytes 393220
  13.7 49.6 %copy-start.7 = (s32[16]{0:T(128)S(1)}, s32[16]{0:T(128)}, u32[]{:S(2)}) copy-start(s32[16]{0:T(128)} %param.18) | copy-start | bytes 196
  15.2 44.4 %collective-permute-start = (f32[544]{0:T(1024)S(1)}, f32[544]{0:T(1024)S(1)}, u32[]{:S(2)}, u32[]{:S(2)}) collective-permute-start(f32[544]{0:T(1024)S(1)} %fusion.1), channel_id=1, source_target_pairs={{0,1},{1,0},{2,3},{3,2},{4,5},{5,4},{6,7},{7,6},{8,9},{9,8},{10,11... | collective-permute-start | bytes 6536 | tf_op jit(solution)/shard_map/ppermute | solution.py:25
  20.4 37.5 %all-to-all-start = ((s32[64,1,1]{2,1,0:T(1,128)}), s32[64,1,1]{2,1,0:T(1,128)S(1)}, u32[]{:S(2)}, u32[]{:S(2)}) async-start(s32[64,1,1]{2,1,0:T(1,128)} %copy.40), calls=%async_computation | async-start | bytes 65536 | tf_op jit(solution)/shard_map/all_to_all | solution.py:100
  59.5 6.3 %collective-permute-start.1 = (f32[544]{0:T(1024)S(1)}, f32[544]{0:T(1024)S(1)}, u32[]{:S(2)}, u32[]{:S(2)}) collective-permute-start(f32[544]{0:T(1024)S(1)} %add.145), channel_id=1, source_target_pairs={{0,2},{1,3},{2,0},{3,1},{4,6},{5,7},{6,4},{7,5},{8,10},{9,11},{10,... | collective-permute-start | bytes 6536 | tf_op jit(solution)/shard_map/ppermute | solution.py:25
  65.8 8.7 %collective-permute-start.2 = (f32[544]{0:T(1024)S(1)}, f32[544]{0:T(1024)S(1)}, u32[]{:S(2)}, u32[]{:S(2)}) collective-permute-start(f32[544]{0:T(1024)S(1)} %add.146), channel_id=1, source_target_pairs={{0,4},{1,5},{2,6},{3,7},{4,0},{5,1},{6,2},{7,3},{8,12},{9,13},{10,... | collective-permute-start | bytes 6536 | tf_op jit(solution)/shard_map/ppermute | solution.py:25
  91.2 46.1 %all-to-all-start.1 = ((bf16[64,16,256]{2,1,0:T(8,128)(2,1)}), bf16[64,16,256]{2,1,0:T(8,128)(2,1)S(1)}, u32[]{:S(2)}, u32[]{:S(2)}) async-start(bf16[64,16,256]{2,1,0:T(8,128)(2,1)} %select_select_fusion), calls=%async_computation.2 | async-start | bytes 1048576 | tf_op jit(solution)/shard_map/all_to_all | solution.py:109
Sparse Core Ops, SparseCore 0:
  13.8 74.5 reduce-scatter.1

commit v2 on v1

v2 whole, which is shorter than its diff:
```python
import jax
import jax.numpy as jnp
from jax import lax
from jax.experimental import pallas as pl
from jax.experimental.pallas import tpu as pltpu
from jax.sharding import PartitionSpec as P

D = 8192
GROUP = 8
HD = 128
STEPS = 2
TILE = 128
EXTRA = 16
ABSENT = 2.0**100
BF = jnp.bfloat16
F32 = jnp.float32
VMEM_BYTES = 40 * 1024 * 1024


def ring_of(tensors):
    return list(range(0, tensors, 2)) + list(range(tensors - 1, 0, -2))


def iota(shape, axis):
    return lax.broadcasted_iota(jnp.int32, shape, axis)


def dot(a, b, contract=((1,), (0,))):
    return lax.dot_general(a, b, (contract, ((), ())), preferred_element_type=F32)


def first_chunks(order, hidden, fresh, gain, weight_a, weight_b, out_a, out_b, scaled, extra):
    rows = hidden.shape[0] + fresh.shape[0]
    wide = jnp.concatenate([hidden[...], fresh[...]], axis=0).astype(F32)
    scaled[...] = (wide * gain[...]).astype(BF)
    square = wide * wide
    high = square.astype(BF)
    low = (square - high.astype(F32)).astype(BF)
    lanes = out_a.shape[1]
    ones = jnp.ones((EXTRA, wide.shape[1]), BF)
    total = jnp.zeros((EXTRA, lanes), F32)
    for index, start in enumerate(range(0, rows, lanes)):
        stop = min(start + lanes, rows)
        part = dot(ones, high[start:stop], ((1,), (1,))) + dot(ones, low[start:stop], ((1,), (1,)))
        if stop - start < lanes:
            part = jnp.concatenate([part, jnp.zeros((EXTRA, lanes - stop + start), F32)], axis=1)
        total = jnp.where(iota((EXTRA, lanes), 0) == index, part, total)
    extra[...] = total.astype(BF)
    for weight, out in ((weight_a, out_a), (weight_b, out_b)):
        out[:rows, :] = dot(scaled[...], weight[...]).astype(BF)
        out[rows:, :] = extra[...]


def later_chunks(order, scaled, extra, *refs):
    count = len(refs) // 2
    rows = scaled.shape[0]
    for weight, out in zip(refs[:count], refs[count:]):
        out[:rows, :] = dot(scaled[...], weight[...]).astype(BF)
        out[rows:, :] = extra[...]


def whole(shape):
    return pl.BlockSpec(shape, lambda i, *_: (0,) * len(shape))


def project_chunks(hidden, fresh, gain, weight, order, lanes):
    rows, depth = hidden.shape[0] + fresh.shape[0], hidden.shape[1]
    chunk = jax.ShapeDtypeStruct((rows + EXTRA, lanes), BF)
    chunk_spec = whole((rows + EXTRA, lanes))
    scaled_type = jax.ShapeDtypeStruct((rows, depth), BF)
    extra_type = jax.ShapeDtypeStruct((EXTRA, lanes), BF)
    tensors = order.shape[0]

    def column_block(place):
        return pl.BlockSpec((depth, lanes), lambda i, order: (0, order[place]))

    params = pltpu.CompilerParams(vmem_limit_bytes=VMEM_BYTES)
    cost = lambda count: pl.CostEstimate(
        flops=2 * rows * depth * lanes * count,
        bytes_accessed=2 * (rows * depth + count * (depth + rows) * lanes),
        transcendentals=0,
    )
    out_a, out_b, scaled, extra = pl.pallas_call(
        first_chunks,
        grid_spec=pltpu.PrefetchScalarGridSpec(
            num_scalar_prefetch=1,
            grid=(1,),
            in_specs=[
                whole(hidden.shape),
                whole(fresh.shape),
                whole(gain.shape),
                column_block(0),
                column_block(1),
            ],
            out_specs=[chunk_spec, chunk_spec, whole(scaled_type.shape), whole(extra_type.shape)],
        ),
        out_shape=[chunk, chunk, scaled_type, extra_type],
        compiler_params=params,
        cost_estimate=cost(2),
        name="first_chunks",
    )(order, hidden, fresh, gain, weight, weight)
    rest = tensors - 2
    later = pl.pallas_call(
        later_chunks,
        grid_spec=pltpu.PrefetchScalarGridSpec(
            num_scalar_prefetch=1,
            grid=(1,),
            in_specs=[whole(scaled.shape), whole(extra.shape)]
            + [column_block(2 + i) for i in range(rest)],
            out_specs=[chunk_spec] * rest,
        ),
        out_shape=[chunk] * rest,
        compiler_params=params,
        cost_estimate=cost(rest),
        name="later_chunks",
    )(order, scaled, extra, *([weight] * rest))
    return [out_a, out_b, *later]


def ring_sums(hidden, fresh, gain, weight, lanes):
    tensors = lax.axis_size("tensor")
    ring = ring_of(tensors)
    ahead, behind = tensors // 2, tensors - 1 - tensors // 2
    offsets = []
    for step in range(ahead):
        offsets.append(ahead - step)
        if step < behind:
            offsets.append(step - behind)
    offsets.append(0)
    table = [
        [ring[(ring.index(device) + offset) % tensors] for offset in offsets]
        for device in range(tensors)
    ]
    order = jnp.array(table, jnp.int32)[lax.axis_index("tensor")]
    chunks = project_chunks(hidden, fresh, gain, weight, order, lanes)
    forward = [(ring[i], ring[(i + 1) % tensors]) for i in range(tensors)]
    backward = [(b, a) for a, b in forward]
    sums = {True: None, False: None}
    for offset, chunk in zip(offsets[:-1], chunks[:-1]):
        way = offset > 0
        if sums[way] is not None:
            chunk = (sums[way].astype(F32) + chunk.astype(F32)).astype(BF)
        sums[way] = lax.ppermute(chunk, "tensor", forward if way else backward)
    return sums[True], sums[False], chunks[-1]


def finish_rows(chosen, sent_len, ahead, behind, own, outgoing, fresh_kv, kept):
    total = ahead[...].astype(F32) + behind[...].astype(F32) + own[...].astype(F32)
    rows, lanes = total.shape[0] - EXTRA, total.shape[1]
    leaving = rows - fresh_kv.shape[0]
    squares = total[rows:]
    for start in range(0, rows, TILE):
        size = min(TILE, rows - start)
        across = squares[start // lanes : start // lanes + 1, start % lanes : start % lanes + TILE]
        diagonal = iota((size, TILE), 0) == iota((size, TILE), 1)
        column = jnp.sum(jnp.where(diagonal, across, 0.0), axis=1, keepdims=True)
        kept[start : start + size, :] = (
            total[start : start + size] * lax.rsqrt(column / D + 1e-06)
        ).astype(BF)
    fresh_kv[...] = kept[leaving:, :]
    context = outgoing.shape[1]

    def place(index, carry):
        start = pl.multiple_of(chosen[index] * context, context)
        block = kept[pl.ds(start, context), :]
        present = iota((context, lanes), 0) < sent_len[index]
        outgoing[index] = jnp.where(present, block, jnp.full((), ABSENT, BF))
        return carry

    lax.fori_loop(0, outgoing.shape[0], place, 0, unroll=8)


def finish(chosen, sent_len, ahead, behind, own, fresh_rows, context):
    rows, lanes = own.shape[0] - EXTRA, own.shape[1]
    slots = chosen.shape[0]
    return pl.pallas_call(
        finish_rows,
        grid_spec=pltpu.PrefetchScalarGridSpec(
            num_scalar_prefetch=2,
            grid=(1,),
            in_specs=[whole(own.shape)] * 3,
            out_specs=[whole((slots, context, lanes)), whole((fresh_rows, lanes))],
            scratch_shapes=[pltpu.VMEM((rows, lanes), BF)],
        ),
        out_shape=[
            jax.ShapeDtypeStruct((slots, context, lanes), BF),
            jax.ShapeDtypeStruct((fresh_rows, lanes), BF),
        ],
        compiler_params=pltpu.CompilerParams(vmem_limit_bytes=VMEM_BYTES),
        name="finish_rows",
    )(chosen, sent_len, ahead, behind, own)


def rebuild_and_attend(
    arrived, resident, resident_valid, queries, fresh, wanted, rebuilt, attended
):
    slots, context, lanes = arrived.shape
    steps, batch, width = queries.shape
    rows = slots * context
    columns = rebuilt.shape[1]
    held = resident.shape[1]
    heads = width // HD
    blocks = arrived[...].reshape(rows, lanes)
    valid = blocks[:, :TILE].astype(F32) < ABSENT / 2
    flags = jnp.where(valid, 1.0, 0.0).astype(BF)
    opening = jnp.where(iota((slots, rows), 1) == iota((slots, rows), 0) * context, 1.0, 0.0)
    living = dot(opening.astype(BF), flags).astype(BF)
    before = jnp.where(iota((rows, slots), 1) < iota((rows, slots), 0) // context, 1.0, 0.0)
    ranking = dot(before.astype(BF), living)
    target = ranking.astype(jnp.int32) * context + iota((rows, TILE), 0) % context
    target = jnp.where(valid, target, -1)
    routes = jnp.concatenate(
        [
            jnp.where(target == iota((rows, TILE), 1) + start, 1.0, 0.0).astype(BF)
            for start in range(0, columns, TILE)
        ],
        axis=1,
    )[:, :columns]
    moved = dot(blocks, routes, ((0,), (0,))).astype(BF)
    rebuilt[...] = moved
    filled = dot(jnp.ones((EXTRA, rows), BF), routes)[:1] > 0.5

    query = jnp.concatenate(
        [queries[s, :, h * HD : (h + 1) * HD] for s in range(steps) for h in range(heads)], axis=0
    )
    count = query.shape[0]
    scale = 1.0 / HD**0.5
    want = wanted[...]

    def request_of(size):
        return iota((count, size), 1) // context

    mask_held = (want == request_of(held)) & (resident_valid[...] > 0)
    mask_moved = (want == request_of(columns) + held // context) & filled
    line, mark = iota((count, steps * batch), 0), iota((count, steps * batch), 1)
    mask_fresh = (line % batch == mark % batch) & (mark // batch <= line // (heads * batch))
    lowest = -1e30
    score_held = jnp.where(mask_held, dot(query, resident[:HD, :]) * scale, lowest)
    score_moved = jnp.where(mask_moved, dot(query, moved[:HD]) * scale, lowest)
    score_fresh = jnp.where(
        mask_fresh, dot(query, fresh[:, :HD], ((1,), (1,))) * scale, lowest
    )
    top = jnp.maximum(
        jnp.maximum(
            jnp.max(score_held, axis=1, keepdims=True), jnp.max(score_moved, axis=1, keepdims=True)
        ),
        jnp.max(score_fresh, axis=1, keepdims=True),
    )
    exp_held = jnp.where(mask_held, jnp.exp(score_held - top), 0.0)
    exp_moved = jnp.where(mask_moved, jnp.exp(score_moved - top), 0.0)
    exp_fresh = jnp.where(mask_fresh, jnp.exp(score_fresh - top), 0.0)
    total = (
        jnp.sum(exp_held, axis=1, keepdims=True)
        + jnp.sum(exp_moved, axis=1, keepdims=True)
        + jnp.sum(exp_fresh, axis=1, keepdims=True)
    )
    across = ((1,), (1,))
    out = dot((exp_held / total).astype(BF), resident[HD:, :], across)
    out = out + dot((exp_moved / total).astype(BF), moved[HD:], across)
    out = out + dot((exp_fresh / total).astype(BF), fresh[:, HD:])
    out = out.astype(BF)
    for s in range(steps):
        for h in range(heads):
            start = (s * heads + h) * batch
            attended[s, :, h * HD : (h + 1) * HD] = out[start : start + batch]


def rebuild(arrived, resident, resident_valid, queries, fresh, wanted, columns):
    return pl.pallas_call(
        rebuild_and_attend,
        out_shape=[
            jax.ShapeDtypeStruct((arrived.shape[2], columns), BF),
            jax.ShapeDtypeStruct(queries.shape, BF),
        ],
        compiler_params=pltpu.CompilerParams(vmem_limit_bytes=VMEM_BYTES),
        name="rebuild_and_attend",
    )(arrived, resident, resident_valid, queries, fresh, wanted)


def shards(
    hidden_rows,
    kv_weight,
    norm_gain,
    resident_cache,
    queries,
    fresh_hidden,
    move_dest,
    move_len,
    resident_len,
    decode_ids,
):
    requests = move_dest.shape[0]
    context = hidden_rows.shape[0] // requests
    instances = lax.axis_size("inst")
    owned = kv_weight.shape[1] // lax.axis_size("tensor")
    assert owned == 2 * HD
    steps, batch_rows, features = fresh_hidden.shape
    heads = queries.shape[2] // HD
    targets = jnp.arange(instances, dtype=jnp.int32)
    matched = (move_dest[None, :] == targets[:, None]).astype(jnp.int32)
    chosen = jnp.sum(matched * jnp.arange(requests, dtype=jnp.int32)[None, :], axis=1)
    sent_len = jnp.sum(matched * move_len[None, :], axis=1)
    resident_valid = (
        jnp.arange(context, dtype=jnp.int32)[None, :] < resident_len[:, None]
    ).astype(jnp.int32)
    resident_valid = resident_valid.reshape(1, -1)
    wanted = jnp.tile(decode_ids, steps * heads)[:, None]

    ahead, behind, own = ring_sums(
        hidden_rows,
        fresh_hidden.reshape(steps * batch_rows, features),
        norm_gain[None, :],
        kv_weight,
        owned,
    )
    outgoing, fresh_kv = finish(
        chosen, sent_len, ahead, behind, own, steps * batch_rows, context
    )
    arrived = lax.all_to_all(outgoing, "inst", split_axis=0, concat_axis=0, tiled=True)
    return tuple(
        rebuild(
            arrived,
            resident_cache,
            resident_valid,
            queries,
            fresh_kv,
            wanted,
            requests * context,
        )
    )


def solution(mesh):
    in_specs = (
        P("inst", "tensor"),
        P("tensor", None),
        P("tensor"),
        P("tensor", "inst"),
        P(None, "inst", "tensor"),
        P(None, "inst", "tensor"),
        P("inst"),
        P("inst"),
        P("inst"),
        P("inst"),
    )
    out_specs = (P("tensor", "inst"), P(None, "inst", "tensor"))
    return jax.shard_map(shards, mesh=mesh, in_specs=in_specs, out_specs=out_specs, check_vma=False)
```

time: 150 us -> 131 us (0.87)
  the two profiles are of different devices: /device:TPU:1 before, /device:TPU:33 now
where the time goes in v2:
time: 131 us
  waiting for transfers between devices  67.5 us (52%)
  starting transfers between devices  47.2 us (36%)
  Pallas kernels  8.63 us (7%)
  local copies, waits for them, and re-layouts  5.86 us (4%)
    all_to_all x1, waiting for transfers between devices, shards(): lax.all_to_all(outgoing, 'inst', split_axis=0, concat_axis=0, tiled=True)  36.4 us
    ppermute x7, waiting for transfers between devices, ring_sums(): sums[way] = lax.ppermute(chunk, 'tensor', forward if way else backward)  31.2 us
    ppermute x7, starting transfers between devices, ring_sums(): sums[way] = lax.ppermute(chunk, 'tensor', forward if way else backward)  26.3 us
    all_to_all x1, starting transfers between devices, shards(): lax.all_to_all(outgoing, 'inst', split_axis=0, concat_axis=0, tiled=True)  20.9 us
    unnamed x22, local copies, waits for them, and re-layouts  4.98 us
  transfers between devices with their start and end apart: 8, of which 8 were waited for; matrix products, arithmetic and copies ran while one was open for 1% of the time, Pallas kernels for 2%

profile of v2, /device:TPU:33, one launch (start us, length us, event | category | flops | bytes accessed | tf_op | source)
XLA Modules:
  0.0 130.6 jit_solution(383833114020757691)
XLA Ops:
  0.6 0.7 dynamic-slice_bitcast_fusion.order
  1.3 2.2 %copy-done = bf16[1024,2048]{1,0:T(8,128)(2,1)S(1)} copy-done((bf16[1024,2048]{1,0:T(8,128)(2,1)S(1)}, bf16[1024,2048]{1,0:T(8,128)(2,1)}, u32[]{:S(2)}) %copy-start) | copy-done | bytes 4194328
  3.5 1.2 copy-done.2
  4.7 0.8 copy-done.4
  6.3 2.1 %first_chunks.1 = (bf16[560,256]{1,0:T(8,128)(2,1)S(1)}, bf16[560,256]{1,0:T(8,128)(2,1)S(1)}, bf16[544,1024]{1,0:T(8,128)(2,1)S(1)}, bf16[16,256]{1,0:T(8,128)(2,1)S(1)}) custom-call(s32[8]{0:T(128)S(1)} %dynamic-slice_bitcast_fusion.order, bf16[512,1024]{1,0:T(8,128)(2,1)S(1)} %copy-done.2, bf16[32,1024]{1,0:T(8,128)(2,1)S(1)} %bitcast.4, ...), custom_call_target="tpu_custom_call" | custom-call | flops 570425344 | bytes 2719744 | tf_op jit(solution)/shard_map/first_chunks/pallas_call | solution.py:83
  8.3 1.9 %collective-permute-start = (bf16[560,256]{1,0:T(8,128)(2,1)S(1)}, bf16[560,256]{1,0:T(8,128)(2,1)S(1)}, u32[]{:S(2)}, u32[]{:S(2)}) collective-permute-start(bf16[560,256]{1,0:T(8,128)(2,1)S(1)} %get-tuple-element.14), channel_id=1, source_target_pairs={{0,2},{2,4},{4,6},{6,7},{7,5},{5,3},{3,1},{1,0},{8,10},{10,12},{12... | collective-permute-start | bytes 860168 | tf_op jit(solution)/shard_map/ppermute | solution.py:143
  10.3 4.9 %collective-permute-start.4 = (bf16[560,256]{1,0:T(8,128)(2,1)S(1)}, bf16[560,256]{1,0:T(8,128)(2,1)S(1)}, u32[]{:S(2)}, u32[]{:S(2)}) collective-permute-start(bf16[560,256]{1,0:T(8,128)(2,1)S(1)} %get-tuple-element.20), channel_id=1, source_target_pairs={{2,0},{4,2},{6,4},{7,6},{5,7},{3,5},{1,3},{0,1},{10,8},{12,10},{14... | collective-permute-start | bytes 860168 | tf_op jit(solution)/shard_map/ppermute | solution.py:143
  15.2 2.5 %later_chunks.1 = (bf16[560,256]{1,0:T(8,128)(2,1)S(1)}, bf16[560,256]{1,0:T(8,128)(2,1)S(1)}, bf16[560,256]{1,0:T(8,128)(2,1)S(1)}, bf16[560,256]{1,0:T(8,128)(...) custom-call(s32[8]{0:T(128)S(1)} %dynamic-slice_bitcast_fusion.order, ...), custom_call_target="tpu_custom_call" | custom-call | flops 1711276032 | bytes 5931008 | tf_op jit(solution)/shard_map/later_chunks/pallas_call | solution.py:103
  17.7 2.1 %collective-permute-done = bf16[560,256]{1,0:T(8,128)(2,1)S(1)} collective-permute-done((bf16[560,256]{1,0:T(8,128)(2,1)S(1)}, bf16[560,256]{1,0:T(8,128)(2,1)S(1)}, u32[]{:S(2)}, u32[]{:S(2)}) %collective-permute-start) | collective-permute-done | bytes 286752 | tf_op jit(solution)/shard_map/ppermute | solution.py:143
  19.9 1.9 %collective-permute-start.1 = (bf16[560,256]{1,0:T(8,128)(2,1)S(1)}, bf16[560,256]{1,0:T(8,128)(2,1)S(1)}, u32[]{:S(2)}, u32[]{:S(2)}) collective-permute-start(bf16[560,256]{1,0:T(8,128)(2,1)S(1)} %add_convert_fusion.4), channel_id=1, source_target_pairs={{0,2},{2,4},{4,6},{6,7},{7,5},{5,3},{3,1},{1,0},{8,10},{10,12},{12... | collective-permute-start | bytes 860168 | tf_op jit(solution)/shard_map/ppermute | solution.py:143
  21.8 2.3 %collective-permute-done.4 = bf16[560,256]{1,0:T(8,128)(2,1)S(1)} collective-permute-done((bf16[560,256]{1,0:T(8,128)(2,1)S(1)}, bf16[560,256]{1,0:T(8,128)(2,1)S(1)}, u32[]{:S(2)}, u32[]{:S(2)}) %collective-permute-start.4) | collective-permute-done | bytes 286752 | tf_op jit(solution)/shard_map/ppermute | solution.py:143
  24.1 5.7 %collective-permute-start.5 = (bf16[560,256]{1,0:T(8,128)(2,1)S(1)}, bf16[560,256]{1,0:T(8,128)(2,1)S(1)}, u32[]{:S(2)}, u32[]{:S(2)}) collective-permute-start(bf16[560,256]{1,0:T(8,128)(2,1)S(1)} %add_convert_fusion.1), channel_id=1, source_target_pairs={{2,0},{4,2},{6,4},{7,6},{5,7},{3,5},{1,3},{0,1},{10,8},{12,10},{14... | collective-permute-start | bytes 860168 | tf_op jit(solution)/shard_map/ppermute | solution.py:143
  29.9 4.5 %collective-permute-done.1 = bf16[560,256]{1,0:T(8,128)(2,1)S(1)} collective-permute-done((bf16[560,256]{1,0:T(8,128)(2,1)S(1)}, bf16[560,256]{1,0:T(8,128)(2,1)S(1)}, u32[]{:S(2)}, u32[]{:S(2)}) %collective-permute-start.1) | collective-permute-done | bytes 286752 | tf_op jit(solution)/shard_map/ppermute | solution.py:143
  34.4 3.2 %collective-permute-start.2 = (bf16[560,256]{1,0:T(8,128)(2,1)S(1)}, bf16[560,256]{1,0:T(8,128)(2,1)S(1)}, u32[]{:S(2)}, u32[]{:S(2)}) collective-permute-start(bf16[560,256]{1,0:T(8,128)(2,1)S(1)} %add_convert_fusion.3), channel_id=1, source_target_pairs={{0,2},{2,4},{4,6},{6,7},{7,5},{5,3},{3,1},{1,0},{8,10},{10,12},{12... | collective-permute-start | bytes 860168 | tf_op jit(solution)/shard_map/ppermute | solution.py:143
  37.7 4.9 %collective-permute-done.5 = bf16[560,256]{1,0:T(8,128)(2,1)S(1)} collective-permute-done((bf16[560,256]{1,0:T(8,128)(2,1)S(1)}, bf16[560,256]{1,0:T(8,128)(2,1)S(1)}, u32[]{:S(2)}, u32[]{:S(2)}) %collective-permute-start.5) | collective-permute-done | bytes 286752 | tf_op jit(solution)/shard_map/ppermute | solution.py:143
  42.6 6.7 %collective-permute-start.6 = (bf16[560,256]{1,0:T(8,128)(2,1)S(1)}, bf16[560,256]{1,0:T(8,128)(2,1)S(1)}, u32[]{:S(2)}, u32[]{:S(2)}) collective-permute-start(bf16[560,256]{1,0:T(8,128)(2,1)S(1)} %add_convert_fusion), channel_id=1, source_target_pairs={{2,0},{4,2},{6,4},{7,6},{5,7},{3,5},{1,3},{0,1},{10,8},{12,10},{14... | collective-permute-start | bytes 860168 | tf_op jit(solution)/shard_map/ppermute | solution.py:143
  49.3 3.6 %collective-permute-done.2 = bf16[560,256]{1,0:T(8,128)(2,1)S(1)} collective-permute-done((bf16[560,256]{1,0:T(8,128)(2,1)S(1)}, bf16[560,256]{1,0:T(8,128)(2,1)S(1)}, u32[]{:S(2)}, u32[]{:S(2)}) %collective-permute-start.2) | collective-permute-done | bytes 286752 | tf_op jit(solution)/shard_map/ppermute | solution.py:143
  53.0 1.9 %collective-permute-start.3 = (bf16[560,256]{1,0:T(8,128)(2,1)S(1)}, bf16[560,256]{1,0:T(8,128)(2,1)S(1)}, u32[]{:S(2)}, u32[]{:S(2)}) collective-permute-start(bf16[560,256]{1,0:T(8,128)(2,1)S(1)} %add_convert_fusion.2), channel_id=1, source_target_pairs={{0,2},{2,4},{4,6},{6,7},{7,5},{5,3},{3,1},{1,0},{8,10},{10,12},{12... | collective-permute-start | bytes 860168 | tf_op jit(solution)/shard_map/ppermute | solution.py:143
  55.0 3.4 %collective-permute-done.6.behind = bf16[560,256]{1,0:T(8,128)(2,1)S(1)} collective-permute-done((bf16[560,256]{1,0:T(8,128)(2,1)S(1)}, bf16[560,256]{1,0:T(8,128)(2,1)S(1)}, u32[]{:S(2)}, u32[]{:S(2)}) %collective-permute-start.6) | collective-permute-done | bytes 286752 | tf_op jit(solution)/shard_map/ppermute | solution.py:143
  58.4 10.5 %collective-permute-done.3.ahead = bf16[560,256]{1,0:T(8,128)(2,1)S(1)} collective-permute-done((bf16[560,256]{1,0:T(8,128)(2,1)S(1)}, bf16[560,256]{1,0:T(8,128)(2,1)S(1)}, u32[]{:S(2)}, u32[]{:S(2)}) %collective-permute-start.3) | collective-permute-done | bytes 286752 | tf_op jit(solution)/shard_map/ppermute | solution.py:143
  69.0 1.7 %finish_rows.1 = (bf16[64,16,256]{2,1,0:T(8,128)(2,1)}, bf16[32,256]{1,0:T(8,128)(2,1)S(1)}) custom-call(s32[64]{0:T(128)S(1)} %get-tuple-element.27.chosen, s32[64]{0:T(128)S(1)} %get-tuple-element.26.sent_len, bf16[560,256]{1,0:T(8,128)(2,1)S(1)} %collective-permute-done.3.ahead, bf16[560,256]{1,0:T(8,128)(2,1)S(1)} %collective-permute-done.6.behind, ...), custom_call_target="tpu_custom_call" | custom-call | tf_op jit(solution)/shard_map/finish_rows/pallas_call | solution.py:176
  70.6 20.9 %all-to-all-start = ((bf16[64,16,256]{2,1,0:T(8,128)(2,1)}), bf16[64,16,256]{2,1,0:T(8,128)(2,1)S(1)}, u32[]{:S(2)}, u32[]{:S(2)}) async-start(bf16[64,16,256]{2,1,0:T(8,128)(2,1)} %get-tuple-element.24), calls=%async_computation | async-start | bytes 1048576 | tf_op jit(solution)/shard_map/all_to_all | solution.py:319
  91.8 36.4 %all-to-all-done.arrived = bf16[64,16,256]{2,1,0:T(8,128)(2,1)S(1)} async-done(((bf16[64,16,256]{2,1,0:T(8,128)(2,1)}), bf16[64,16,256]{2,1,0:T(8,128)(2,1)S(1)}, u32[]{:S(2)}, u32[]{:S(2)}) %all-to-all-start) | async-done | bytes 524320 | tf_op jit(solution)/shard_map/all_to_all | solution.py:319
  128.2 2.5 %rebuild_and_attend.1 = (bf16[256,512]{1,0:T(8,128)(2,1)}, bf16[2,16,1024]{2,1,0:T(8,128)(2,1)}) custom-call(bf16[64,16,256]{2,1,0:T(8,128)(2,1)S(1)} %all-to-all-done.arrived, bf16[256,256]{1,0:T(8,128)(2,1)S(1)} %copy-done.3, s32[1,256]{1,0:T(1,128)S(1)} %reshape.40.resident_valid, bf16[2,16,1024]{2,1,0:T(8,128)(2,1)S(1)} %copy-done.5, ...), custom_call_target="tpu_custom_call" | custom-call | tf_op jit(solution)/shard_map/rebuild_and_attend/pallas_call | solution.py:269
  (29 shorter events, 1.5 us)
Async XLA Ops:
  1.3 2.2 %copy-start = (bf16[1024,2048]{1,0:T(8,128)(2,1)S(1)}, bf16[1024,2048]{1,0:T(8,128)(2,1)}, u32[]{:S(2)}) copy-start(bf16[1024,2048]{1,0:T(8,128)(2,1)} %refs_5_.1) | copy-start | bytes 12582916
  3.5 1.2 copy-start.2
  4.7 0.8 copy-start.4
  5.6 0.7 copy-start.6
  6.3 8.9 %copy-start.1 = (bf16[1024,2048]{1,0:T(8,128)(2,1)S(1)}, bf16[1024,2048]{1,0:T(8,128)(2,1)}, u32[]{:S(2)}) copy-start(bf16[1024,2048]{1,0:T(8,128)(2,1)} %refs_5_.1) | copy-start | bytes 12582916
  8.3 11.4 %collective-permute-start = (bf16[560,256]{1,0:T(8,128)(2,1)S(1)}, bf16[560,256]{1,0:T(8,128)(2,1)S(1)}, u32[]{:S(2)}, u32[]{:S(2)}) collective-permute-start(bf16[560,256]{1,0:T(8,128)(2,1)S(1)} %get-tuple-element.14), channel_id=1, source_target_pairs={{0,2},{2,4},{4,6},{6,7},{7,5},{5,3},{3,1},{1,0},{8,10},{10,12},{12... | collective-permute-start | bytes 860168 | tf_op jit(solution)/shard_map/ppermute | solution.py:143
  10.3 13.8 %collective-permute-start.4 = (bf16[560,256]{1,0:T(8,128)(2,1)S(1)}, bf16[560,256]{1,0:T(8,128)(2,1)S(1)}, u32[]{:S(2)}, u32[]{:S(2)}) collective-permute-start(bf16[560,256]{1,0:T(8,128)(2,1)S(1)} %get-tuple-element.20), channel_id=1, source_target_pairs={{2,0},{4,2},{6,4},{7,6},{5,7},{3,5},{1,3},{0,1},{10,8},{12,10},{14... | collective-permute-start | bytes 860168 | tf_op jit(solution)/shard_map/ppermute | solution.py:143
  17.7 37.2 %copy-start.9 = (s32[32]{0:T(128)S(1)}, s32[32]{0:T(128)}, u32[]{:S(2)}) copy-start(s32[32]{0:T(128)} %param.18) | copy-start | bytes 388
  17.7 37.2 %copy-start.10 = (s32[32]{0:T(128)S(1)}, s32[32]{0:T(128)}, u32[]{:S(2)}) copy-start(s32[32]{0:T(128)} %param.17) | copy-start | bytes 388
  17.7 73.8 %copy-start.7 = (s32[16]{0:T(128)S(1)}, s32[16]{0:T(128)}, u32[]{:S(2)}) copy-start(s32[16]{0:T(128)} %param.20) | copy-start | bytes 196
  17.7 73.9 %copy-start.8 = (s32[16]{0:T(128)S(1)}, s32[16]{0:T(128)}, u32[]{:S(2)}) copy-start(s32[16]{0:T(128)} %param.19) | copy-start | bytes 196
  17.7 110.5 %copy-start.3 = (bf16[256,256]{1,0:T(8,128)(2,1)S(1)}, bf16[256,256]{1,0:T(8,128)(2,1)}, u32[]{:S(2)}) copy-start(bf16[256,256]{1,0:T(8,128)(2,1)} %resident.1) | copy-start | bytes 393220
  17.7 110.4 %copy-start.5 = (bf16[2,16,1024]{2,1,0:T(8,128)(2,1)S(1)}, bf16[2,16,1024]{2,1,0:T(8,128)(2,1)}, u32[]{:S(2)}) copy-start(bf16[2,16,1024]{2,1,0:T(8,128)(2,1)} %queries.1) | copy-start | bytes 196612
  19.9 14.5 %collective-permute-start.1 = (bf16[560,256]{1,0:T(8,128)(2,1)S(1)}, bf16[560,256]{1,0:T(8,128)(2,1)S(1)}, u32[]{:S(2)}, u32[]{:S(2)}) collective-permute-start(bf16[560,256]{1,0:T(8,128)(2,1)S(1)} %add_convert_fusion.4), channel_id=1, source_target_pairs={{0,2},{2,4},{4,6},{6,7},{7,5},{5,3},{3,1},{1,0},{8,10},{10,12},{12... | collective-permute-start | bytes 860168 | tf_op jit(solution)/shard_map/ppermute | solution.py:143
  24.1 18.4 %collective-permute-start.5 = (bf16[560,256]{1,0:T(8,128)(2,1)S(1)}, bf16[560,256]{1,0:T(8,128)(2,1)S(1)}, u32[]{:S(2)}, u32[]{:S(2)}) collective-permute-start(bf16[560,256]{1,0:T(8,128)(2,1)S(1)} %add_convert_fusion.1), channel_id=1, source_target_pairs={{2,0},{4,2},{6,4},{7,6},{5,7},{3,5},{1,3},{0,1},{10,8},{12,10},{14... | collective-permute-start | bytes 860168 | tf_op jit(solution)/shard_map/ppermute | solution.py:143
  34.4 18.5 %collective-permute-start.2 = (bf16[560,256]{1,0:T(8,128)(2,1)S(1)}, bf16[560,256]{1,0:T(8,128)(2,1)S(1)}, u32[]{:S(2)}, u32[]{:S(2)}) collective-permute-start(bf16[560,256]{1,0:T(8,128)(2,1)S(1)} %add_convert_fusion.3), channel_id=1, source_target_pairs={{0,2},{2,4},{4,6},{6,7},{7,5},{5,3},{3,1},{1,0},{8,10},{10,12},{12... | collective-permute-start | bytes 860168 | tf_op jit(solution)/shard_map/ppermute | solution.py:143
  42.6 15.8 %collective-permute-start.6 = (bf16[560,256]{1,0:T(8,128)(2,1)S(1)}, bf16[560,256]{1,0:T(8,128)(2,1)S(1)}, u32[]{:S(2)}, u32[]{:S(2)}) collective-permute-start(bf16[560,256]{1,0:T(8,128)(2,1)S(1)} %add_convert_fusion), channel_id=1, source_target_pairs={{2,0},{4,2},{6,4},{7,6},{5,7},{3,5},{1,3},{0,1},{10,8},{12,10},{14... | collective-permute-start | bytes 860168 | tf_op jit(solution)/shard_map/ppermute | solution.py:143
  53.0 16.0 %collective-permute-start.3 = (bf16[560,256]{1,0:T(8,128)(2,1)S(1)}, bf16[560,256]{1,0:T(8,128)(2,1)S(1)}, u32[]{:S(2)}, u32[]{:S(2)}) collective-permute-start(bf16[560,256]{1,0:T(8,128)(2,1)S(1)} %add_convert_fusion.2), channel_id=1, source_target_pairs={{0,2},{2,4},{4,6},{6,7},{7,5},{5,3},{3,1},{1,0},{8,10},{10,12},{12... | collective-permute-start | bytes 860168 | tf_op jit(solution)/shard_map/ppermute | solution.py:143
  70.6 57.5 %all-to-all-start = ((bf16[64,16,256]{2,1,0:T(8,128)(2,1)}), bf16[64,16,256]{2,1,0:T(8,128)(2,1)S(1)}, u32[]{:S(2)}, u32[]{:S(2)}) async-start(bf16[64,16,256]{2,1,0:T(8,128)(2,1)} %get-tuple-element.24), calls=%async_computation | async-start | bytes 1048576 | tf_op jit(solution)/shard_map/all_to_all | solution.py:319

commit v3 on v2

--- a/solution.py
+++ b/solution.py
@@ -10,11 +10,13 @@
 HD = 128
 STEPS = 2
 TILE = 128
+CONTEXT = 16
 EXTRA = 16
+NOWHERE = 63
 ABSENT = 2.0**100
 BF = jnp.bfloat16
 F32 = jnp.float32
-VMEM_BYTES = 40 * 1024 * 1024
+VMEM_BYTES = 60 * 1024 * 1024
 
 
 def ring_of(tensors):
@@ -29,9 +31,53 @@
     return lax.dot_general(a, b, (contract, ((), ())), preferred_element_type=F32)
 
 
-def first_chunks(order, hidden, fresh, gain, weight_a, weight_b, out_a, out_b, scaled, extra):
-    rows = hidden.shape[0] + fresh.shape[0]
-    wide = jnp.concatenate([hidden[...], fresh[...]], axis=0).astype(F32)
+def plane_of(instance):
+    return (instance >> 2) * 2 + (instance & 1)
+
+
+def half_of(instance):
+    return (instance >> 1) & 1
+
+
+def first_chunks(
+    order, dest, length, me, hidden, fresh, gain, weight_a, weight_b, out_a, out_b, scaled, extra, codes
+):
+    requests = dest.shape[0]
+    context = hidden.shape[0] // requests
+    rows, capacity = scaled.shape[0], scaled.shape[0] - fresh.shape[0]
+    half = half_of(me[0])
+
+    def crosses(j):
+        return half_of(dest[j]) != half
+
+    def count(j, crossing):
+        return crossing + jnp.where(crosses(j), length[j], 0)
+
+    crossing = lax.fori_loop(0, requests, count, jnp.int32(0), unroll=8)
+    lane = iota((1, hidden.shape[0]), 1)
+
+    def place(j, carry):
+        next_cross, next_stay, target, code = carry
+        cross = crosses(j)
+        start = jnp.where(cross, next_cross, next_stay)
+        place_here = (lane // context == j) & (lane % context < length[j])
+        target = jnp.where(place_here, start + lane % context, target)
+        inside = (lane >= start) & (lane < start + length[j])
+        code = jnp.where(inside, plane_of(dest[j]) * context + lane - start, code)
+        return (
+            next_cross + jnp.where(cross, length[j], 0),
+            next_stay + jnp.where(cross, 0, length[j]),
+            target,
+            code,
+        )
+
+    nowhere = jnp.full(lane.shape, -1, jnp.int32)
+    _, _, target, code = lax.fori_loop(
+        0, requests, place, (jnp.int32(0), crossing, nowhere, nowhere), unroll=8
+    )
+    codes[...] = jnp.where(iota(codes.shape, 0) == 0, code, crossing)
+    select = jnp.where(target == iota((capacity, hidden.shape[0]), 0), 1.0, 0.0).astype(BF)
+    wide = jnp.concatenate([dot(select, hidden[...]), fresh[...].astype(F32)], axis=0)
     scaled[...] = (wide * gain[...]).astype(BF)
     square = wide * wide
     high = square.astype(BF)
@@ -63,16 +109,17 @@
     return pl.BlockSpec(shape, lambda i, *_: (0,) * len(shape))
 
 
-def project_chunks(hidden, fresh, gain, weight, order, lanes):
-    rows, depth = hidden.shape[0] + fresh.shape[0], hidden.shape[1]
+def project_chunks(hidden, fresh, gain, weight, order, dest, length, me, capacity, lanes):
+    rows, depth = capacity + fresh.shape[0], hidden.shape[1]
     chunk = jax.ShapeDtypeStruct((rows + EXTRA, lanes), BF)
     chunk_spec = whole((rows + EXTRA, lanes))
     scaled_type = jax.ShapeDtypeStruct((rows, depth), BF)
     extra_type = jax.ShapeDtypeStruct((EXTRA, lanes), BF)
+    codes_type = jax.ShapeDtypeStruct((8, hidden.shape[0]), jnp.int32)
     tensors = order.shape[0]
 
     def column_block(place):
-        return pl.BlockSpec((depth, lanes), lambda i, order: (0, order[place]))
+        return pl.BlockSpec((depth, lanes), lambda i, order, *_: (0, order[place]))
 
     params = pltpu.CompilerParams(vmem_limit_bytes=VMEM_BYTES)
     cost = lambda count: pl.CostEstimate(
@@ -80,10 +127,10 @@
         bytes_accessed=2 * (rows * depth + count * (depth + rows) * lanes),
         transcendentals=0,
     )
-    out_a, out_b, scaled, extra = pl.pallas_call(
+    out_a, out_b, scaled, extra, codes = pl.pallas_call(
         first_chunks,
         grid_spec=pltpu.PrefetchScalarGridSpec(
-            num_scalar_prefetch=1,
+            num_scalar_prefetch=4,
             grid=(1,),
             in_specs=[
                 whole(hidden.shape),
@@ -92,13 +139,19 @@
                 column_block(0),
                 column_block(1),
             ],
-            out_specs=[chunk_spec, chunk_spec, whole(scaled_type.shape), whole(extra_type.shape)],
+            out_specs=[
+                chunk_spec,
+                chunk_spec,
+                whole(scaled_type.shape),
+                whole(extra_type.shape),
+                whole(codes_type.shape),
+            ],
         ),
-        out_shape=[chunk, chunk, scaled_type, extra_type],
+        out_shape=[chunk, chunk, scaled_type, extra_type, codes_type],
         compiler_params=params,
         cost_estimate=cost(2),
         name="first_chunks",
-    )(order, hidden, fresh, gain, weight, weight)
+    )(order, dest, length, me, hidden, fresh, gain, weight, weight)
     rest = tensors - 2
     later = pl.pallas_call(
         later_chunks,
@@ -114,29 +167,36 @@
         cost_estimate=cost(rest),
         name="later_chunks",
     )(order, scaled, extra, *([weight] * rest))
-    return [out_a, out_b, *later]
-
-
-def ring_sums(hidden, fresh, gain, weight, lanes):
-    tensors = lax.axis_size("tensor")
-    ring = ring_of(tensors)
-    ahead, behind = tensors // 2, tensors - 1 - tensors // 2
+    return [out_a, out_b, *later], codes
+
+
+def ring_offsets(tensors):
+    ahead = tensors // 2
+    behind = tensors - 1 - ahead
     offsets = []
     for step in range(ahead):
         offsets.append(ahead - step)
         if step < behind:
             offsets.append(step - behind)
-    offsets.append(0)
+    return offsets + [0]
+
+
+def ring_order(tensors):
+    ring = ring_of(tensors)
     table = [
-        [ring[(ring.index(device) + offset) % tensors] for offset in offsets]
+        [ring[(ring.index(device) + offset) % tensors] for offset in ring_offsets(tensors)]
         for device in range(tensors)
     ]
-    order = jnp.array(table, jnp.int32)[lax.axis_index("tensor")]
-    chunks = project_chunks(hidden, fresh, gain, weight, order, lanes)
+    return jnp.array(table, jnp.int32)[lax.axis_index("tensor")]
+
+
+def ring_sums(chunks):
+    tensors = lax.axis_size("tensor")
+    ring = ring_of(tensors)
     forward = [(ring[i], ring[(i + 1) % tensors]) for i in range(tensors)]
     backward = [(b, a) for a, b in forward]
     sums = {True: None, False: None}
-    for offset, chunk in zip(offsets[:-1], chunks[:-1]):
+    for offset, chunk in zip(ring_offsets(tensors), chunks[:-1]):
         way = offset > 0
         if sums[way] is not None:
             chunk = (sums[way].astype(F32) + chunk.astype(F32)).astype(BF)
@@ -144,10 +204,9 @@
     return sums[True], sums[False], chunks[-1]
 
 
-def finish_rows(chosen, sent_len, ahead, behind, own, outgoing, fresh_kv, kept):
+def finish_rows(codes, ahead, behind, own, crossing_rows, kept):
     total = ahead[...].astype(F32) + behind[...].astype(F32) + own[...].astype(F32)
-    rows, lanes = total.shape[0] - EXTRA, total.shape[1]
-    leaving = rows - fresh_kv.shape[0]
+    rows, lanes = kept.shape
     squares = total[rows:]
     for start in range(0, rows, TILE):
         size = min(TILE, rows - start)
@@ -157,55 +216,93 @@
         kept[start : start + size, :] = (
             total[start : start + size] * lax.rsqrt(column / D + 1e-06)
         ).astype(BF)
-    fresh_kv[...] = kept[leaving:, :]
-    context = outgoing.shape[1]
-
-    def place(index, carry):
-        start = pl.multiple_of(chosen[index] * context, context)
-        block = kept[pl.ds(start, context), :]
-        present = iota((context, lanes), 0) < sent_len[index]
-        outgoing[index] = jnp.where(present, block, jnp.full((), ABSENT, BF))
-        return carry
-
-    lax.fori_loop(0, outgoing.shape[0], place, 0, unroll=8)
-
-
-def finish(chosen, sent_len, ahead, behind, own, fresh_rows, context):
+    sent = crossing_rows.shape[0] - EXTRA
+    crossing_rows[:sent, :] = kept[:sent, :]
+    wide = min(lanes, codes.shape[1])
+    code, count = codes[0:1, :wide], codes[1:2, :wide]
+    if wide < lanes:
+        code = jnp.concatenate([code, jnp.zeros((1, lanes - wide), jnp.int32)], axis=1)
+        count = jnp.concatenate([count, jnp.zeros((1, lanes - wide), jnp.int32)], axis=1)
+    lane, line = iota((EXTRA, lanes), 1), iota((EXTRA, lanes), 0)
+    used = (lane < count) & (lane < sent)
+    notes = jnp.where(used, code // CONTEXT, NOWHERE)
+    notes = jnp.where(line == 1, code % CONTEXT, notes)
+    notes = jnp.where(line == 2, count // CONTEXT, notes)
+    notes = jnp.where(line == 3, count % CONTEXT, notes)
+    crossing_rows[sent:, :] = notes.astype(F32).astype(BF)
+
+
+def finish(codes, ahead, behind, own, sent):
     rows, lanes = own.shape[0] - EXTRA, own.shape[1]
-    slots = chosen.shape[0]
     return pl.pallas_call(
         finish_rows,
-        grid_spec=pltpu.PrefetchScalarGridSpec(
-            num_scalar_prefetch=2,
-            grid=(1,),
-            in_specs=[whole(own.shape)] * 3,
-            out_specs=[whole((slots, context, lanes)), whole((fresh_rows, lanes))],
-            scratch_shapes=[pltpu.VMEM((rows, lanes), BF)],
-        ),
         out_shape=[
-            jax.ShapeDtypeStruct((slots, context, lanes), BF),
-            jax.ShapeDtypeStruct((fresh_rows, lanes), BF),
+            jax.ShapeDtypeStruct((sent + EXTRA, lanes), BF),
+            jax.ShapeDtypeStruct((rows, lanes), BF),
         ],
         compiler_params=pltpu.CompilerParams(vmem_limit_bytes=VMEM_BYTES),
         name="finish_rows",
-    )(chosen, sent_len, ahead, behind, own)
+    )(codes, ahead, behind, own)
+
+
+def routed(route, rows):
+    found = jnp.sum(route, axis=1, keepdims=True) > 0.5
+    return jnp.where(found, dot(route.astype(BF), rows), ABSENT).astype(BF)
+
+
+def place_staying(codes, first, second, out):
+    capacity = codes.shape[1] - second.shape[0]
+    slots, context, lanes = out.shape
+    shape = (slots * context, codes.shape[1])
+    code, crossing = codes[0:1, :], codes[1:2, :]
+    route = (iota(shape, 0) == code) & (iota(shape, 1) >= crossing)
+    rows = jnp.concatenate([first[:capacity, :], second[...]], axis=0)
+    out[...] = routed(jnp.where(route, 1.0, 0.0), rows).reshape(out.shape)
+
+
+def place_crossing(received, out):
+    slots, context, lanes = out.shape
+    sent = received.shape[0] - EXTRA
+    notes = received[sent:, :].astype(F32).astype(jnp.int32)
+    code = notes[0:1, :sent] * context + notes[1:2, :sent]
+    route = iota((slots * context, sent), 0) == code
+    out[...] = routed(jnp.where(route, 1.0, 0.0), received[:sent, :]).reshape(out.shape)
+
+
+def place(kernel, slots, lanes, *operands):
+    return pl.pallas_call(
+        kernel,
+        out_shape=jax.ShapeDtypeStruct((slots, CONTEXT, lanes), BF),
+        compiler_params=pltpu.CompilerParams(vmem_limit_bytes=VMEM_BYTES),
+        name=kernel.__name__,
+    )(*operands)
 
 
 def rebuild_and_attend(
-    arrived, resident, resident_valid, queries, fresh, wanted, rebuilt, attended
+    me, near, far, resident, resident_valid, queries, kept, wanted, rebuilt, attended
 ):
-    slots, context, lanes = arrived.shape
+    plane, context, lanes = near.shape
+    slots = 2 * plane
     steps, batch, width = queries.shape
     rows = slots * context
+    fresh = kept[kept.shape[0] - steps * batch :, :]
     columns = rebuilt.shape[1]
     held = resident.shape[1]
     heads = width // HD
-    blocks = arrived[...].reshape(rows, lanes)
+    blocks = jnp.concatenate([near[...], far[...]], axis=0).reshape(rows, lanes)
+    half = half_of(me[0])
+
+    def instance_of(slot):
+        place = slot % plane
+        there = jnp.where(slot < plane, half, 1 - half)
+        return (place >> 1) * 4 + there * 2 + (place & 1)
+
     valid = blocks[:, :TILE].astype(F32) < ABSENT / 2
     flags = jnp.where(valid, 1.0, 0.0).astype(BF)
     opening = jnp.where(iota((slots, rows), 1) == iota((slots, rows), 0) * context, 1.0, 0.0)
     living = dot(opening.astype(BF), flags).astype(BF)
-    before = jnp.where(iota((rows, slots), 1) < iota((rows, slots), 0) // context, 1.0, 0.0)
+    sooner = instance_of(iota((rows, slots), 1)) < instance_of(iota((rows, slots), 0) // context)
+    before = jnp.where(sooner, 1.0, 0.0)
     ranking = dot(before.astype(BF), living)
     target = ranking.astype(jnp.int32) * context + iota((rows, TILE), 0) % context
     target = jnp.where(valid, target, -1)
@@ -265,16 +362,39 @@
             attended[s, :, h * HD : (h + 1) * HD] = out[start : start + batch]
 
 
-def rebuild(arrived, resident, resident_valid, queries, fresh, wanted, columns):
+def rebuild(me, near, far, resident, resident_valid, queries, kept, wanted, columns):
+    vmem = pl.BlockSpec(memory_space=pltpu.VMEM)
     return pl.pallas_call(
         rebuild_and_attend,
+        in_specs=[pl.BlockSpec(memory_space=pltpu.SMEM)] + [vmem] * 7,
         out_shape=[
-            jax.ShapeDtypeStruct((arrived.shape[2], columns), BF),
+            jax.ShapeDtypeStruct((near.shape[2], columns), BF),
             jax.ShapeDtypeStruct(queries.shape, BF),
         ],
         compiler_params=pltpu.CompilerParams(vmem_limit_bytes=VMEM_BYTES),
         name="rebuild_and_attend",
-    )(arrived, resident, resident_valid, queries, fresh, wanted)
+    )(me, near, far, resident, resident_valid, queries, kept, wanted)
+
+
+def remaining_rows(hidden, gain, weight, codes, target_of, capacity, lanes):
+    tensors = lax.axis_size("tensor")
+    left = hidden.shape[0] - capacity
+    select = (target_of[None, :] == capacity + jnp.arange(left, dtype=jnp.int32)[:, None]).astype(BF)
+    wide = jnp.dot(select, hidden, preferred_element_type=F32)
+    squares = jnp.sum(wide * wide, axis=1)
+    distance = 1
+    while distance < tensors:
+        pairs = [(i, i ^ distance) for i in range(tensors)]
+        squares = squares + lax.ppermute(squares, "tensor", pairs)
+        distance *= 2
+    parts = jnp.dot((wide * gain).astype(BF), weight, preferred_element_type=F32).astype(BF)
+    order = ring_order(tensors)
+    chunks = [
+        lax.dynamic_slice_in_dim(parts, order[i] * lanes, lanes, 1) for i in range(tensors)
+    ]
+    ahead, behind, own = ring_sums(chunks)
+    total = ahead.astype(F32) + behind.astype(F32) + own.astype(F32)
+    return (total * lax.rsqrt(squares / D + 1e-06)[:, None]).astype(BF)
 
 
 def shards(
@@ -290,42 +410,88 @@
     decode_ids,
 ):
     requests = move_dest.shape[0]
-    context = hidden_rows.shape[0] // requests
+    leaving = hidden_rows.shape[0]
+    context = leaving // requests
     instances = lax.axis_size("inst")
     owned = kv_weight.shape[1] // lax.axis_size("tensor")
-    assert owned == 2 * HD
+    assert owned == 2 * HD and context == CONTEXT
     steps, batch_rows, features = fresh_hidden.shape
     heads = queries.shape[2] // HD
-    targets = jnp.arange(instances, dtype=jnp.int32)
-    matched = (move_dest[None, :] == targets[:, None]).astype(jnp.int32)
-    chosen = jnp.sum(matched * jnp.arange(requests, dtype=jnp.int32)[None, :], axis=1)
-    sent_len = jnp.sum(matched * move_len[None, :], axis=1)
+    fresh_rows = steps * batch_rows
+    capacity = max(leaving * 23 // 32 // 16, 1) * 16
+    sent = max(leaving * 15 // 32 // 16, 1) * 16
+    plane = instances // 2
+    mine = lax.axis_index("inst").astype(jnp.int32)[None]
+    fresh = fresh_hidden.reshape(fresh_rows, features)
+    gain = norm_gain[None, :]
     resident_valid = (
         jnp.arange(context, dtype=jnp.int32)[None, :] < resident_len[:, None]
     ).astype(jnp.int32)
     resident_valid = resident_valid.reshape(1, -1)
     wanted = jnp.tile(decode_ids, steps * heads)[:, None]
 
-    ahead, behind, own = ring_sums(
-        hidden_rows,
-        fresh_hidden.reshape(steps * batch_rows, features),
-        norm_gain[None, :],
-        kv_weight,
-        owned,
-    )
-    outgoing, fresh_kv = finish(
-        chosen, sent_len, ahead, behind, own, steps * batch_rows, context
-    )
-    arrived = lax.all_to_all(outgoing, "inst", split_axis=0, concat_axis=0, tiled=True)
+    order = ring_order(lax.axis_size("tensor"))
+    chunks, codes = project_chunks(
+        hidden_rows, fresh, gain, kv_weight, order, move_dest, move_len, mine, capacity, owned
+    )
+    ahead, behind, own = ring_sums(chunks)
+    crossing_rows, kept = finish(codes, ahead, behind, own, sent)
+
+    def second_pass():
+        cross = half_of(move_dest) != half_of(mine)
+        index = jnp.arange(requests, dtype=jnp.int32)
+        sooner = (cross[:, None] > cross[None, :]) | (
+            (cross[:, None] == cross[None, :]) & (index[:, None] < index[None, :])
+        )
+        start = jnp.sum(jnp.where(sooner, move_len[:, None], 0), axis=0)
+        position = jnp.arange(context, dtype=jnp.int32)[None, :]
+        target = jnp.where(position < move_len[:, None], start[:, None] + position, -1)
+        return remaining_rows(
+            hidden_rows, gain, kv_weight, codes, target.reshape(-1), capacity, owned
+        )
+
+    rest = lax.cond(
+        jnp.sum(move_len) > capacity,
+        second_pass,
+        lambda: jnp.zeros((leaving - capacity, owned), BF),
+    )
+
+    halves = [(i, i ^ 2) for i in range(instances)]
+    planes = [[i for i in range(instances) if half_of(i) == half] for half in range(2)]
+
+    def over_plane(rows):
+        return lax.all_to_all(
+            rows, "inst", split_axis=0, concat_axis=0, tiled=True, axis_index_groups=planes
+        )
+
+    received = lax.ppermute(crossing_rows, "inst", halves)
+    near = over_plane(place(place_staying, plane, owned, codes, kept, rest))
+    crossing = place(place_crossing, plane, owned, received)
+
+    def all_crossing():
+        rows = jnp.concatenate([kept[:capacity], rest], axis=0)
+        rows = lax.ppermute(rows, "inst", halves)
+        notes = lax.ppermute(codes, "inst", halves)
+        lane = jnp.arange(leaving, dtype=jnp.int32)[None, :]
+        slot = jnp.arange(plane * context, dtype=jnp.int32)[:, None]
+        route = (slot == notes[0:1]) & (lane < notes[1:2])
+        return routed(route.astype(F32), rows).reshape(crossing.shape)
+
+    theirs = received[sent + 2, 0].astype(F32) * context + received[sent + 3, 0].astype(F32)
+    most = jnp.maximum(theirs, codes[1, 0].astype(F32))
+    crossing = lax.cond(most > sent, all_crossing, lambda: crossing)
+    far = over_plane(crossing)
     return tuple(
         rebuild(
-            arrived,
+            mine,
+            near,
+            far,
             resident_cache,
             resident_valid,
             queries,
-            fresh_kv,
+            kept,
             wanted,
-            requests * context,
+            leaving,
         )
     )
 

time: 131 us -> 123 us (0.939)
  the two profiles are of different devices: /device:TPU:33 before, /device:TPU:97 now
where the time goes in v3:
time: 123 us; the launch traced here: 122 us
  starting transfers between devices  62.8 us (51%)
  waiting for transfers between devices  26.4 us (21%)
  Pallas kernels  18.8 us (15%)
  other arithmetic  5.64 us (5%)
  local copies, waits for them, and re-layouts  5.18 us (4%)
  between operations  3.47 us (3%)
    ppermute x7, starting transfers between devices, ring_sums(): sums[way] = lax.ppermute(chunk, 'tensor', forward if way else backward)  26.4 us
    all_to_all x2, starting transfers between devices, over_plane(): lax.all_to_all(rows, 'inst', split_axis=0, concat_axis=0, tiled=True, axi...  20.6 us
    ppermute x1, starting transfers between devices, shards(): received = lax.ppermute(crossing_rows, 'inst', halves)  15.8 us
    ppermute x1, waiting for transfers between devices, shards(): received = lax.ppermute(crossing_rows, 'inst', halves)  10.2 us
    ppermute x7, waiting for transfers between devices, ring_sums(): sums[way] = lax.ppermute(chunk, 'tensor', forward if way else backward)  8.72 us
    all_to_all x2, waiting for transfers between devices, over_plane(): lax.all_to_all(rows, 'inst', split_axis=0, concat_axis=0, tiled=True, axi...  7.52 us
    pallas_call x1, Pallas kernels, project_chunks(): pl.pallas_call(later_chunks, grid_spec=pltpu.PrefetchScalarGridSpec(num_s...  5.36 us
    pallas_call x1, Pallas kernels, project_chunks(): pl.pallas_call(first_chunks, grid_spec=pltpu.PrefetchScalarGridSpec(num_s...  4.97 us
  transfers between devices with their start and end apart: 10, of which 7 were waited for; matrix products, arithmetic and copies ran while one was open for 7% of the time, Pallas kernels for 6%

profile of v3, /device:TPU:97, one launch (start us, length us, event | category | flops | bytes accessed | tf_op | source)
XLA Modules:
  0.0 122.3 jit_solution(3694911589362463969)
XLA Ops:
  0.6 1.3 %dynamic-slice_bitcast_fusion.order = s32[8]{0:T(128)} fusion(s32[8,8]{1,0:T(8,128)} %constant.65.clone, s32[]{:T(128)S(6)} %select_n.49), kind=kLoop, calls=%fused_computation.44 | loop fusion | bytes 68 | tf_op jit(solution)/shard_map/squeeze | solution.py:190
  1.9 5.0 %first_chunks.1 = (bf16[416,256]{1,0:T(8,128)(2,1)}, bf16[416,256]{1,0:T(8,128)(2,1)}, bf16[400,1024]{1,0:T(8,128)(2,1)}, bf16[16,256]{1,0:T(8,128)(2,1)}, s32[8,512]{1,0:T(8,128)S(1)}) custom-call(s32[8]{0:T(128)} %dynamic-slice_bitcast_fusion.order, s32[32]{0:T(128)} %dest.1, s32[32]{0:T(128)} %length.1, s32[1]{0:T(128)} %bitcast.12.me, ...), custom_call_target="tpu_custom_call" | custom-call | flops 419430400 | bytes 2277376 | tf_op jit(solution)/shard_map/first_chunks/pallas_call | solution.py:130
  6.9 1.9 %collective-permute-start.12 = (bf16[416,256]{1,0:T(8,128)(2,1)}, bf16[416,256]{1,0:T(8,128)(2,1)S(1)}, u32[]{:S(2)}, u32[]{:S(2)}) collective-permute-start(bf16[416,256]{1,0:T(8,128)(2,1)} %get-tuple-element.53), channel_id=1, source_target_pairs={{0,2},{2,4},{4,6},{6,7},{7,5},{5,3},{3,1},{1,0},{8,10},{10,12},{12... | collective-permute-start | bytes 638984 | tf_op jit(solution)/shard_map/ppermute | solution.py:203
  8.8 6.1 %collective-permute-start.16 = (bf16[416,256]{1,0:T(8,128)(2,1)}, bf16[416,256]{1,0:T(8,128)(2,1)S(1)}, u32[]{:S(2)}, u32[]{:S(2)}) collective-permute-start(bf16[416,256]{1,0:T(8,128)(2,1)} %get-tuple-element.59), channel_id=1, source_target_pairs={{2,0},{4,2},{6,4},{7,6},{5,7},{3,5},{1,3},{0,1},{10,8},{12,10},{14... | collective-permute-start | bytes 638984 | tf_op jit(solution)/shard_map/ppermute | solution.py:203
  15.0 5.4 %later_chunks.1 = (bf16[416,256]{1,0:T(8,128)(2,1)}, bf16[416,256]{1,0:T(8,128)(2,1)}, bf16[416,256]{1,0:T(8,128)(2,1)}, bf16[416,256]{1,0:T(8,128)(2,1)}, bf16[...) custom-call(s32[8]{0:T(128)} %dynamic-slice_bitcast_fusion.order, bf16[400,1024]{1,0:T(8,128)(2,1)} %get-tuple-element.54.scaled, ...), custom_call_target="tpu_custom_call" | custom-call | flops 1258291200 | bytes 5193728 | tf_op jit(solution)/shard_map/later_chunks/pallas_call | solution.py:156
  21.3 1.9 %collective-permute-start.13 = (bf16[416,256]{1,0:T(8,128)(2,1)S(1)}, bf16[416,256]{1,0:T(8,128)(2,1)S(1)}, u32[]{:S(2)}, u32[]{:S(2)}) collective-permute-start(bf16[416,256]{1,0:T(8,128)(2,1)S(1)} %add_convert_fusion.9), channel_id=1, source_target_pairs={{0,2},{2,4},{4,6},{6,7},{7,5},{5,3},{3,1},{1,0},{8,10},{10,12},{12... | collective-permute-start | bytes 638984 | tf_op jit(solution)/shard_map/ppermute | solution.py:203
  24.3 6.3 %collective-permute-start.17 = (bf16[416,256]{1,0:T(8,128)(2,1)S(1)}, bf16[416,256]{1,0:T(8,128)(2,1)S(1)}, u32[]{:S(2)}, u32[]{:S(2)}) collective-permute-start(bf16[416,256]{1,0:T(8,128)(2,1)S(1)} %add_convert_fusion.6), channel_id=1, source_target_pairs={{2,0},{4,2},{6,4},{7,6},{5,7},{3,5},{1,3},{0,1},{10,8},{12,10},{14... | collective-permute-start | bytes 638984 | tf_op jit(solution)/shard_map/ppermute | solution.py:203
  32.1 1.9 %collective-permute-start.14 = (bf16[416,256]{1,0:T(8,128)(2,1)S(1)}, bf16[416,256]{1,0:T(8,128)(2,1)S(1)}, u32[]{:S(2)}, u32[]{:S(2)}) collective-permute-start(bf16[416,256]{1,0:T(8,128)(2,1)S(1)} %add_convert_fusion.8), channel_id=1, source_target_pairs={{0,2},{2,4},{4,6},{6,7},{7,5},{5,3},{3,1},{1,0},{8,10},{10,12},{12... | collective-permute-start | bytes 638984 | tf_op jit(solution)/shard_map/ppermute | solution.py:203
  34.0 3.3 %collective-permute-done.17 = bf16[416,256]{1,0:T(8,128)(2,1)S(1)} collective-permute-done((bf16[416,256]{1,0:T(8,128)(2,1)S(1)}, bf16[416,256]{1,0:T(8,128)(2,1)S(1)}, u32[]{:S(2)}, u32[]{:S(2)}) %collective-permute-start.17) | collective-permute-done | bytes 213024 | tf_op jit(solution)/shard_map/ppermute | solution.py:203
  37.3 1.0 add_convert_fusion.5
  38.3 5.1 %collective-permute-start.18 = (bf16[416,256]{1,0:T(8,128)(2,1)S(1)}, bf16[416,256]{1,0:T(8,128)(2,1)S(1)}, u32[]{:S(2)}, u32[]{:S(2)}) collective-permute-start(bf16[416,256]{1,0:T(8,128)(2,1)S(1)} %add_convert_fusion.5), channel_id=1, source_target_pairs={{2,0},{4,2},{6,4},{7,6},{5,7},{3,5},{1,3},{0,1},{10,8},{12,10},{14... | collective-permute-start | bytes 638984 | tf_op jit(solution)/shard_map/ppermute | solution.py:203
  43.5 1.0 add_convert_fusion.7
  44.5 3.2 %collective-permute-start.15 = (bf16[416,256]{1,0:T(8,128)(2,1)S(1)}, bf16[416,256]{1,0:T(8,128)(2,1)S(1)}, u32[]{:S(2)}, u32[]{:S(2)}) collective-permute-start(bf16[416,256]{1,0:T(8,128)(2,1)S(1)} %add_convert_fusion.7), channel_id=1, source_target_pairs={{0,2},{2,4},{4,6},{6,7},{7,5},{5,3},{3,1},{1,0},{8,10},{10,12},{12... | collective-permute-start | bytes 638984 | tf_op jit(solution)/shard_map/ppermute | solution.py:203
  49.1 3.8 %collective-permute-done.18.behind = bf16[416,256]{1,0:T(8,128)(2,1)S(1)} collective-permute-done((bf16[416,256]{1,0:T(8,128)(2,1)S(1)}, bf16[416,256]{1,0:T(8,128)(2,1)S(1)}, u32[]{:S(2)}, u32[]{:S(2)}) %collective-permute-start.18) | collective-permute-done | bytes 213024 | tf_op jit(solution)/shard_map/ppermute | solution.py:203
  52.8 1.0 collective-permute-done.15.ahead
  54.5 1.9 %finish_rows.1 = (bf16[256,256]{1,0:T(8,128)(2,1)}, bf16[400,256]{1,0:T(8,128)(2,1)S(1)}) custom-call(s32[8,512]{1,0:T(8,128)S(1)} %get-tuple-element.52.codes, bf16[416,256]{1,0:T(8,128)(2,1)} %copy-done.4, bf16[416,256]{1,0:T(8,128)(2,1)} %copy-done.3, bf16[416,256]{1,0:T(8,128)(2,1)} %get-tuple-element.62.own), custom_call_target="tpu_custom_call" | custom-call | tf_op jit(solution)/shard_map/finish_rows/pallas_call | solution.py:237
  56.4 1.1 place_staying.1
  57.5 13.1 %all-to-all-start = ((bf16[32,16,256]{2,1,0:T(8,128)(2,1)}), bf16[32,16,256]{2,1,0:T(8,128)(2,1)S(1)}, u32[]{:S(2)}, u32[]{:S(2)}) async-start(bf16[32,16,256]{2,1,0:T(8,128)(2,1)} %place_staying.1), calls=%async_computation | async-start | bytes 524288 | tf_op jit(solution)/shard_map/all_to_all | solution.py:463
  70.6 15.8 %collective-permute-start.19 = (bf16[256,256]{1,0:T(8,128)(2,1)}, bf16[256,256]{1,0:T(8,128)(2,1)S(1)}, u32[]{:S(2)}, u32[]{:S(2)}) collective-permute-start(bf16[256,256]{1,0:T(8,128)(2,1)} %get-tuple-element.64), channel_id=1, source_target_pairs={{0,16},{8,24},{16,0},{24,8},{32,48},{40,56},{48,32},{56,40},{64,80... | collective-permute-start | bytes 393224 | tf_op jit(solution)/shard_map/ppermute | solution.py:467
  87.6 10.2 %collective-permute-done.19.received = bf16[256,256]{1,0:T(8,128)(2,1)S(1)} collective-permute-done((bf16[256,256]{1,0:T(8,128)(2,1)}, bf16[256,256]{1,0:T(8,128)(2,1)S(1)}, u32[]{:S(2)}, u32[]{:S(2)}) %collective-permute-start.19) | collective-permute-done | bytes 131104 | tf_op jit(solution)/shard_map/ppermute | solution.py:467
  99.7 1.9 %place_crossing.1 = bf16[32,16,256]{2,1,0:T(8,128)(2,1)} custom-call(bf16[256,256]{1,0:T(8,128)(2,1)} %copy-done.5), custom_call_target="tpu_custom_call" | custom-call | tf_op jit(solution)/shard_map/place_crossing/pallas_call | solution.py:273
  101.5 7.5 %all-to-all-start.1 = ((bf16[32,16,256]{2,1,0:T(8,128)(2,1)}), bf16[32,16,256]{2,1,0:T(8,128)(2,1)S(1)}, u32[]{:S(2)}, u32[]{:S(2)}) async-start(bf16[32,16,256]{2,1,0:T(8,128)(2,1)} %get-tuple-element.84), calls=%async_computation.1 | async-start | bytes 524288 | tf_op jit(solution)/shard_map/all_to_all | solution.py:463
  110.5 7.5 %all-to-all-done.1.far = bf16[32,16,256]{2,1,0:T(8,128)(2,1)S(1)} async-done(((bf16[32,16,256]{2,1,0:T(8,128)(2,1)}), bf16[32,16,256]{2,1,0:T(8,128)(2,1)S(1)}, u32[]{:S(2)}, u32[]{:S(2)}) %all-to-all-start.1) | async-done | bytes 262176 | tf_op jit(solution)/shard_map/all_to_all | solution.py:463
  118.7 3.6 %rebuild_and_attend.1 = (bf16[256,512]{1,0:T(8,128)(2,1)}, bf16[2,16,1024]{2,1,0:T(8,128)(2,1)}) custom-call(s32[1]{0:T(128)} %bitcast.12.me, bf16[32,16,256]{2,1,0:T(8,128)(2,1)} %copy-done.1, bf16[32,16,256]{2,1,0:T(8,128)(2,1)} %copy-done.2, bf16[256,256]{1,0:T(8,128)(2,1)} %resident.1, s32[1,256]{1,0:T(1,128)} %reshape.128.resident_valid, ...), custom_call_target="tpu_custom_call" | custom-call | tf_op jit(solution)/shard_map/rebuild_and_attend/pallas_call | solution.py:367
  (40 shorter events, 8.2 us)
Async XLA Ops:
  6.9 13.4 %collective-permute-start.12 = (bf16[416,256]{1,0:T(8,128)(2,1)}, bf16[416,256]{1,0:T(8,128)(2,1)S(1)}, u32[]{:S(2)}, u32[]{:S(2)}) collective-permute-start(bf16[416,256]{1,0:T(8,128)(2,1)} %get-tuple-element.53), channel_id=1, source_target_pairs={{0,2},{2,4},{4,6},{6,7},{7,5},{5,3},{3,1},{1,0},{8,10},{10,12},{12... | collective-permute-start | bytes 638984 | tf_op jit(solution)/shard_map/ppermute | solution.py:203
  8.8 14.5 %collective-permute-start.16 = (bf16[416,256]{1,0:T(8,128)(2,1)}, bf16[416,256]{1,0:T(8,128)(2,1)S(1)}, u32[]{:S(2)}, u32[]{:S(2)}) collective-permute-start(bf16[416,256]{1,0:T(8,128)(2,1)} %get-tuple-element.59), channel_id=1, source_target_pairs={{2,0},{4,2},{6,4},{7,6},{5,7},{3,5},{1,3},{0,1},{10,8},{12,10},{14... | collective-permute-start | bytes 638984 | tf_op jit(solution)/shard_map/ppermute | solution.py:203
  14.9 32.8 %copy-start.7 = (s32[32]{0:T(128)S(1)}, s32[32]{0:T(128)}, u32[]{:S(2)}) copy-start(s32[32]{0:T(128)} %length.1) | copy-start | bytes 388
  14.9 34.1 %copy-start = (bf16[512,1024]{1,0:T(8,128)(2,1)S(1)}, bf16[512,1024]{1,0:T(8,128)(2,1)}, u32[]{:S(2)}) copy-start(bf16[512,1024]{1,0:T(8,128)(2,1)} %hidden.1) | copy-start | bytes 3145732
  14.9 34.1 %copy-start.6 = (f32[1024]{0:T(1024)S(1)}, f32[1024]{0:T(1024)}, u32[]{:S(2)}) copy-start(f32[1024]{0:T(1024)} %param.18) | copy-start | bytes 12292
  14.9 34.1 %copy-start.8 = (s32[32]{0:T(128)S(1)}, s32[32]{0:T(128)}, u32[]{:S(2)}) copy-start(s32[32]{0:T(128)} %dest.1) | copy-start | bytes 388
  21.3 9.8 %collective-permute-start.13 = (bf16[416,256]{1,0:T(8,128)(2,1)S(1)}, bf16[416,256]{1,0:T(8,128)(2,1)S(1)}, u32[]{:S(2)}, u32[]{:S(2)}) collective-permute-start(bf16[416,256]{1,0:T(8,128)(2,1)S(1)} %add_convert_fusion.9), channel_id=1, source_target_pairs={{0,2},{2,4},{4,6},{6,7},{7,5},{5,3},{3,1},{1,0},{8,10},{10,12},{12... | collective-permute-start | bytes 638984 | tf_op jit(solution)/shard_map/ppermute | solution.py:203
  24.3 13.1 %collective-permute-start.17 = (bf16[416,256]{1,0:T(8,128)(2,1)S(1)}, bf16[416,256]{1,0:T(8,128)(2,1)S(1)}, u32[]{:S(2)}, u32[]{:S(2)}) collective-permute-start(bf16[416,256]{1,0:T(8,128)(2,1)S(1)} %add_convert_fusion.6), channel_id=1, source_target_pairs={{2,0},{4,2},{6,4},{7,6},{5,7},{3,5},{1,3},{0,1},{10,8},{12,10},{14... | collective-permute-start | bytes 638984 | tf_op jit(solution)/shard_map/ppermute | solution.py:203
  32.1 11.3 %collective-permute-start.14 = (bf16[416,256]{1,0:T(8,128)(2,1)S(1)}, bf16[416,256]{1,0:T(8,128)(2,1)S(1)}, u32[]{:S(2)}, u32[]{:S(2)}) collective-permute-start(bf16[416,256]{1,0:T(8,128)(2,1)S(1)} %add_convert_fusion.8), channel_id=1, source_target_pairs={{0,2},{2,4},{4,6},{6,7},{7,5},{5,3},{3,1},{1,0},{8,10},{10,12},{12... | collective-permute-start | bytes 638984 | tf_op jit(solution)/shard_map/ppermute | solution.py:203
  38.3 14.5 %collective-permute-start.18 = (bf16[416,256]{1,0:T(8,128)(2,1)S(1)}, bf16[416,256]{1,0:T(8,128)(2,1)S(1)}, u32[]{:S(2)}, u32[]{:S(2)}) collective-permute-start(bf16[416,256]{1,0:T(8,128)(2,1)S(1)} %add_convert_fusion.5), channel_id=1, source_target_pairs={{2,0},{4,2},{6,4},{7,6},{5,7},{3,5},{1,3},{0,1},{10,8},{12,10},{14... | collective-permute-start | bytes 638984 | tf_op jit(solution)/shard_map/ppermute | solution.py:203
  44.5 9.4 %collective-permute-start.15 = (bf16[416,256]{1,0:T(8,128)(2,1)S(1)}, bf16[416,256]{1,0:T(8,128)(2,1)S(1)}, u32[]{:S(2)}, u32[]{:S(2)}) collective-permute-start(bf16[416,256]{1,0:T(8,128)(2,1)S(1)} %add_convert_fusion.7), channel_id=1, source_target_pairs={{0,2},{2,4},{4,6},{6,7},{7,5},{5,3},{3,1},{1,0},{8,10},{10,12},{12... | collective-permute-start | bytes 638984 | tf_op jit(solution)/shard_map/ppermute | solution.py:203
  49.1 60.0 %copy-start.9 = (s32[16]{0:T(128)S(1)}, s32[16]{0:T(128)}, u32[]{:S(2)}) copy-start(s32[16]{0:T(128)} %param.25) | copy-start | bytes 196
  49.1 60.7 %copy-start.10 = (s32[16]{0:T(128)S(1)}, s32[16]{0:T(128)}, u32[]{:S(2)}) copy-start(s32[16]{0:T(128)} %param.24) | copy-start | bytes 196
  52.8 1.0 copy-start.3
  53.9 0.7 copy-start.4
  57.5 44.0 %all-to-all-start = ((bf16[32,16,256]{2,1,0:T(8,128)(2,1)}), bf16[32,16,256]{2,1,0:T(8,128)(2,1)S(1)}, u32[]{:S(2)}, u32[]{:S(2)}) async-start(bf16[32,16,256]{2,1,0:T(8,128)(2,1)} %place_staying.1), calls=%async_computation | async-start | bytes 524288 | tf_op jit(solution)/shard_map/all_to_all | solution.py:463
  70.6 27.2 %collective-permute-start.19 = (bf16[256,256]{1,0:T(8,128)(2,1)}, bf16[256,256]{1,0:T(8,128)(2,1)S(1)}, u32[]{:S(2)}, u32[]{:S(2)}) collective-permute-start(bf16[256,256]{1,0:T(8,128)(2,1)} %get-tuple-element.64), channel_id=1, source_target_pairs={{0,16},{8,24},{16,0},{24,8},{32,48},{40,56},{48,32},{56,40},{64,80... | collective-permute-start | bytes 393224 | tf_op jit(solution)/shard_map/ppermute | solution.py:467
  97.8 1.9 %copy-start.5 = (bf16[256,256]{1,0:T(8,128)(2,1)}, bf16[256,256]{1,0:T(8,128)(2,1)S(1)}, u32[]{:S(2)}) copy-start(bf16[256,256]{1,0:T(8,128)(2,1)S(1)} %collective-permute-done.19.received) | copy-start | bytes 393220
  101.5 16.5 %copy-start.1 = (bf16[32,16,256]{2,1,0:T(8,128)(2,1)}, bf16[32,16,256]{2,1,0:T(8,128)(2,1)S(1)}, u32[]{:S(2)}) copy-start(bf16[32,16,256]{2,1,0:T(8,128)(2,1)S(1)} %all-to-all-done.near) | copy-start | bytes 786436
  101.5 16.5 %all-to-all-start.1 = ((bf16[32,16,256]{2,1,0:T(8,128)(2,1)}), bf16[32,16,256]{2,1,0:T(8,128)(2,1)S(1)}, u32[]{:S(2)}, u32[]{:S(2)}) async-start(bf16[32,16,256]{2,1,0:T(8,128)(2,1)} %get-tuple-element.84), calls=%async_computation.1 | async-start | bytes 524288 | tf_op jit(solution)/shard_map/all_to_all | solution.py:463
  118.0 0.7 copy-start.2

commit v4 on v3

--- a/solution.py
+++ b/solution.py
@@ -1,3 +1,5 @@
+import functools
+
 import jax
 import jax.numpy as jnp
 from jax import lax
@@ -16,7 +18,7 @@
 ABSENT = 2.0**100
 BF = jnp.bfloat16
 F32 = jnp.float32
-VMEM_BYTES = 60 * 1024 * 1024
+VMEM_BYTES = 32 * 1024 * 1024
 
 
 def ring_of(tensors):
@@ -39,13 +41,26 @@
     return (instance >> 1) & 1
 
 
+def weight_copy(weight, blocks, sems, offset, place):
+    tensors, lanes = lax.axis_size("tensor"), blocks.shape[2]
+    me = lax.axis_index("tensor")
+    at = jnp.where(me % 2 == 0, me // 2, tensors - 1 - me // 2)
+    at = (at + offset + tensors) % tensors
+    owner = jnp.where(at < (tensors + 1) // 2, 2 * at, 2 * (tensors - at) - 1)
+    columns = pl.ds(pl.multiple_of(owner * lanes, lanes), lanes)
+    return pltpu.make_async_copy(weight.at[:, columns], blocks.at[place], sems.at[place])
+
+
 def first_chunks(
-    order, dest, length, me, hidden, fresh, gain, weight_a, weight_b, out_a, out_b, scaled, extra, codes
+    offsets, dest, length, hidden, fresh, gain, weight, out_a, out_b, scaled, extra, codes, blocks, sems
 ):
+    copies = [weight_copy(weight, blocks, sems, offset, i) for i, offset in enumerate(offsets)]
+    for copy in copies:
+        copy.start()
     requests = dest.shape[0]
     context = hidden.shape[0] // requests
     rows, capacity = scaled.shape[0], scaled.shape[0] - fresh.shape[0]
-    half = half_of(me[0])
+    half = half_of(lax.axis_index("inst"))
 
     def crosses(j):
         return half_of(dest[j]) != half
@@ -92,81 +107,66 @@
             part = jnp.concatenate([part, jnp.zeros((EXTRA, lanes - stop + start), F32)], axis=1)
         total = jnp.where(iota((EXTRA, lanes), 0) == index, part, total)
     extra[...] = total.astype(BF)
-    for weight, out in ((weight_a, out_a), (weight_b, out_b)):
-        out[:rows, :] = dot(scaled[...], weight[...]).astype(BF)
+    for place_here, out in enumerate((out_a, out_b)):
+        copies[place_here].wait()
+        out[:rows, :] = dot(scaled[...], blocks[place_here]).astype(BF)
         out[rows:, :] = extra[...]
 
 
-def later_chunks(order, scaled, extra, *refs):
-    count = len(refs) // 2
+def later_chunks(offsets, scaled, extra, weight, *refs):
+    outs, (blocks, sems) = refs[:-2], refs[-2:]
+    copies = [weight_copy(weight, blocks, sems, offset, i) for i, offset in enumerate(offsets)]
+    for copy in copies:
+        copy.start()
     rows = scaled.shape[0]
-    for weight, out in zip(refs[:count], refs[count:]):
-        out[:rows, :] = dot(scaled[...], weight[...]).astype(BF)
+    for place_here, out in enumerate(outs):
+        copies[place_here].wait()
+        out[:rows, :] = dot(scaled[...], blocks[place_here]).astype(BF)
         out[rows:, :] = extra[...]
 
 
-def whole(shape):
-    return pl.BlockSpec(shape, lambda i, *_: (0,) * len(shape))
-
-
-def project_chunks(hidden, fresh, gain, weight, order, dest, length, me, capacity, lanes):
+def project_chunks(hidden, fresh, gain, weight, dest, length, capacity, lanes):
     rows, depth = capacity + fresh.shape[0], hidden.shape[1]
     chunk = jax.ShapeDtypeStruct((rows + EXTRA, lanes), BF)
-    chunk_spec = whole((rows + EXTRA, lanes))
-    scaled_type = jax.ShapeDtypeStruct((rows, depth), BF)
-    extra_type = jax.ShapeDtypeStruct((EXTRA, lanes), BF)
-    codes_type = jax.ShapeDtypeStruct((8, hidden.shape[0]), jnp.int32)
-    tensors = order.shape[0]
-
-    def column_block(place):
-        return pl.BlockSpec((depth, lanes), lambda i, order, *_: (0, order[place]))
-
-    params = pltpu.CompilerParams(vmem_limit_bytes=VMEM_BYTES)
-    cost = lambda count: pl.CostEstimate(
-        flops=2 * rows * depth * lanes * count,
-        bytes_accessed=2 * (rows * depth + count * (depth + rows) * lanes),
-        transcendentals=0,
-    )
+    offsets = ring_offsets(lax.axis_size("tensor"))
+    vmem = pl.BlockSpec(memory_space=pltpu.VMEM)
+    smem = pl.BlockSpec(memory_space=pltpu.SMEM)
+    hbm = pl.BlockSpec(memory_space=pltpu.HBM)
+
+    def options(count, name):
+        return dict(
+            scratch_shapes=[
+                pltpu.VMEM((count, depth, lanes), BF),
+                pltpu.SemaphoreType.DMA((count,)),
+            ],
+            compiler_params=pltpu.CompilerParams(vmem_limit_bytes=VMEM_BYTES),
+            cost_estimate=pl.CostEstimate(
+                flops=2 * rows * depth * lanes * count,
+                bytes_accessed=2 * (rows * depth + count * (depth + rows) * lanes),
+                transcendentals=0,
+            ),
+            name=name,
+        )
+
     out_a, out_b, scaled, extra, codes = pl.pallas_call(
-        first_chunks,
-        grid_spec=pltpu.PrefetchScalarGridSpec(
-            num_scalar_prefetch=4,
-            grid=(1,),
-            in_specs=[
-                whole(hidden.shape),
-                whole(fresh.shape),
-                whole(gain.shape),
-                column_block(0),
-                column_block(1),
-            ],
-            out_specs=[
-                chunk_spec,
-                chunk_spec,
-                whole(scaled_type.shape),
-                whole(extra_type.shape),
-                whole(codes_type.shape),
-            ],
-        ),
-        out_shape=[chunk, chunk, scaled_type, extra_type, codes_type],
-        compiler_params=params,
-        cost_estimate=cost(2),
-        name="first_chunks",
-    )(order, dest, length, me, hidden, fresh, gain, weight, weight)
-    rest = tensors - 2
+        functools.partial(first_chunks, offsets[:2]),
+        in_specs=[smem, smem, vmem, vmem, vmem, hbm],
+        out_shape=[
+            chunk,
+            chunk,
+            jax.ShapeDtypeStruct((rows, depth), BF),
+            jax.ShapeDtypeStruct((EXTRA, lanes), BF),
+            jax.ShapeDtypeStruct((8, hidden.shape[0]), jnp.int32),
+        ],
+        **options(2, "first_chunks"),
+    )(dest, length, hidden, fresh, gain, weight)
+    rest = len(offsets) - 2
     later = pl.pallas_call(
-        later_chunks,
-        grid_spec=pltpu.PrefetchScalarGridSpec(
-            num_scalar_prefetch=1,
-            grid=(1,),
-            in_specs=[whole(scaled.shape), whole(extra.shape)]
-            + [column_block(2 + i) for i in range(rest)],
-            out_specs=[chunk_spec] * rest,
-        ),
+        functools.partial(later_chunks, offsets[2:]),
+        in_specs=[vmem, vmem, hbm],
         out_shape=[chunk] * rest,
-        compiler_params=params,
-        cost_estimate=cost(rest),
-        name="later_chunks",
-    )(order, scaled, extra, *([weight] * rest))
+        **options(rest, "later_chunks"),
+    )(scaled, extra, weight)
     return [out_a, out_b, *later], codes
 
 
@@ -260,41 +260,44 @@
     out[...] = routed(jnp.where(route, 1.0, 0.0), rows).reshape(out.shape)
 
 
-def place_crossing(received, out):
-    slots, context, lanes = out.shape
+def place_crossing(received, codes, near, out, most):
+    slots, context, lanes = near.shape
     sent = received.shape[0] - EXTRA
     notes = received[sent:, :].astype(F32).astype(jnp.int32)
     code = notes[0:1, :sent] * context + notes[1:2, :sent]
     route = iota((slots * context, sent), 0) == code
-    out[...] = routed(jnp.where(route, 1.0, 0.0), received[:sent, :]).reshape(out.shape)
-
-
-def place(kernel, slots, lanes, *operands):
+    out[:, :context, :] = near[...]
+    out[:, context:, :] = routed(jnp.where(route, 1.0, 0.0), received[:sent, :]).reshape(near.shape)
+    theirs = notes[2:3, :TILE] * context + notes[3:4, :TILE]
+    most[...] = jnp.broadcast_to(jnp.maximum(theirs, codes[1:2, :1]), most.shape)
+
+
+def place(kernel, out_shape, *operands):
     return pl.pallas_call(
         kernel,
-        out_shape=jax.ShapeDtypeStruct((slots, CONTEXT, lanes), BF),
+        out_shape=out_shape,
         compiler_params=pltpu.CompilerParams(vmem_limit_bytes=VMEM_BYTES),
         name=kernel.__name__,
     )(*operands)
 
 
 def rebuild_and_attend(
-    me, near, far, resident, resident_valid, queries, kept, wanted, rebuilt, attended
+    arrived, resident, resident_valid, queries, kept, wanted, rebuilt, attended
 ):
-    plane, context, lanes = near.shape
-    slots = 2 * plane
+    plane, context, lanes = arrived.shape
+    slots, context = 2 * plane, context // 2
     steps, batch, width = queries.shape
     rows = slots * context
     fresh = kept[kept.shape[0] - steps * batch :, :]
     columns = rebuilt.shape[1]
     held = resident.shape[1]
     heads = width // HD
-    blocks = jnp.concatenate([near[...], far[...]], axis=0).reshape(rows, lanes)
-    half = half_of(me[0])
+    blocks = arrived[...].reshape(rows, lanes)
+    half = half_of(lax.axis_index("inst"))
 
     def instance_of(slot):
-        place = slot % plane
-        there = jnp.where(slot < plane, half, 1 - half)
+        place = slot >> 1
+        there = jnp.where(slot % 2 == 0, half, 1 - half)
         return (place >> 1) * 4 + there * 2 + (place & 1)
 
     valid = blocks[:, :TILE].astype(F32) < ABSENT / 2
@@ -362,18 +365,16 @@
             attended[s, :, h * HD : (h + 1) * HD] = out[start : start + batch]
 
 
-def rebuild(me, near, far, resident, resident_valid, queries, kept, wanted, columns):
-    vmem = pl.BlockSpec(memory_space=pltpu.VMEM)
+def rebuild(arrived, resident, resident_valid, queries, kept, wanted, columns):
     return pl.pallas_call(
         rebuild_and_attend,
-        in_specs=[pl.BlockSpec(memory_space=pltpu.SMEM)] + [vmem] * 7,
         out_shape=[
-            jax.ShapeDtypeStruct((near.shape[2], columns), BF),
+            jax.ShapeDtypeStruct((arrived.shape[2], columns), BF),
             jax.ShapeDtypeStruct(queries.shape, BF),
         ],
         compiler_params=pltpu.CompilerParams(vmem_limit_bytes=VMEM_BYTES),
         name="rebuild_and_attend",
-    )(me, near, far, resident, resident_valid, queries, kept, wanted)
+    )(arrived, resident, resident_valid, queries, kept, wanted)
 
 
 def remaining_rows(hidden, gain, weight, codes, target_of, capacity, lanes):
@@ -430,9 +431,8 @@
     resident_valid = resident_valid.reshape(1, -1)
     wanted = jnp.tile(decode_ids, steps * heads)[:, None]
 
-    order = ring_order(lax.axis_size("tensor"))
     chunks, codes = project_chunks(
-        hidden_rows, fresh, gain, kv_weight, order, move_dest, move_len, mine, capacity, owned
+        hidden_rows, fresh, gain, kv_weight, move_dest, move_len, capacity, owned
     )
     ahead, behind, own = ring_sums(chunks)
     crossing_rows, kept = finish(codes, ahead, behind, own, sent)
@@ -459,14 +459,12 @@
     halves = [(i, i ^ 2) for i in range(instances)]
     planes = [[i for i in range(instances) if half_of(i) == half] for half in range(2)]
 
-    def over_plane(rows):
-        return lax.all_to_all(
-            rows, "inst", split_axis=0, concat_axis=0, tiled=True, axis_index_groups=planes
-        )
-
     received = lax.ppermute(crossing_rows, "inst", halves)
-    near = over_plane(place(place_staying, plane, owned, codes, kept, rest))
-    crossing = place(place_crossing, plane, owned, received)
+    near_type = jax.ShapeDtypeStruct((plane, context, owned), BF)
+    near = place(place_staying, near_type, codes, kept, rest)
+    both_type = jax.ShapeDtypeStruct((plane, 2 * context, owned), BF)
+    most_type = jax.ShapeDtypeStruct((8, TILE), jnp.int32)
+    outgoing, most = place(place_crossing, (both_type, most_type), received, codes, near)
 
     def all_crossing():
         rows = jnp.concatenate([kept[:capacity], rest], axis=0)
@@ -475,24 +473,15 @@
         lane = jnp.arange(leaving, dtype=jnp.int32)[None, :]
         slot = jnp.arange(plane * context, dtype=jnp.int32)[:, None]
         route = (slot == notes[0:1]) & (lane < notes[1:2])
-        return routed(route.astype(F32), rows).reshape(crossing.shape)
-
-    theirs = received[sent + 2, 0].astype(F32) * context + received[sent + 3, 0].astype(F32)
-    most = jnp.maximum(theirs, codes[1, 0].astype(F32))
-    crossing = lax.cond(most > sent, all_crossing, lambda: crossing)
-    far = over_plane(crossing)
+        far = routed(route.astype(F32), rows).reshape(near.shape)
+        return jnp.concatenate([near, far], axis=1)
+
+    outgoing = lax.cond(most[0, 0] > sent, all_crossing, lambda: outgoing)
+    arrived = lax.all_to_all(
+        outgoing, "inst", split_axis=0, concat_axis=0, tiled=True, axis_index_groups=planes
+    )
     return tuple(
-        rebuild(
-            mine,
-            near,
-            far,
-            resident_cache,
-            resident_valid,
-            queries,
-            kept,
-            wanted,
-            leaving,
-        )
+        rebuild(arrived, resident_cache, resident_valid, queries, kept, wanted, leaving)
     )
 
 

time: 123 us -> 104 us (0.85)
  the two profiles are of different devices: /device:TPU:97 before, /device:TPU:33 now
where the time goes in v4:
time: 104 us
  starting transfers between devices  64.1 us (62%)
  waiting for transfers between devices  23 us (22%)
  Pallas kernels  12 us (12%)
  between operations  2.25 us (2%)
  local copies, waits for them, and re-layouts  1.59 us (2%)
    ppermute x7, starting transfers between devices, ring_sums(): sums[way] = lax.ppermute(chunk, 'tensor', forward if way else backward)  30.4 us
    all_to_all x1, starting transfers between devices, shards(): lax.all_to_all(outgoing, 'inst', split_axis=0, concat_axis=0, tiled=True,...  23.8 us
    all_to_all x1, waiting for transfers between devices, shards(): lax.all_to_all(outgoing, 'inst', split_axis=0, concat_axis=0, tiled=True,...  11.3 us
    ppermute x1, starting transfers between devices, shards(): received = lax.ppermute(crossing_rows, 'inst', halves)  9.91 us
    ppermute x7, waiting for transfers between devices, ring_sums(): sums[way] = lax.ppermute(chunk, 'tensor', forward if way else backward)  8.83 us
    pallas_call x1, Pallas kernels, project_chunks(): pl.pallas_call(functools.partial(later_chunks, offsets[2:]), in_specs=[vm...  3.99 us
    pallas_call x1, Pallas kernels, project_chunks(): pl.pallas_call(functools.partial(first_chunks, offsets[:2]), in_specs=[sm...  3.88 us
    ppermute x1, waiting for transfers between devices, shards(): received = lax.ppermute(crossing_rows, 'inst', halves)  2.81 us
  transfers between devices with their start and end apart: 9, of which 6 were waited for; matrix products, arithmetic and copies ran while one was open for 1% of the time, Pallas kernels for 4%

profile of v4, /device:TPU:33, one launch (start us, length us, event | category | flops | bytes accessed | tf_op | source)
XLA Modules:
  0.0 103.9 jit_solution(14419290713196273819)
XLA Ops:
  0.6 0.8 copy-done.1
  1.5 3.9 %first_chunks.1 = (bf16[416,256]{1,0:T(8,128)(2,1)S(1)}, bf16[416,256]{1,0:T(8,128)(2,1)S(1)}, bf16[400,1024]{1,0:T(8,128)(2,1)S(1)}, bf16[16,256]{1,0:T(8,128)(2,1)S(1)}, s32[8,512]{1,0:T(8,128)S(1)}) custom-call(s32[32]{0:T(128)} %dest.1, s32[32]{0:T(128)} %length.1, bf16[512,1024]{1,0:T(8,128)(2,1)} %hidden.1, bf16[32,1024]{1,0:T(8,128)(2,1)S(1)} %bitcast.17, ...), custom_call_target="tpu_custom_call" | custom-call | flops 419430400 | bytes 2277376 | tf_op jit(solution)/shard_map/first_chunks/pallas_call | solution.py:151
  5.4 1.9 %collective-permute-start.12 = (bf16[416,256]{1,0:T(8,128)(2,1)S(1)}, bf16[416,256]{1,0:T(8,128)(2,1)S(1)}, u32[]{:S(2)}, u32[]{:S(2)}) collective-permute-start(bf16[416,256]{1,0:T(8,128)(2,1)S(1)} %get-tuple-element.58), channel_id=1, source_target_pairs={{0,2},{2,4},{4,6},{6,7},{7,5},{5,3},{3,1},{1,0},{8,10},{10,12},{12... | collective-permute-start | bytes 638984 | tf_op jit(solution)/shard_map/ppermute | solution.py:203
  7.3 4.9 %collective-permute-start.16 = (bf16[416,256]{1,0:T(8,128)(2,1)S(1)}, bf16[416,256]{1,0:T(8,128)(2,1)S(1)}, u32[]{:S(2)}, u32[]{:S(2)}) collective-permute-start(bf16[416,256]{1,0:T(8,128)(2,1)S(1)} %get-tuple-element.64), channel_id=1, source_target_pairs={{2,0},{4,2},{6,4},{7,6},{5,7},{3,5},{1,3},{0,1},{10,8},{12,10},{14... | collective-permute-start | bytes 638984 | tf_op jit(solution)/shard_map/ppermute | solution.py:203
  12.3 4.0 %later_chunks.1 = (bf16[416,256]{1,0:T(8,128)(2,1)S(1)}, bf16[416,256]{1,0:T(8,128)(2,1)S(1)}, bf16[416,256]{1,0:T(8,128)(2,1)S(1)}, bf16[416,256]{1,0:T(8,128)(...) custom-call(bf16[400,1024]{1,0:T(8,128)(2,1)S(1)} %get-tuple-element.59.scaled, ...), custom_call_target="tpu_custom_call" | custom-call | flops 1258291200 | bytes 5193728 | tf_op jit(solution)/shard_map/later_chunks/pallas_call | solution.py:164
  16.3 1.9 %collective-permute-start.13 = (bf16[416,256]{1,0:T(8,128)(2,1)S(1)}, bf16[416,256]{1,0:T(8,128)(2,1)S(1)}, u32[]{:S(2)}, u32[]{:S(2)}) collective-permute-start(bf16[416,256]{1,0:T(8,128)(2,1)S(1)} %add_convert_fusion.9), channel_id=1, source_target_pairs={{0,2},{2,4},{4,6},{6,7},{7,5},{5,3},{3,1},{1,0},{8,10},{10,12},{12... | collective-permute-start | bytes 638984 | tf_op jit(solution)/shard_map/ppermute | solution.py:203
  18.3 8.1 %collective-permute-start.17 = (bf16[416,256]{1,0:T(8,128)(2,1)S(1)}, bf16[416,256]{1,0:T(8,128)(2,1)S(1)}, u32[]{:S(2)}, u32[]{:S(2)}) collective-permute-start(bf16[416,256]{1,0:T(8,128)(2,1)S(1)} %add_convert_fusion.6), channel_id=1, source_target_pairs={{2,0},{4,2},{6,4},{7,6},{5,7},{3,5},{1,3},{0,1},{10,8},{12,10},{14... | collective-permute-start | bytes 638984 | tf_op jit(solution)/shard_map/ppermute | solution.py:203
  26.6 4.8 %collective-permute-start.14 = (bf16[416,256]{1,0:T(8,128)(2,1)S(1)}, bf16[416,256]{1,0:T(8,128)(2,1)S(1)}, u32[]{:S(2)}, u32[]{:S(2)}) collective-permute-start(bf16[416,256]{1,0:T(8,128)(2,1)S(1)} %add_convert_fusion.8), channel_id=1, source_target_pairs={{0,2},{2,4},{4,6},{6,7},{7,5},{5,3},{3,1},{1,0},{8,10},{10,12},{12... | collective-permute-start | bytes 638984 | tf_op jit(solution)/shard_map/ppermute | solution.py:203
  31.4 3.3 %collective-permute-done.17 = bf16[416,256]{1,0:T(8,128)(2,1)S(1)} collective-permute-done((bf16[416,256]{1,0:T(8,128)(2,1)S(1)}, bf16[416,256]{1,0:T(8,128)(2,1)S(1)}, u32[]{:S(2)}, u32[]{:S(2)}) %collective-permute-start.17) | collective-permute-done | bytes 213024 | tf_op jit(solution)/shard_map/ppermute | solution.py:203
  34.8 4.8 %collective-permute-start.18 = (bf16[416,256]{1,0:T(8,128)(2,1)S(1)}, bf16[416,256]{1,0:T(8,128)(2,1)S(1)}, u32[]{:S(2)}, u32[]{:S(2)}) collective-permute-start(bf16[416,256]{1,0:T(8,128)(2,1)S(1)} %add_convert_fusion.5), channel_id=1, source_target_pairs={{2,0},{4,2},{6,4},{7,6},{5,7},{3,5},{1,3},{0,1},{10,8},{12,10},{14... | collective-permute-start | bytes 638984 | tf_op jit(solution)/shard_map/ppermute | solution.py:203
  39.6 1.2 %collective-permute-done.14 = bf16[416,256]{1,0:T(8,128)(2,1)S(1)} collective-permute-done((bf16[416,256]{1,0:T(8,128)(2,1)S(1)}, bf16[416,256]{1,0:T(8,128)(2,1)S(1)}, u32[]{:S(2)}, u32[]{:S(2)}) %collective-permute-start.14) | collective-permute-done | bytes 213024 | tf_op jit(solution)/shard_map/ppermute | solution.py:203
  40.8 3.9 %collective-permute-start.15 = (bf16[416,256]{1,0:T(8,128)(2,1)S(1)}, bf16[416,256]{1,0:T(8,128)(2,1)S(1)}, u32[]{:S(2)}, u32[]{:S(2)}) collective-permute-start(bf16[416,256]{1,0:T(8,128)(2,1)S(1)} %add_convert_fusion.7), channel_id=1, source_target_pairs={{0,2},{2,4},{4,6},{6,7},{7,5},{5,3},{3,1},{1,0},{8,10},{10,12},{12... | collective-permute-start | bytes 638984 | tf_op jit(solution)/shard_map/ppermute | solution.py:203
  44.7 4.3 %collective-permute-done.18.behind = bf16[416,256]{1,0:T(8,128)(2,1)S(1)} collective-permute-done((bf16[416,256]{1,0:T(8,128)(2,1)S(1)}, bf16[416,256]{1,0:T(8,128)(2,1)S(1)}, u32[]{:S(2)}, u32[]{:S(2)}) %collective-permute-start.18) | collective-permute-done | bytes 213024 | tf_op jit(solution)/shard_map/ppermute | solution.py:203
  49.0 0.1 finish_rows.1
  49.1 9.9 %collective-permute-start.19 = (bf16[256,256]{1,0:T(8,128)(2,1)S(1)}, bf16[256,256]{1,0:T(8,128)(2,1)S(1)}, u32[]{:S(2)}, u32[]{:S(2)}) collective-permute-start(bf16[256,256]{1,0:T(8,128)(2,1)S(1)} %get-tuple-element.68), channel_id=1, source_target_pairs={{0,16},{8,24},{16,0},{24,8},{32,48},{40,56},{48,32},{56,40},{64,80... | collective-permute-start | bytes 393224 | tf_op jit(solution)/shard_map/ppermute | solution.py:462
  59.1 0.6 reduce_sum.36
  60.5 0.4 place_staying.1.near
  60.9 2.8 %collective-permute-done.19.received = bf16[256,256]{1,0:T(8,128)(2,1)S(1)} collective-permute-done((bf16[256,256]{1,0:T(8,128)(2,1)S(1)}, bf16[256,256]{1,0:T(8,128)(2,1)S(1)}, u32[]{:S(2)}, u32[]{:S(2)}) %collective-permute-start.19) | collective-permute-done | bytes 131104 | tf_op jit(solution)/shard_map/ppermute | solution.py:462
  63.7 1.1 %place_crossing.1 = (bf16[32,32,256]{2,1,0:T(8,128)(2,1)}, s32[8,128]{1,0:T(8,128)S(1)}) custom-call(bf16[256,256]{1,0:T(8,128)(2,1)S(1)} %collective-permute-done.19.received, s32[8,512]{1,0:T(8,128)S(1)} %get-tuple-element.57.codes, bf16[32,16,256]{2,1,0:T(8,128)(2,1)S(1)} %place_staying.1.near), custom_call_target="tpu_custom_call" | custom-call | tf_op jit(solution)/shard_map/place_crossing/pallas_call | solution.py:276
  64.8 0.5 slice.44
  66.0 23.8 %all-to-all-start = ((bf16[32,32,256]{2,1,0:T(8,128)(2,1)}), bf16[32,32,256]{2,1,0:T(8,128)(2,1)S(1)}, u32[]{:S(2)}, u32[]{:S(2)}) async-start(bf16[32,32,256]{2,1,0:T(8,128)(2,1)} %get-tuple-element.92), calls=%async_computation | async-start | bytes 1048576 | tf_op jit(solution)/shard_map/all_to_all | solution.py:480
  89.8 0.1 broadcast_in_dim_tile.4.wanted
  90.1 11.3 %all-to-all-done.arrived = bf16[32,32,256]{2,1,0:T(8,128)(2,1)S(1)} async-done(((bf16[32,32,256]{2,1,0:T(8,128)(2,1)}), bf16[32,32,256]{2,1,0:T(8,128)(2,1)S(1)}, u32[]{:S(2)}, u32[]{:S(2)}) %all-to-all-start) | async-done | bytes 524320 | tf_op jit(solution)/shard_map/all_to_all | solution.py:480
  101.4 2.5 %rebuild_and_attend.1 = (bf16[256,512]{1,0:T(8,128)(2,1)}, bf16[2,16,1024]{2,1,0:T(8,128)(2,1)}) custom-call(bf16[32,32,256]{2,1,0:T(8,128)(2,1)S(1)} %all-to-all-done.arrived, bf16[256,256]{1,0:T(8,128)(2,1)S(1)} %copy-done, s32[1,256]{1,0:T(1,128)S(1)} %reshape.126.resident_valid, bf16[2,16,1024]{2,1,0:T(8,128)(2,1)S(1)} %copy-done.2, ...), custom_call_target="tpu_custom_call" | custom-call | tf_op jit(solution)/shard_map/rebuild_and_attend/pallas_call | solution.py:369
  (34 shorter events, 0.6 us)
Async XLA Ops:
  0.6 0.8 copy-start.1
  1.5 10.7 %copy-start.3 = (bf16[1024,2048]{1,0:T(8,128)(2,1)S(1)}, bf16[1024,2048]{1,0:T(8,128)(2,1)}, u32[]{:S(2)}) copy-start(bf16[1024,2048]{1,0:T(8,128)(2,1)} %weight.3) | copy-start | bytes 12582916
  5.4 10.9 %collective-permute-start.12 = (bf16[416,256]{1,0:T(8,128)(2,1)S(1)}, bf16[416,256]{1,0:T(8,128)(2,1)S(1)}, u32[]{:S(2)}, u32[]{:S(2)}) collective-permute-start(bf16[416,256]{1,0:T(8,128)(2,1)S(1)} %get-tuple-element.58), channel_id=1, source_target_pairs={{0,2},{2,4},{4,6},{6,7},{7,5},{5,3},{3,1},{1,0},{8,10},{10,12},{12... | collective-permute-start | bytes 638984 | tf_op jit(solution)/shard_map/ppermute | solution.py:203
  7.3 11.0 %collective-permute-start.16 = (bf16[416,256]{1,0:T(8,128)(2,1)S(1)}, bf16[416,256]{1,0:T(8,128)(2,1)S(1)}, u32[]{:S(2)}, u32[]{:S(2)}) collective-permute-start(bf16[416,256]{1,0:T(8,128)(2,1)S(1)} %get-tuple-element.64), channel_id=1, source_target_pairs={{2,0},{4,2},{6,4},{7,6},{5,7},{3,5},{1,3},{0,1},{10,8},{12,10},{14... | collective-permute-start | bytes 638984 | tf_op jit(solution)/shard_map/ppermute | solution.py:203
  12.2 46.9 %copy-start.6 = (s32[32]{0:T(128)S(1)}, s32[32]{0:T(128)}, u32[]{:S(2)}) copy-start(s32[32]{0:T(128)} %length.1) | copy-start | bytes 388
  12.2 48.1 %copy-start.4 = (bf16[512,1024]{1,0:T(8,128)(2,1)S(1)}, bf16[512,1024]{1,0:T(8,128)(2,1)}, u32[]{:S(2)}) copy-start(bf16[512,1024]{1,0:T(8,128)(2,1)} %hidden.1) | copy-start | bytes 3145732
  12.2 48.1 %copy-start.5 = (f32[1024]{0:T(1024)S(1)}, f32[1024]{0:T(1024)}, u32[]{:S(2)}) copy-start(f32[1024]{0:T(1024)} %param.17) | copy-start | bytes 12292
  12.2 48.1 %copy-start.7 = (s32[32]{0:T(128)S(1)}, s32[32]{0:T(128)}, u32[]{:S(2)}) copy-start(s32[32]{0:T(128)} %dest.1) | copy-start | bytes 388
  16.3 10.2 %collective-permute-start.13 = (bf16[416,256]{1,0:T(8,128)(2,1)S(1)}, bf16[416,256]{1,0:T(8,128)(2,1)S(1)}, u32[]{:S(2)}, u32[]{:S(2)}) collective-permute-start(bf16[416,256]{1,0:T(8,128)(2,1)S(1)} %add_convert_fusion.9), channel_id=1, source_target_pairs={{0,2},{2,4},{4,6},{6,7},{7,5},{5,3},{3,1},{1,0},{8,10},{10,12},{12... | collective-permute-start | bytes 638984 | tf_op jit(solution)/shard_map/ppermute | solution.py:203
  18.3 16.4 %collective-permute-start.17 = (bf16[416,256]{1,0:T(8,128)(2,1)S(1)}, bf16[416,256]{1,0:T(8,128)(2,1)S(1)}, u32[]{:S(2)}, u32[]{:S(2)}) collective-permute-start(bf16[416,256]{1,0:T(8,128)(2,1)S(1)} %add_convert_fusion.6), channel_id=1, source_target_pairs={{2,0},{4,2},{6,4},{7,6},{5,7},{3,5},{1,3},{0,1},{10,8},{12,10},{14... | collective-permute-start | bytes 638984 | tf_op jit(solution)/shard_map/ppermute | solution.py:203
  26.6 14.1 %collective-permute-start.14 = (bf16[416,256]{1,0:T(8,128)(2,1)S(1)}, bf16[416,256]{1,0:T(8,128)(2,1)S(1)}, u32[]{:S(2)}, u32[]{:S(2)}) collective-permute-start(bf16[416,256]{1,0:T(8,128)(2,1)S(1)} %add_convert_fusion.8), channel_id=1, source_target_pairs={{0,2},{2,4},{4,6},{6,7},{7,5},{5,3},{3,1},{1,0},{8,10},{10,12},{12... | collective-permute-start | bytes 638984 | tf_op jit(solution)/shard_map/ppermute | solution.py:203
  34.8 14.2 %collective-permute-start.18 = (bf16[416,256]{1,0:T(8,128)(2,1)S(1)}, bf16[416,256]{1,0:T(8,128)(2,1)S(1)}, u32[]{:S(2)}, u32[]{:S(2)}) collective-permute-start(bf16[416,256]{1,0:T(8,128)(2,1)S(1)} %add_convert_fusion.5), channel_id=1, source_target_pairs={{2,0},{4,2},{6,4},{7,6},{5,7},{3,5},{1,3},{0,1},{10,8},{12,10},{14... | collective-permute-start | bytes 638984 | tf_op jit(solution)/shard_map/ppermute | solution.py:203
  40.8 8.2 %collective-permute-start.15 = (bf16[416,256]{1,0:T(8,128)(2,1)S(1)}, bf16[416,256]{1,0:T(8,128)(2,1)S(1)}, u32[]{:S(2)}, u32[]{:S(2)}) collective-permute-start(bf16[416,256]{1,0:T(8,128)(2,1)S(1)} %add_convert_fusion.7), channel_id=1, source_target_pairs={{0,2},{2,4},{4,6},{6,7},{7,5},{5,3},{3,1},{1,0},{8,10},{10,12},{12... | collective-permute-start | bytes 638984 | tf_op jit(solution)/shard_map/ppermute | solution.py:203
  49.1 14.5 %collective-permute-start.19 = (bf16[256,256]{1,0:T(8,128)(2,1)S(1)}, bf16[256,256]{1,0:T(8,128)(2,1)S(1)}, u32[]{:S(2)}, u32[]{:S(2)}) collective-permute-start(bf16[256,256]{1,0:T(8,128)(2,1)S(1)} %get-tuple-element.68), channel_id=1, source_target_pairs={{0,16},{8,24},{16,0},{24,8},{32,48},{40,56},{48,32},{56,40},{64,80... | collective-permute-start | bytes 393224 | tf_op jit(solution)/shard_map/ppermute | solution.py:462
  60.4 29.4 %copy-start.8 = (s32[16]{0:T(128)S(1)}, s32[16]{0:T(128)}, u32[]{:S(2)}) copy-start(s32[16]{0:T(128)} %param.24) | copy-start | bytes 196
  60.4 29.5 %copy-start.9 = (s32[16]{0:T(128)S(1)}, s32[16]{0:T(128)}, u32[]{:S(2)}) copy-start(s32[16]{0:T(128)} %param.23) | copy-start | bytes 196
  60.4 41.0 %copy-start = (bf16[256,256]{1,0:T(8,128)(2,1)S(1)}, bf16[256,256]{1,0:T(8,128)(2,1)}, u32[]{:S(2)}) copy-start(bf16[256,256]{1,0:T(8,128)(2,1)} %resident.1) | copy-start | bytes 393220
  60.5 41.0 %copy-start.2 = (bf16[2,16,1024]{2,1,0:T(8,128)(2,1)S(1)}, bf16[2,16,1024]{2,1,0:T(8,128)(2,1)}, u32[]{:S(2)}) copy-start(bf16[2,16,1024]{2,1,0:T(8,128)(2,1)} %queries.1) | copy-start | bytes 196612
  66.0 35.5 %all-to-all-start = ((bf16[32,32,256]{2,1,0:T(8,128)(2,1)}), bf16[32,32,256]{2,1,0:T(8,128)(2,1)S(1)}, u32[]{:S(2)}, u32[]{:S(2)}) async-start(bf16[32,32,256]{2,1,0:T(8,128)(2,1)} %get-tuple-element.92), calls=%async_computation | async-start | bytes 1048576 | tf_op jit(solution)/shard_map/all_to_all | solution.py:480

commit v5 on v4

--- a/solution.py
+++ b/solution.py
@@ -51,9 +51,21 @@
     return pltpu.make_async_copy(weight.at[:, columns], blocks.at[place], sems.at[place])
 
 
+def project(scaled, extra, block, top, bottom):
+    rows, split = scaled.shape[0], top.shape[0]
+    chunk = dot(scaled[...], block[...]).astype(BF)
+    top[...] = chunk[:split]
+    bottom[: rows - split, :] = chunk[split:]
+    bottom[rows - split :, :] = extra[...]
+
+
 def first_chunks(
-    offsets, dest, length, hidden, fresh, gain, weight, out_a, out_b, scaled, extra, codes, blocks, sems
+    offsets, dest, length, hidden_hbm, fresh, gain, weight, *refs
 ):
+    outs, (scaled, extra, codes, blocks, sems, hidden, hidden_sem) = refs[:4], refs[4:]
+    lanes = blocks.shape[2]
+    hidden_copy = pltpu.make_async_copy(hidden_hbm, hidden, hidden_sem)
+    hidden_copy.start()
     copies = [weight_copy(weight, blocks, sems, offset, i) for i, offset in enumerate(offsets)]
     for copy in copies:
         copy.start()
@@ -92,12 +104,12 @@
     )
     codes[...] = jnp.where(iota(codes.shape, 0) == 0, code, crossing)
     select = jnp.where(target == iota((capacity, hidden.shape[0]), 0), 1.0, 0.0).astype(BF)
+    hidden_copy.wait()
     wide = jnp.concatenate([dot(select, hidden[...]), fresh[...].astype(F32)], axis=0)
     scaled[...] = (wide * gain[...]).astype(BF)
     square = wide * wide
     high = square.astype(BF)
     low = (square - high.astype(F32)).astype(BF)
-    lanes = out_a.shape[1]
     ones = jnp.ones((EXTRA, wide.shape[1]), BF)
     total = jnp.zeros((EXTRA, lanes), F32)
     for index, start in enumerate(range(0, rows, lanes)):
@@ -107,10 +119,9 @@
             part = jnp.concatenate([part, jnp.zeros((EXTRA, lanes - stop + start), F32)], axis=1)
         total = jnp.where(iota((EXTRA, lanes), 0) == index, part, total)
     extra[...] = total.astype(BF)
-    for place_here, out in enumerate((out_a, out_b)):
-        copies[place_here].wait()
-        out[:rows, :] = dot(scaled[...], blocks[place_here]).astype(BF)
-        out[rows:, :] = extra[...]
+    for i, copy in enumerate(copies):
+        copy.wait()
+        project(scaled, extra, blocks.at[i], outs[2 * i], outs[2 * i + 1])
 
 
 def later_chunks(offsets, scaled, extra, weight, *refs):
@@ -118,26 +129,29 @@
     copies = [weight_copy(weight, blocks, sems, offset, i) for i, offset in enumerate(offsets)]
     for copy in copies:
         copy.start()
-    rows = scaled.shape[0]
-    for place_here, out in enumerate(outs):
-        copies[place_here].wait()
-        out[:rows, :] = dot(scaled[...], blocks[place_here]).astype(BF)
-        out[rows:, :] = extra[...]
+    for i, copy in enumerate(copies):
+        copy.wait()
+        project(scaled, extra, blocks.at[i], outs[2 * i], outs[2 * i + 1])
 
 
 def project_chunks(hidden, fresh, gain, weight, dest, length, capacity, lanes):
     rows, depth = capacity + fresh.shape[0], hidden.shape[1]
-    chunk = jax.ShapeDtypeStruct((rows + EXTRA, lanes), BF)
+    split = (rows + EXTRA) // 32 * 16
+    pieces = [
+        jax.ShapeDtypeStruct((split, lanes), BF),
+        jax.ShapeDtypeStruct((rows + EXTRA - split, lanes), BF),
+    ]
     offsets = ring_offsets(lax.axis_size("tensor"))
     vmem = pl.BlockSpec(memory_space=pltpu.VMEM)
     smem = pl.BlockSpec(memory_space=pltpu.SMEM)
     hbm = pl.BlockSpec(memory_space=pltpu.HBM)
 
-    def options(count, name):
+    def options(count, name, *more):
         return dict(
             scratch_shapes=[
                 pltpu.VMEM((count, depth, lanes), BF),
                 pltpu.SemaphoreType.DMA((count,)),
+                *more,
             ],
             compiler_params=pltpu.CompilerParams(vmem_limit_bytes=VMEM_BYTES),
             cost_estimate=pl.CostEstimate(
@@ -148,26 +162,29 @@
             name=name,
         )
 
-    out_a, out_b, scaled, extra, codes = pl.pallas_call(
+    *first, scaled, extra, codes = pl.pallas_call(
         functools.partial(first_chunks, offsets[:2]),
-        in_specs=[smem, smem, vmem, vmem, vmem, hbm],
+        in_specs=[smem, smem, hbm, vmem, vmem, hbm],
         out_shape=[
-            chunk,
-            chunk,
+            *pieces,
+            *pieces,
             jax.ShapeDtypeStruct((rows, depth), BF),
             jax.ShapeDtypeStruct((EXTRA, lanes), BF),
             jax.ShapeDtypeStruct((8, hidden.shape[0]), jnp.int32),
         ],
-        **options(2, "first_chunks"),
+        **options(
+            2, "first_chunks", pltpu.VMEM(hidden.shape, BF), pltpu.SemaphoreType.DMA(())
+        ),
     )(dest, length, hidden, fresh, gain, weight)
     rest = len(offsets) - 2
     later = pl.pallas_call(
         functools.partial(later_chunks, offsets[2:]),
         in_specs=[vmem, vmem, hbm],
-        out_shape=[chunk] * rest,
+        out_shape=pieces * rest,
         **options(rest, "later_chunks"),
     )(scaled, extra, weight)
-    return [out_a, out_b, *later], codes
+    every = [*first, *later]
+    return [every[i : i + 2] for i in range(0, len(every), 2)], codes
 
 
 def ring_offsets(tensors):
@@ -195,17 +212,25 @@
     ring = ring_of(tensors)
     forward = [(ring[i], ring[(i + 1) % tensors]) for i in range(tensors)]
     backward = [(b, a) for a, b in forward]
-    sums = {True: None, False: None}
-    for offset, chunk in zip(ring_offsets(tensors), chunks[:-1]):
+    sums = {}
+    for offset, pieces in zip(ring_offsets(tensors), chunks[:-1]):
         way = offset > 0
-        if sums[way] is not None:
-            chunk = (sums[way].astype(F32) + chunk.astype(F32)).astype(BF)
-        sums[way] = lax.ppermute(chunk, "tensor", forward if way else backward)
-    return sums[True], sums[False], chunks[-1]
-
-
-def finish_rows(codes, ahead, behind, own, crossing_rows, kept):
-    total = ahead[...].astype(F32) + behind[...].astype(F32) + own[...].astype(F32)
+        for i, piece in enumerate(pieces):
+            if (way, i) in sums:
+                piece = (sums[way, i].astype(F32) + piece.astype(F32)).astype(BF)
+            sums[way, i] = lax.ppermute(piece, "tensor", forward if way else backward)
+    return [
+        (sums[True, i], sums[False, i], own) for i, own in enumerate(chunks[-1])
+    ]
+
+
+def total_of(parts):
+    return sum(part[...].astype(F32) for part in parts[1:]) + parts[0][...].astype(F32)
+
+
+def finish_rows(codes, *refs):
+    terms, (crossing_rows, kept) = refs[:-2], refs[-2:]
+    total = jnp.concatenate([total_of(terms[:3]), total_of(terms[3:])], axis=0)
     rows, lanes = kept.shape
     squares = total[rows:]
     for start in range(0, rows, TILE):
@@ -232,8 +257,9 @@
     crossing_rows[sent:, :] = notes.astype(F32).astype(BF)
 
 
-def finish(codes, ahead, behind, own, sent):
-    rows, lanes = own.shape[0] - EXTRA, own.shape[1]
+def finish(codes, terms, sent):
+    lanes = terms[0].shape[1]
+    rows = terms[0].shape[0] + terms[3].shape[0] - EXTRA
     return pl.pallas_call(
         finish_rows,
         out_shape=[
@@ -242,7 +268,7 @@
         ],
         compiler_params=pltpu.CompilerParams(vmem_limit_bytes=VMEM_BYTES),
         name="finish_rows",
-    )(codes, ahead, behind, own)
+    )(codes, *terms)
 
 
 def routed(route, rows):
@@ -268,14 +294,15 @@
     route = iota((slots * context, sent), 0) == code
     out[:, :context, :] = near[...]
     out[:, context:, :] = routed(jnp.where(route, 1.0, 0.0), received[:sent, :]).reshape(near.shape)
-    theirs = notes[2:3, :TILE] * context + notes[3:4, :TILE]
-    most[...] = jnp.broadcast_to(jnp.maximum(theirs, codes[1:2, :1]), most.shape)
-
-
-def place(kernel, out_shape, *operands):
+    counts = jnp.maximum(notes[2:3, :sent] * context + notes[3:4, :sent], codes[1:2, :sent])
+    most[0] = jnp.max(counts)
+
+
+def place(kernel, out_shape, out_specs, *operands):
     return pl.pallas_call(
         kernel,
         out_shape=out_shape,
+        out_specs=out_specs,
         compiler_params=pltpu.CompilerParams(vmem_limit_bytes=VMEM_BYTES),
         name=kernel.__name__,
     )(*operands)
@@ -391,10 +418,9 @@
     parts = jnp.dot((wide * gain).astype(BF), weight, preferred_element_type=F32).astype(BF)
     order = ring_order(tensors)
     chunks = [
-        lax.dynamic_slice_in_dim(parts, order[i] * lanes, lanes, 1) for i in range(tensors)
+        [lax.dynamic_slice_in_dim(parts, order[i] * lanes, lanes, 1)] for i in range(tensors)
     ]
-    ahead, behind, own = ring_sums(chunks)
-    total = ahead.astype(F32) + behind.astype(F32) + own.astype(F32)
+    total = total_of(ring_sums(chunks)[0])
     return (total * lax.rsqrt(squares / D + 1e-06)[:, None]).astype(BF)
 
 
@@ -434,8 +460,8 @@
     chunks, codes = project_chunks(
         hidden_rows, fresh, gain, kv_weight, move_dest, move_len, capacity, owned
     )
-    ahead, behind, own = ring_sums(chunks)
-    crossing_rows, kept = finish(codes, ahead, behind, own, sent)
+    terms = [term for piece in ring_sums(chunks) for term in piece]
+    crossing_rows, kept = finish(codes, terms, sent)
 
     def second_pass():
         cross = half_of(move_dest) != half_of(mine)
@@ -461,10 +487,18 @@
 
     received = lax.ppermute(crossing_rows, "inst", halves)
     near_type = jax.ShapeDtypeStruct((plane, context, owned), BF)
-    near = place(place_staying, near_type, codes, kept, rest)
+    vmem = pl.BlockSpec(memory_space=pltpu.VMEM)
+    near = place(place_staying, near_type, vmem, codes, kept, rest)
     both_type = jax.ShapeDtypeStruct((plane, 2 * context, owned), BF)
-    most_type = jax.ShapeDtypeStruct((8, TILE), jnp.int32)
-    outgoing, most = place(place_crossing, (both_type, most_type), received, codes, near)
+    most_type = jax.ShapeDtypeStruct((1,), jnp.int32)
+    outgoing, most = place(
+        place_crossing,
+        (both_type, most_type),
+        (vmem, pl.BlockSpec(memory_space=pltpu.SMEM)),
+        received,
+        codes,
+        near,
+    )
 
     def all_crossing():
         rows = jnp.concatenate([kept[:capacity], rest], axis=0)
@@ -476,7 +510,7 @@
         far = routed(route.astype(F32), rows).reshape(near.shape)
         return jnp.concatenate([near, far], axis=1)
 
-    outgoing = lax.cond(most[0, 0] > sent, all_crossing, lambda: outgoing)
+    outgoing = lax.cond(most[0] > sent, all_crossing, lambda: outgoing)
     arrived = lax.all_to_all(
         outgoing, "inst", split_axis=0, concat_axis=0, tiled=True, axis_index_groups=planes
     )

time: 104 us -> 112 us (1.077)
  the two profiles are of different devices: /device:TPU:33 before, /device:TPU:97 now
where the time goes in v5:
time: 112 us
  starting transfers between devices  76.2 us (68%)
  waiting for transfers between devices  18.4 us (16%)
  Pallas kernels  12.5 us (11%)
  between operations  2.43 us (2%)
    ppermute x14, starting transfers between devices, ring_sums(): sums[way, i] = lax.ppermute(piece, 'tensor', forward if way else backward)  45.8 us
    all_to_all x1, starting transfers between devices, shards(): lax.all_to_all(outgoing, 'inst', split_axis=0, concat_axis=0, tiled=True,...  17.8 us
    ppermute x1, starting transfers between devices, shards(): received = lax.ppermute(crossing_rows, 'inst', halves)  12.6 us
    all_to_all x1, waiting for transfers between devices, shards(): lax.all_to_all(outgoing, 'inst', split_axis=0, concat_axis=0, tiled=True,...  11.3 us
    ppermute x14, waiting for transfers between devices, ring_sums(): sums[way, i] = lax.ppermute(piece, 'tensor', forward if way else backward)  5.71 us
    pallas_call x1, Pallas kernels, project_chunks(): pl.pallas_call(functools.partial(first_chunks, offsets[:2]), in_specs=[sm...  4.45 us
    pallas_call x1, Pallas kernels, project_chunks(): pl.pallas_call(functools.partial(later_chunks, offsets[2:]), in_specs=[vm...  4.03 us
    pallas_call x1, Pallas kernels, rebuild(): pl.pallas_call(rebuild_and_attend, out_shape=[jax.ShapeDtypeStruct((arriv...  2.49 us
  transfers between devices with their start and end apart: 16, of which 4 were waited for; matrix products, arithmetic and copies ran while one was open for 1% of the time, Pallas kernels for 4%

profile of v5, /device:TPU:97, one launch (start us, length us, event | category | flops | bytes accessed | tf_op | source)
XLA Modules:
  0.0 111.7 jit_solution(9688251703485555596)
XLA Ops:
  1.5 4.5 %first_chunks.1 = (bf16[208,256]{1,0:T(8,128)(2,1)S(1)}, bf16[208,256]{1,0:T(8,128)(2,1)S(1)}, bf16[208,256]{1,0:T(8,128)(2,1)S(1)}, bf16[208,256]{1,0:T(8,128)(...) custom-call(s32[32]{0:T(128)} %dest.1, s32[32]{0:T(128)} %length.1, ...), custom_call_target="tpu_custom_call" | custom-call | flops 419430400 | bytes 2277376 | tf_op jit(solution)/shard_map/first_chunks/pallas_call | solution.py:165
  5.9 1.9 %collective-permute-start.19 = (bf16[208,256]{1,0:T(8,128)(2,1)S(1)}, bf16[208,256]{1,0:T(8,128)(2,1)S(1)}, u32[]{:S(2)}, u32[]{:S(2)}) collective-permute-start(bf16[208,256]{1,0:T(8,128)(2,1)S(1)} %get-tuple-element.76), channel_id=1, source_target_pairs={{0,2},{2,4},{4,6},{6,7},{7,5},{5,3},{3,1},{1,0},{8,10},{10,12},{12... | collective-permute-start | bytes 319496 | tf_op jit(solution)/shard_map/ppermute | solution.py:221
  7.9 1.9 %collective-permute-start.12 = (bf16[208,256]{1,0:T(8,128)(2,1)S(1)}, bf16[208,256]{1,0:T(8,128)(2,1)S(1)}, u32[]{:S(2)}, u32[]{:S(2)}) collective-permute-start(bf16[208,256]{1,0:T(8,128)(2,1)S(1)} %get-tuple-element.66), channel_id=1, source_target_pairs={{0,2},{2,4},{4,6},{6,7},{7,5},{5,3},{3,1},{1,0},{8,10},{10,12},{12... | collective-permute-start | bytes 319496 | tf_op jit(solution)/shard_map/ppermute | solution.py:221
  9.8 6.1 %collective-permute-start.23 = (bf16[208,256]{1,0:T(8,128)(2,1)S(1)}, bf16[208,256]{1,0:T(8,128)(2,1)S(1)}, u32[]{:S(2)}, u32[]{:S(2)}) collective-permute-start(bf16[208,256]{1,0:T(8,128)(2,1)S(1)} %get-tuple-element.80), channel_id=1, source_target_pairs={{2,0},{4,2},{6,4},{7,6},{5,7},{3,5},{1,3},{0,1},{10,8},{12,10},{14... | collective-permute-start | bytes 319496 | tf_op jit(solution)/shard_map/ppermute | solution.py:221
  15.9 4.9 %collective-permute-start.16 = (bf16[208,256]{1,0:T(8,128)(2,1)S(1)}, bf16[208,256]{1,0:T(8,128)(2,1)S(1)}, u32[]{:S(2)}, u32[]{:S(2)}) collective-permute-start(bf16[208,256]{1,0:T(8,128)(2,1)S(1)} %get-tuple-element.72), channel_id=1, source_target_pairs={{2,0},{4,2},{6,4},{7,6},{5,7},{3,5},{1,3},{0,1},{10,8},{12,10},{14... | collective-permute-start | bytes 319496 | tf_op jit(solution)/shard_map/ppermute | solution.py:221
  20.9 4.0 %later_chunks.1 = (bf16[208,256]{1,0:T(8,128)(2,1)S(1)}, bf16[208,256]{1,0:T(8,128)(2,1)S(1)}, bf16[208,256]{1,0:T(8,128)(2,1)S(1)}, bf16[208,256]{1,0:T(8,128)(...) custom-call(bf16[400,1024]{1,0:T(8,128)(2,1)S(1)} %get-tuple-element, ...), custom_call_target="tpu_custom_call" | custom-call | flops 1258291200 | bytes 5193728 | tf_op jit(solution)/shard_map/later_chunks/pallas_call | solution.py:180
  25.0 1.9 %collective-permute-start.20 = (bf16[208,256]{1,0:T(8,128)(2,1)S(1)}, bf16[208,256]{1,0:T(8,128)(2,1)S(1)}, u32[]{:S(2)}, u32[]{:S(2)}) collective-permute-start(bf16[208,256]{1,0:T(8,128)(2,1)S(1)} %add_convert_fusion.9), channel_id=1, source_target_pairs={{0,2},{2,4},{4,6},{6,7},{7,5},{5,3},{3,1},{1,0},{8,10},{10,12},{12... | collective-permute-start | bytes 319496 | tf_op jit(solution)/shard_map/ppermute | solution.py:221
  26.9 1.9 %collective-permute-start.13 = (bf16[208,256]{1,0:T(8,128)(2,1)S(1)}, bf16[208,256]{1,0:T(8,128)(2,1)S(1)}, u32[]{:S(2)}, u32[]{:S(2)}) collective-permute-start(bf16[208,256]{1,0:T(8,128)(2,1)S(1)} %add_convert_fusion.14), channel_id=1, source_target_pairs={{0,2},{2,4},{4,6},{6,7},{7,5},{5,3},{3,1},{1,0},{8,10},{10,12},{12... | collective-permute-start | bytes 319496 | tf_op jit(solution)/shard_map/ppermute | solution.py:221
  28.9 5.5 %collective-permute-start.24 = (bf16[208,256]{1,0:T(8,128)(2,1)S(1)}, bf16[208,256]{1,0:T(8,128)(2,1)S(1)}, u32[]{:S(2)}, u32[]{:S(2)}) collective-permute-start(bf16[208,256]{1,0:T(8,128)(2,1)S(1)} %add_convert_fusion.6), channel_id=1, source_target_pairs={{2,0},{4,2},{6,4},{7,6},{5,7},{3,5},{1,3},{0,1},{10,8},{12,10},{14... | collective-permute-start | bytes 319496 | tf_op jit(solution)/shard_map/ppermute | solution.py:221
  34.4 4.3 %collective-permute-start.17 = (bf16[208,256]{1,0:T(8,128)(2,1)S(1)}, bf16[208,256]{1,0:T(8,128)(2,1)S(1)}, u32[]{:S(2)}, u32[]{:S(2)}) collective-permute-start(bf16[208,256]{1,0:T(8,128)(2,1)S(1)} %add_convert_fusion.11), channel_id=1, source_target_pairs={{2,0},{4,2},{6,4},{7,6},{5,7},{3,5},{1,3},{0,1},{10,8},{12,10},{14... | collective-permute-start | bytes 319496 | tf_op jit(solution)/shard_map/ppermute | solution.py:221
  38.8 1.9 %collective-permute-start.21 = (bf16[208,256]{1,0:T(8,128)(2,1)S(1)}, bf16[208,256]{1,0:T(8,128)(2,1)S(1)}, u32[]{:S(2)}, u32[]{:S(2)}) collective-permute-start(bf16[208,256]{1,0:T(8,128)(2,1)S(1)} %add_convert_fusion.8), channel_id=1, source_target_pairs={{0,2},{2,4},{4,6},{6,7},{7,5},{5,3},{3,1},{1,0},{8,10},{10,12},{12... | collective-permute-start | bytes 319496 | tf_op jit(solution)/shard_map/ppermute | solution.py:221
  40.7 1.9 %collective-permute-start.14 = (bf16[208,256]{1,0:T(8,128)(2,1)S(1)}, bf16[208,256]{1,0:T(8,128)(2,1)S(1)}, u32[]{:S(2)}, u32[]{:S(2)}) collective-permute-start(bf16[208,256]{1,0:T(8,128)(2,1)S(1)} %add_convert_fusion.13), channel_id=1, source_target_pairs={{0,2},{2,4},{4,6},{6,7},{7,5},{5,3},{3,1},{1,0},{8,10},{10,12},{12... | collective-permute-start | bytes 319496 | tf_op jit(solution)/shard_map/ppermute | solution.py:221
  42.7 5.5 %collective-permute-start.25 = (bf16[208,256]{1,0:T(8,128)(2,1)S(1)}, bf16[208,256]{1,0:T(8,128)(2,1)S(1)}, u32[]{:S(2)}, u32[]{:S(2)}) collective-permute-start(bf16[208,256]{1,0:T(8,128)(2,1)S(1)} %add_convert_fusion.5), channel_id=1, source_target_pairs={{2,0},{4,2},{6,4},{7,6},{5,7},{3,5},{1,3},{0,1},{10,8},{12,10},{14... | collective-permute-start | bytes 319496 | tf_op jit(solution)/shard_map/ppermute | solution.py:221
  48.2 4.3 %collective-permute-start.18 = (bf16[208,256]{1,0:T(8,128)(2,1)S(1)}, bf16[208,256]{1,0:T(8,128)(2,1)S(1)}, u32[]{:S(2)}, u32[]{:S(2)}) collective-permute-start(bf16[208,256]{1,0:T(8,128)(2,1)S(1)} %add_convert_fusion.10), channel_id=1, source_target_pairs={{2,0},{4,2},{6,4},{7,6},{5,7},{3,5},{1,3},{0,1},{10,8},{12,10},{14... | collective-permute-start | bytes 319496 | tf_op jit(solution)/shard_map/ppermute | solution.py:221
  52.5 1.9 %collective-permute-start.22 = (bf16[208,256]{1,0:T(8,128)(2,1)S(1)}, bf16[208,256]{1,0:T(8,128)(2,1)S(1)}, u32[]{:S(2)}, u32[]{:S(2)}) collective-permute-start(bf16[208,256]{1,0:T(8,128)(2,1)S(1)} %add_convert_fusion.7), channel_id=1, source_target_pairs={{0,2},{2,4},{4,6},{6,7},{7,5},{5,3},{3,1},{1,0},{8,10},{10,12},{12... | collective-permute-start | bytes 319496 | tf_op jit(solution)/shard_map/ppermute | solution.py:221
  54.5 1.9 %collective-permute-start.15 = (bf16[208,256]{1,0:T(8,128)(2,1)S(1)}, bf16[208,256]{1,0:T(8,128)(2,1)S(1)}, u32[]{:S(2)}, u32[]{:S(2)}) collective-permute-start(bf16[208,256]{1,0:T(8,128)(2,1)S(1)} %add_convert_fusion.12), channel_id=1, source_target_pairs={{0,2},{2,4},{4,6},{6,7},{7,5},{5,3},{3,1},{1,0},{8,10},{10,12},{12... | collective-permute-start | bytes 319496 | tf_op jit(solution)/shard_map/ppermute | solution.py:221
  56.5 4.5 %collective-permute-done.22.refs_3_ = bf16[208,256]{1,0:T(8,128)(2,1)S(1)} collective-permute-done((bf16[208,256]{1,0:T(8,128)(2,1)S(1)}, bf16[208,256]{1,0:T(8,128)(2,1)S(1)}, u32[]{:S(2)}, u32[]{:S(2)}) %collective-permute-start.22) | collective-permute-done | bytes 106528 | tf_op jit(solution)/shard_map/ppermute | solution.py:221
  61.0 1.1 %collective-permute-done.15.refs_0_ = bf16[208,256]{1,0:T(8,128)(2,1)S(1)} collective-permute-done((bf16[208,256]{1,0:T(8,128)(2,1)S(1)}, bf16[208,256]{1,0:T(8,128)(2,1)S(1)}, u32[]{:S(2)}, u32[]{:S(2)}) %collective-permute-start.15) | collective-permute-done | bytes 106528 | tf_op jit(solution)/shard_map/ppermute | solution.py:221
  62.3 12.6 %collective-permute-start.26 = (bf16[256,256]{1,0:T(8,128)(2,1)S(1)}, bf16[256,256]{1,0:T(8,128)(2,1)S(1)}, u32[]{:S(2)}, u32[]{:S(2)}) collective-permute-start(bf16[256,256]{1,0:T(8,128)(2,1)S(1)} %get-tuple-element.84), channel_id=1, source_target_pairs={{0,16},{8,24},{16,0},{24,8},{32,48},{40,56},{48,32},{56,40},{64,80... | collective-permute-start | bytes 393224 | tf_op jit(solution)/shard_map/ppermute | solution.py:488
  76.7 1.4 %collective-permute-done.26.received = bf16[256,256]{1,0:T(8,128)(2,1)S(1)} collective-permute-done((bf16[256,256]{1,0:T(8,128)(2,1)S(1)}, bf16[256,256]{1,0:T(8,128)(2,1)S(1)}, u32[]{:S(2)}, u32[]{:S(2)}) %collective-permute-start.26) | collective-permute-done | bytes 131104 | tf_op jit(solution)/shard_map/ppermute | solution.py:488
  78.0 1.1 place_crossing.1
  79.8 17.8 %all-to-all-start = ((bf16[32,32,256]{2,1,0:T(8,128)(2,1)}), bf16[32,32,256]{2,1,0:T(8,128)(2,1)S(1)}, u32[]{:S(2)}, u32[]{:S(2)}) async-start(bf16[32,32,256]{2,1,0:T(8,128)(2,1)} %get-tuple-element.108), calls=%async_computation | async-start | bytes 1048576 | tf_op jit(solution)/shard_map/all_to_all | solution.py:514
  97.8 11.3 %all-to-all-done.arrived = bf16[32,32,256]{2,1,0:T(8,128)(2,1)S(1)} async-done(((bf16[32,32,256]{2,1,0:T(8,128)(2,1)}), bf16[32,32,256]{2,1,0:T(8,128)(2,1)S(1)}, u32[]{:S(2)}, u32[]{:S(2)}) %all-to-all-start) | async-done | bytes 524320 | tf_op jit(solution)/shard_map/all_to_all | solution.py:514
  109.2 2.5 %rebuild_and_attend.1 = (bf16[256,512]{1,0:T(8,128)(2,1)}, bf16[2,16,1024]{2,1,0:T(8,128)(2,1)}) custom-call(bf16[32,32,256]{2,1,0:T(8,128)(2,1)S(1)} %all-to-all-done.arrived, bf16[256,256]{1,0:T(8,128)(2,1)S(1)} %copy-done, s32[1,256]{1,0:T(1,128)S(1)} %reshape.126.resident_valid, bf16[2,16,1024]{2,1,0:T(8,128)(2,1)S(1)} %copy-done.2, ...), custom_call_target="tpu_custom_call" | custom-call | tf_op jit(solution)/shard_map/rebuild_and_attend/pallas_call | solution.py:396
  (52 shorter events, 2.7 us)
Async XLA Ops:
  5.9 19.0 %collective-permute-start.19 = (bf16[208,256]{1,0:T(8,128)(2,1)S(1)}, bf16[208,256]{1,0:T(8,128)(2,1)S(1)}, u32[]{:S(2)}, u32[]{:S(2)}) collective-permute-start(bf16[208,256]{1,0:T(8,128)(2,1)S(1)} %get-tuple-element.76), channel_id=1, source_target_pairs={{0,2},{2,4},{4,6},{6,7},{7,5},{5,3},{3,1},{1,0},{8,10},{10,12},{12... | collective-permute-start | bytes 319496 | tf_op jit(solution)/shard_map/ppermute | solution.py:221
  7.9 19.0 %collective-permute-start.12 = (bf16[208,256]{1,0:T(8,128)(2,1)S(1)}, bf16[208,256]{1,0:T(8,128)(2,1)S(1)}, u32[]{:S(2)}, u32[]{:S(2)}) collective-permute-start(bf16[208,256]{1,0:T(8,128)(2,1)S(1)} %get-tuple-element.66), channel_id=1, source_target_pairs={{0,2},{2,4},{4,6},{6,7},{7,5},{5,3},{3,1},{1,0},{8,10},{10,12},{12... | collective-permute-start | bytes 319496 | tf_op jit(solution)/shard_map/ppermute | solution.py:221
  9.8 19.1 %collective-permute-start.23 = (bf16[208,256]{1,0:T(8,128)(2,1)S(1)}, bf16[208,256]{1,0:T(8,128)(2,1)S(1)}, u32[]{:S(2)}, u32[]{:S(2)}) collective-permute-start(bf16[208,256]{1,0:T(8,128)(2,1)S(1)} %get-tuple-element.80), channel_id=1, source_target_pairs={{2,0},{4,2},{6,4},{7,6},{5,7},{3,5},{1,3},{0,1},{10,8},{12,10},{14... | collective-permute-start | bytes 319496 | tf_op jit(solution)/shard_map/ppermute | solution.py:221
  15.9 18.5 %collective-permute-start.16 = (bf16[208,256]{1,0:T(8,128)(2,1)S(1)}, bf16[208,256]{1,0:T(8,128)(2,1)S(1)}, u32[]{:S(2)}, u32[]{:S(2)}) collective-permute-start(bf16[208,256]{1,0:T(8,128)(2,1)S(1)} %get-tuple-element.72), channel_id=1, source_target_pairs={{2,0},{4,2},{6,4},{7,6},{5,7},{3,5},{1,3},{0,1},{10,8},{12,10},{14... | collective-permute-start | bytes 319496 | tf_op jit(solution)/shard_map/ppermute | solution.py:221
  20.8 54.0 %copy-start.6 = (s32[32]{0:T(128)S(1)}, s32[32]{0:T(128)}, u32[]{:S(2)}) copy-start(s32[32]{0:T(128)} %length.1) | copy-start | bytes 388
  20.8 55.3 %copy-start.4 = (bf16[512,1024]{1,0:T(8,128)(2,1)S(1)}, bf16[512,1024]{1,0:T(8,128)(2,1)}, u32[]{:S(2)}) copy-start(bf16[512,1024]{1,0:T(8,128)(2,1)} %hidden_hbm.1) | copy-start | bytes 3145732
  20.8 55.3 %copy-start.5 = (f32[1024]{0:T(1024)S(1)}, f32[1024]{0:T(1024)}, u32[]{:S(2)}) copy-start(f32[1024]{0:T(1024)} %param.17) | copy-start | bytes 12292
  20.9 55.3 %copy-start.7 = (s32[32]{0:T(128)S(1)}, s32[32]{0:T(128)}, u32[]{:S(2)}) copy-start(s32[32]{0:T(128)} %dest.1) | copy-start | bytes 388
  25.0 13.8 %collective-permute-start.20 = (bf16[208,256]{1,0:T(8,128)(2,1)S(1)}, bf16[208,256]{1,0:T(8,128)(2,1)S(1)}, u32[]{:S(2)}, u32[]{:S(2)}) collective-permute-start(bf16[208,256]{1,0:T(8,128)(2,1)S(1)} %add_convert_fusion.9), channel_id=1, source_target_pairs={{0,2},{2,4},{4,6},{6,7},{7,5},{5,3},{3,1},{1,0},{8,10},{10,12},{12... | collective-permute-start | bytes 319496 | tf_op jit(solution)/shard_map/ppermute | solution.py:221
  26.9 13.8 %collective-permute-start.13 = (bf16[208,256]{1,0:T(8,128)(2,1)S(1)}, bf16[208,256]{1,0:T(8,128)(2,1)S(1)}, u32[]{:S(2)}, u32[]{:S(2)}) collective-permute-start(bf16[208,256]{1,0:T(8,128)(2,1)S(1)} %add_convert_fusion.14), channel_id=1, source_target_pairs={{0,2},{2,4},{4,6},{6,7},{7,5},{5,3},{3,1},{1,0},{8,10},{10,12},{12... | collective-permute-start | bytes 319496 | tf_op jit(solution)/shard_map/ppermute | solution.py:221
  28.9 13.8 %collective-permute-start.24 = (bf16[208,256]{1,0:T(8,128)(2,1)S(1)}, bf16[208,256]{1,0:T(8,128)(2,1)S(1)}, u32[]{:S(2)}, u32[]{:S(2)}) collective-permute-start(bf16[208,256]{1,0:T(8,128)(2,1)S(1)} %add_convert_fusion.6), channel_id=1, source_target_pairs={{2,0},{4,2},{6,4},{7,6},{5,7},{3,5},{1,3},{0,1},{10,8},{12,10},{14... | collective-permute-start | bytes 319496 | tf_op jit(solution)/shard_map/ppermute | solution.py:221
  34.4 13.8 %collective-permute-start.17 = (bf16[208,256]{1,0:T(8,128)(2,1)S(1)}, bf16[208,256]{1,0:T(8,128)(2,1)S(1)}, u32[]{:S(2)}, u32[]{:S(2)}) collective-permute-start(bf16[208,256]{1,0:T(8,128)(2,1)S(1)} %add_convert_fusion.11), channel_id=1, source_target_pairs={{2,0},{4,2},{6,4},{7,6},{5,7},{3,5},{1,3},{0,1},{10,8},{12,10},{14... | collective-permute-start | bytes 319496 | tf_op jit(solution)/shard_map/ppermute | solution.py:221
  38.8 13.8 %collective-permute-start.21 = (bf16[208,256]{1,0:T(8,128)(2,1)S(1)}, bf16[208,256]{1,0:T(8,128)(2,1)S(1)}, u32[]{:S(2)}, u32[]{:S(2)}) collective-permute-start(bf16[208,256]{1,0:T(8,128)(2,1)S(1)} %add_convert_fusion.8), channel_id=1, source_target_pairs={{0,2},{2,4},{4,6},{6,7},{7,5},{5,3},{3,1},{1,0},{8,10},{10,12},{12... | collective-permute-start | bytes 319496 | tf_op jit(solution)/shard_map/ppermute | solution.py:221
  40.7 13.8 %collective-permute-start.14 = (bf16[208,256]{1,0:T(8,128)(2,1)S(1)}, bf16[208,256]{1,0:T(8,128)(2,1)S(1)}, u32[]{:S(2)}, u32[]{:S(2)}) collective-permute-start(bf16[208,256]{1,0:T(8,128)(2,1)S(1)} %add_convert_fusion.13), channel_id=1, source_target_pairs={{0,2},{2,4},{4,6},{6,7},{7,5},{5,3},{3,1},{1,0},{8,10},{10,12},{12... | collective-permute-start | bytes 319496 | tf_op jit(solution)/shard_map/ppermute | solution.py:221
  42.7 13.8 %collective-permute-start.25 = (bf16[208,256]{1,0:T(8,128)(2,1)S(1)}, bf16[208,256]{1,0:T(8,128)(2,1)S(1)}, u32[]{:S(2)}, u32[]{:S(2)}) collective-permute-start(bf16[208,256]{1,0:T(8,128)(2,1)S(1)} %add_convert_fusion.5), channel_id=1, source_target_pairs={{2,0},{4,2},{6,4},{7,6},{5,7},{3,5},{1,3},{0,1},{10,8},{12,10},{14... | collective-permute-start | bytes 319496 | tf_op jit(solution)/shard_map/ppermute | solution.py:221
  48.2 8.2 %collective-permute-start.18 = (bf16[208,256]{1,0:T(8,128)(2,1)S(1)}, bf16[208,256]{1,0:T(8,128)(2,1)S(1)}, u32[]{:S(2)}, u32[]{:S(2)}) collective-permute-start(bf16[208,256]{1,0:T(8,128)(2,1)S(1)} %add_convert_fusion.10), channel_id=1, source_target_pairs={{2,0},{4,2},{6,4},{7,6},{5,7},{3,5},{1,3},{0,1},{10,8},{12,10},{14... | collective-permute-start | bytes 319496 | tf_op jit(solution)/shard_map/ppermute | solution.py:221
  52.5 8.5 %collective-permute-start.22 = (bf16[208,256]{1,0:T(8,128)(2,1)S(1)}, bf16[208,256]{1,0:T(8,128)(2,1)S(1)}, u32[]{:S(2)}, u32[]{:S(2)}) collective-permute-start(bf16[208,256]{1,0:T(8,128)(2,1)S(1)} %add_convert_fusion.7), channel_id=1, source_target_pairs={{0,2},{2,4},{4,6},{6,7},{7,5},{5,3},{3,1},{1,0},{8,10},{10,12},{12... | collective-permute-start | bytes 319496 | tf_op jit(solution)/shard_map/ppermute | solution.py:221
  54.5 7.6 %collective-permute-start.15 = (bf16[208,256]{1,0:T(8,128)(2,1)S(1)}, bf16[208,256]{1,0:T(8,128)(2,1)S(1)}, u32[]{:S(2)}, u32[]{:S(2)}) collective-permute-start(bf16[208,256]{1,0:T(8,128)(2,1)S(1)} %add_convert_fusion.12), channel_id=1, source_target_pairs={{0,2},{2,4},{4,6},{6,7},{7,5},{5,3},{3,1},{1,0},{8,10},{10,12},{12... | collective-permute-start | bytes 319496 | tf_op jit(solution)/shard_map/ppermute | solution.py:221
  62.3 15.7 %collective-permute-start.26 = (bf16[256,256]{1,0:T(8,128)(2,1)S(1)}, bf16[256,256]{1,0:T(8,128)(2,1)S(1)}, u32[]{:S(2)}, u32[]{:S(2)}) collective-permute-start(bf16[256,256]{1,0:T(8,128)(2,1)S(1)} %get-tuple-element.84), channel_id=1, source_target_pairs={{0,16},{8,24},{16,0},{24,8},{32,48},{40,56},{48,32},{56,40},{64,80... | collective-permute-start | bytes 393224 | tf_op jit(solution)/shard_map/ppermute | solution.py:488
  76.2 21.3 %copy-start.8 = (s32[16]{0:T(128)S(1)}, s32[16]{0:T(128)}, u32[]{:S(2)}) copy-start(s32[16]{0:T(128)} %param.24) | copy-start | bytes 196
  76.2 21.4 %copy-start.9 = (s32[16]{0:T(128)S(1)}, s32[16]{0:T(128)}, u32[]{:S(2)}) copy-start(s32[16]{0:T(128)} %param.23) | copy-start | bytes 196
  76.3 32.9 %copy-start = (bf16[256,256]{1,0:T(8,128)(2,1)S(1)}, bf16[256,256]{1,0:T(8,128)(2,1)}, u32[]{:S(2)}) copy-start(bf16[256,256]{1,0:T(8,128)(2,1)} %resident.1) | copy-start | bytes 393220
  76.3 32.9 %copy-start.2 = (bf16[2,16,1024]{2,1,0:T(8,128)(2,1)S(1)}, bf16[2,16,1024]{2,1,0:T(8,128)(2,1)}, u32[]{:S(2)}) copy-start(bf16[2,16,1024]{2,1,0:T(8,128)(2,1)} %queries.1) | copy-start | bytes 196612
  79.8 29.4 %all-to-all-start = ((bf16[32,32,256]{2,1,0:T(8,128)(2,1)}), bf16[32,32,256]{2,1,0:T(8,128)(2,1)S(1)}, u32[]{:S(2)}, u32[]{:S(2)}) async-start(bf16[32,32,256]{2,1,0:T(8,128)(2,1)} %get-tuple-element.108), calls=%async_computation | async-start | bytes 1048576 | tf_op jit(solution)/shard_map/all_to_all | solution.py:514
  (2 other events, 20.2 us)

commit v6 on v4

--- a/solution.py
+++ b/solution.py
@@ -57,39 +57,30 @@
     copies = [weight_copy(weight, blocks, sems, offset, i) for i, offset in enumerate(offsets)]
     for copy in copies:
         copy.start()
-    requests = dest.shape[0]
+    requests = dest.shape[1]
     context = hidden.shape[0] // requests
     rows, capacity = scaled.shape[0], scaled.shape[0] - fresh.shape[0]
     half = half_of(lax.axis_index("inst"))
 
-    def crosses(j):
-        return half_of(dest[j]) != half
-
-    def count(j, crossing):
-        return crossing + jnp.where(crosses(j), length[j], 0)
-
-    crossing = lax.fori_loop(0, requests, count, jnp.int32(0), unroll=8)
-    lane = iota((1, hidden.shape[0]), 1)
-
-    def place(j, carry):
-        next_cross, next_stay, target, code = carry
-        cross = crosses(j)
-        start = jnp.where(cross, next_cross, next_stay)
-        place_here = (lane // context == j) & (lane % context < length[j])
-        target = jnp.where(place_here, start + lane % context, target)
-        inside = (lane >= start) & (lane < start + length[j])
-        code = jnp.where(inside, plane_of(dest[j]) * context + lane - start, code)
-        return (
-            next_cross + jnp.where(cross, length[j], 0),
-            next_stay + jnp.where(cross, 0, length[j]),
-            target,
-            code,
-        )
-
-    nowhere = jnp.full(lane.shape, -1, jnp.int32)
-    _, _, target, code = lax.fori_loop(
-        0, requests, place, (jnp.int32(0), crossing, nowhere, nowhere), unroll=8
-    )
+    def upright(line):
+        diagonal = iota((requests, requests), 0) == iota((requests, requests), 1)
+        return jnp.sum(jnp.where(diagonal, line, 0), axis=1, keepdims=True)
+
+    lengths, dests = length[...], dest[...]
+    cross = jnp.where(half_of(dests) != half, 1, 0)
+    crossing = jnp.sum(cross * lengths, axis=1, keepdims=True)
+    cross_up, lengths_up, dests_up = upright(cross), upright(lengths), upright(dests)
+    earlier = iota((requests, requests), 1) < iota((requests, requests), 0)
+    sooner = (cross > cross_up) | ((cross == cross_up) & earlier)
+    start = jnp.sum(jnp.where(sooner, lengths, 0), axis=1, keepdims=True)
+    shape = (requests, hidden.shape[0])
+    lane = iota(shape, 1)
+    at = lane % context
+    here = (lane // context == iota(shape, 0)) & (at < lengths_up)
+    target = jnp.sum(jnp.where(here, start + at + 1, 0), axis=0, keepdims=True) - 1
+    inside = (lane >= start) & (lane < start + lengths_up)
+    code = jnp.where(inside, plane_of(dests_up) * context + lane - start + 1, 0)
+    code = jnp.sum(code, axis=0, keepdims=True) - 1
     codes[...] = jnp.where(iota(codes.shape, 0) == 0, code, crossing)
     select = jnp.where(target == iota((capacity, hidden.shape[0]), 0), 1.0, 0.0).astype(BF)
     wide = jnp.concatenate([dot(select, hidden[...]), fresh[...].astype(F32)], axis=0)
@@ -130,7 +121,6 @@
     chunk = jax.ShapeDtypeStruct((rows + EXTRA, lanes), BF)
     offsets = ring_offsets(lax.axis_size("tensor"))
     vmem = pl.BlockSpec(memory_space=pltpu.VMEM)
-    smem = pl.BlockSpec(memory_space=pltpu.SMEM)
     hbm = pl.BlockSpec(memory_space=pltpu.HBM)
 
     def options(count, name):
@@ -150,7 +140,7 @@
 
     out_a, out_b, scaled, extra, codes = pl.pallas_call(
         functools.partial(first_chunks, offsets[:2]),
-        in_specs=[smem, smem, vmem, vmem, vmem, hbm],
+        in_specs=[vmem, vmem, vmem, vmem, vmem, hbm],
         out_shape=[
             chunk,
             chunk,
@@ -159,7 +149,7 @@
             jax.ShapeDtypeStruct((8, hidden.shape[0]), jnp.int32),
         ],
         **options(2, "first_chunks"),
-    )(dest, length, hidden, fresh, gain, weight)
+    )(dest[None, :], length[None, :], hidden, fresh, gain, weight)
     rest = len(offsets) - 2
     later = pl.pallas_call(
         functools.partial(later_chunks, offsets[2:]),
@@ -260,44 +250,45 @@
     out[...] = routed(jnp.where(route, 1.0, 0.0), rows).reshape(out.shape)
 
 
-def place_crossing(received, codes, near, out, most):
-    slots, context, lanes = near.shape
+def place_crossing(received, codes, out, most):
+    slots, context, lanes = out.shape
     sent = received.shape[0] - EXTRA
     notes = received[sent:, :].astype(F32).astype(jnp.int32)
     code = notes[0:1, :sent] * context + notes[1:2, :sent]
     route = iota((slots * context, sent), 0) == code
-    out[:, :context, :] = near[...]
-    out[:, context:, :] = routed(jnp.where(route, 1.0, 0.0), received[:sent, :]).reshape(near.shape)
-    theirs = notes[2:3, :TILE] * context + notes[3:4, :TILE]
-    most[...] = jnp.broadcast_to(jnp.maximum(theirs, codes[1:2, :1]), most.shape)
-
-
-def place(kernel, out_shape, *operands):
+    out[...] = routed(jnp.where(route, 1.0, 0.0), received[:sent, :]).reshape(out.shape)
+    counts = jnp.maximum(notes[2:3, :sent] * context + notes[3:4, :sent], codes[1:2, :sent])
+    most[0] = jnp.max(counts)
+
+
+def place(kernel, out_shape, out_specs, weighs, *operands):
     return pl.pallas_call(
         kernel,
         out_shape=out_shape,
+        out_specs=out_specs,
         compiler_params=pltpu.CompilerParams(vmem_limit_bytes=VMEM_BYTES),
+        cost_estimate=pl.CostEstimate(flops=weighs, bytes_accessed=1 << 20, transcendentals=0),
         name=kernel.__name__,
     )(*operands)
 
 
 def rebuild_and_attend(
-    arrived, resident, resident_valid, queries, kept, wanted, rebuilt, attended
+    near, far, resident, resident_valid, queries, kept, wanted, rebuilt, attended
 ):
-    plane, context, lanes = arrived.shape
-    slots, context = 2 * plane, context // 2
+    plane, context, lanes = near.shape
+    slots = 2 * plane
     steps, batch, width = queries.shape
     rows = slots * context
     fresh = kept[kept.shape[0] - steps * batch :, :]
     columns = rebuilt.shape[1]
     held = resident.shape[1]
     heads = width // HD
-    blocks = arrived[...].reshape(rows, lanes)
+    blocks = jnp.concatenate([near[...], far[...]], axis=0).reshape(rows, lanes)
     half = half_of(lax.axis_index("inst"))
 
     def instance_of(slot):
-        place = slot >> 1
-        there = jnp.where(slot % 2 == 0, half, 1 - half)
+        place = slot % plane
+        there = jnp.where(slot < plane, half, 1 - half)
         return (place >> 1) * 4 + there * 2 + (place & 1)
 
     valid = blocks[:, :TILE].astype(F32) < ABSENT / 2
@@ -365,16 +356,16 @@
             attended[s, :, h * HD : (h + 1) * HD] = out[start : start + batch]
 
 
-def rebuild(arrived, resident, resident_valid, queries, kept, wanted, columns):
+def rebuild(near, far, resident, resident_valid, queries, kept, wanted, columns):
     return pl.pallas_call(
         rebuild_and_attend,
         out_shape=[
-            jax.ShapeDtypeStruct((arrived.shape[2], columns), BF),
+            jax.ShapeDtypeStruct((near.shape[2], columns), BF),
             jax.ShapeDtypeStruct(queries.shape, BF),
         ],
         compiler_params=pltpu.CompilerParams(vmem_limit_bytes=VMEM_BYTES),
         name="rebuild_and_attend",
-    )(arrived, resident, resident_valid, queries, kept, wanted)
+    )(near, far, resident, resident_valid, queries, kept, wanted)
 
 
 def remaining_rows(hidden, gain, weight, codes, target_of, capacity, lanes):
@@ -460,11 +451,23 @@
     planes = [[i for i in range(instances) if half_of(i) == half] for half in range(2)]
 
     received = lax.ppermute(crossing_rows, "inst", halves)
-    near_type = jax.ShapeDtypeStruct((plane, context, owned), BF)
-    near = place(place_staying, near_type, codes, kept, rest)
-    both_type = jax.ShapeDtypeStruct((plane, 2 * context, owned), BF)
-    most_type = jax.ShapeDtypeStruct((8, TILE), jnp.int32)
-    outgoing, most = place(place_crossing, (both_type, most_type), received, codes, near)
+    blocks_type = jax.ShapeDtypeStruct((plane, context, owned), BF)
+    vmem = pl.BlockSpec(memory_space=pltpu.VMEM)
+    staying = place(place_staying, blocks_type, vmem, 1 << 33, codes, kept, rest)
+    most_type = jax.ShapeDtypeStruct((1,), jnp.int32)
+    crossing, most = place(
+        place_crossing,
+        (blocks_type, most_type),
+        (vmem, pl.BlockSpec(memory_space=pltpu.SMEM)),
+        1 << 36,
+        received,
+        codes,
+    )
+
+    def over_plane(rows):
+        return lax.all_to_all(
+            rows, "inst", split_axis=0, concat_axis=0, tiled=True, axis_index_groups=planes
+        )
 
     def all_crossing():
         rows = jnp.concatenate([kept[:capacity], rest], axis=0)
@@ -473,15 +476,12 @@
         lane = jnp.arange(leaving, dtype=jnp.int32)[None, :]
         slot = jnp.arange(plane * context, dtype=jnp.int32)[:, None]
         route = (slot == notes[0:1]) & (lane < notes[1:2])
-        far = routed(route.astype(F32), rows).reshape(near.shape)
-        return jnp.concatenate([near, far], axis=1)
-
-    outgoing = lax.cond(most[0, 0] > sent, all_crossing, lambda: outgoing)
-    arrived = lax.all_to_all(
-        outgoing, "inst", split_axis=0, concat_axis=0, tiled=True, axis_index_groups=planes
-    )
+        return routed(route.astype(F32), rows).reshape(crossing.shape)
+
+    near = over_plane(staying)
+    far = over_plane(lax.cond(most[0] > sent, all_crossing, lambda: crossing))
     return tuple(
-        rebuild(arrived, resident_cache, resident_valid, queries, kept, wanted, leaving)
+        rebuild(near, far, resident_cache, resident_valid, queries, kept, wanted, leaving)
     )
 
 

time: 104 us -> 102 us (0.981)
  the two profiles are of different devices: /device:TPU:33 before, /device:TPU:129 now
where the time goes in v6:
time: 102 us; the launch traced here: 101 us
  starting transfers between devices  43.9 us (43%)
  waiting for transfers between devices  39.9 us (39%)
  Pallas kernels  13 us (13%)
  between operations  2.25 us (2%)
  local copies, waits for them, and re-layouts  1.08 us (1%)
    ppermute x7, starting transfers between devices, ring_sums(): sums[way] = lax.ppermute(chunk, 'tensor', forward if way else backward)  24.2 us
    ppermute x7, waiting for transfers between devices, ring_sums(): sums[way] = lax.ppermute(chunk, 'tensor', forward if way else backward)  23.9 us
    all_to_all x2, starting transfers between devices, over_plane(): lax.all_to_all(rows, 'inst', split_axis=0, concat_axis=0, tiled=True, axi...  17.8 us
    all_to_all x2, waiting for transfers between devices, over_plane(): lax.all_to_all(rows, 'inst', split_axis=0, concat_axis=0, tiled=True, axi...  12.3 us
    pallas_call x1, Pallas kernels, project_chunks(): pl.pallas_call(functools.partial(first_chunks, offsets[:2]), in_specs=[vm...  4.39 us
    pallas_call x1, Pallas kernels, project_chunks(): pl.pallas_call(functools.partial(later_chunks, offsets[2:]), in_specs=[vm...  3.99 us
    ppermute x1, waiting for transfers between devices, shards(): received = lax.ppermute(crossing_rows, 'inst', halves)  3.72 us
    pallas_call x1, Pallas kernels, rebuild(): pl.pallas_call(rebuild_and_attend, out_shape=[jax.ShapeDtypeStruct((near....  2.49 us
  transfers between devices with their start and end apart: 10, of which 7 were waited for; matrix products, arithmetic and copies ran while one was open for 1% of the time, Pallas kernels for 6%

profile of v6, /device:TPU:129, one launch (start us, length us, event | category | flops | bytes accessed | tf_op | source)
XLA Modules:
  0.0 101.3 jit_solution(11771766461837589148)
XLA Ops:
  0.6 0.8 copy-done.1
  1.5 4.4 %first_chunks.1 = (bf16[416,256]{1,0:T(8,128)(2,1)S(1)}, bf16[416,256]{1,0:T(8,128)(2,1)S(1)}, bf16[400,1024]{1,0:T(8,128)(2,1)S(1)}, bf16[16,256]{1,0:T(8,128)(2,1)S(1)}, s32[8,512]{1,0:T(8,128)S(1)}) custom-call(s32[1,32]{1,0:T(1,128)} %bitcast.26, s32[1,32]{1,0:T(1,128)} %bitcast.25, bf16[512,1024]{1,0:T(8,128)(2,1)} %hidden.1, ...), custom_call_target="tpu_custom_call" | custom-call | flops 419430400 | bytes 2277376 | tf_op jit(solution)/shard_map/first_chunks/pallas_call | solution.py:141
  5.9 5.0 %collective-permute-start.12 = (bf16[416,256]{1,0:T(8,128)(2,1)S(1)}, bf16[416,256]{1,0:T(8,128)(2,1)S(1)}, u32[]{:S(2)}, u32[]{:S(2)}) collective-permute-start(bf16[416,256]{1,0:T(8,128)(2,1)S(1)} %get-tuple-element.55), channel_id=1, source_target_pairs={{0,2},{2,4},{4,6},{6,7},{7,5},{5,3},{3,1},{1,0},{8,10},{10,12},{12... | collective-permute-start | bytes 638984 | tf_op jit(solution)/shard_map/ppermute | solution.py:193
  11.0 2.5 %collective-permute-start.16 = (bf16[416,256]{1,0:T(8,128)(2,1)S(1)}, bf16[416,256]{1,0:T(8,128)(2,1)S(1)}, u32[]{:S(2)}, u32[]{:S(2)}) collective-permute-start(bf16[416,256]{1,0:T(8,128)(2,1)S(1)} %get-tuple-element.61), channel_id=1, source_target_pairs={{2,0},{4,2},{6,4},{7,6},{5,7},{3,5},{1,3},{0,1},{10,8},{12,10},{14... | collective-permute-start | bytes 638984 | tf_op jit(solution)/shard_map/ppermute | solution.py:193
  13.5 4.0 %later_chunks.1 = (bf16[416,256]{1,0:T(8,128)(2,1)S(1)}, bf16[416,256]{1,0:T(8,128)(2,1)S(1)}, bf16[416,256]{1,0:T(8,128)(2,1)S(1)}, bf16[416,256]{1,0:T(8,128)(...) custom-call(bf16[400,1024]{1,0:T(8,128)(2,1)S(1)} %get-tuple-element.56.scaled, ...), custom_call_target="tpu_custom_call" | custom-call | flops 1258291200 | bytes 5193728 | tf_op jit(solution)/shard_map/later_chunks/pallas_call | solution.py:154
  17.5 4.1 %collective-permute-done.12 = bf16[416,256]{1,0:T(8,128)(2,1)S(1)} collective-permute-done((bf16[416,256]{1,0:T(8,128)(2,1)S(1)}, bf16[416,256]{1,0:T(8,128)(2,1)S(1)}, u32[]{:S(2)}, u32[]{:S(2)}) %collective-permute-start.12) | collective-permute-done | bytes 213024 | tf_op jit(solution)/shard_map/ppermute | solution.py:193
  21.6 1.9 %collective-permute-start.13 = (bf16[416,256]{1,0:T(8,128)(2,1)S(1)}, bf16[416,256]{1,0:T(8,128)(2,1)S(1)}, u32[]{:S(2)}, u32[]{:S(2)}) collective-permute-start(bf16[416,256]{1,0:T(8,128)(2,1)S(1)} %add_convert_fusion.9), channel_id=1, source_target_pairs={{0,2},{2,4},{4,6},{6,7},{7,5},{5,3},{3,1},{1,0},{8,10},{10,12},{12... | collective-permute-start | bytes 638984 | tf_op jit(solution)/shard_map/ppermute | solution.py:193
  23.7 5.5 %collective-permute-start.17 = (bf16[416,256]{1,0:T(8,128)(2,1)S(1)}, bf16[416,256]{1,0:T(8,128)(2,1)S(1)}, u32[]{:S(2)}, u32[]{:S(2)}) collective-permute-start(bf16[416,256]{1,0:T(8,128)(2,1)S(1)} %add_convert_fusion.6), channel_id=1, source_target_pairs={{2,0},{4,2},{6,4},{7,6},{5,7},{3,5},{1,3},{0,1},{10,8},{12,10},{14... | collective-permute-start | bytes 638984 | tf_op jit(solution)/shard_map/ppermute | solution.py:193
  29.1 7.0 %collective-permute-done.13 = bf16[416,256]{1,0:T(8,128)(2,1)S(1)} collective-permute-done((bf16[416,256]{1,0:T(8,128)(2,1)S(1)}, bf16[416,256]{1,0:T(8,128)(2,1)S(1)}, u32[]{:S(2)}, u32[]{:S(2)}) %collective-permute-start.13) | collective-permute-done | bytes 213024 | tf_op jit(solution)/shard_map/ppermute | solution.py:193
  36.1 1.9 %collective-permute-start.14 = (bf16[416,256]{1,0:T(8,128)(2,1)S(1)}, bf16[416,256]{1,0:T(8,128)(2,1)S(1)}, u32[]{:S(2)}, u32[]{:S(2)}) collective-permute-start(bf16[416,256]{1,0:T(8,128)(2,1)S(1)} %add_convert_fusion.8), channel_id=1, source_target_pairs={{0,2},{2,4},{4,6},{6,7},{7,5},{5,3},{3,1},{1,0},{8,10},{10,12},{12... | collective-permute-start | bytes 638984 | tf_op jit(solution)/shard_map/ppermute | solution.py:193
  38.1 5.5 %collective-permute-start.18 = (bf16[416,256]{1,0:T(8,128)(2,1)S(1)}, bf16[416,256]{1,0:T(8,128)(2,1)S(1)}, u32[]{:S(2)}, u32[]{:S(2)}) collective-permute-start(bf16[416,256]{1,0:T(8,128)(2,1)S(1)} %add_convert_fusion.5), channel_id=1, source_target_pairs={{2,0},{4,2},{6,4},{7,6},{5,7},{3,5},{1,3},{0,1},{10,8},{12,10},{14... | collective-permute-start | bytes 638984 | tf_op jit(solution)/shard_map/ppermute | solution.py:193
  43.6 7.0 %collective-permute-done.14 = bf16[416,256]{1,0:T(8,128)(2,1)S(1)} collective-permute-done((bf16[416,256]{1,0:T(8,128)(2,1)S(1)}, bf16[416,256]{1,0:T(8,128)(2,1)S(1)}, u32[]{:S(2)}, u32[]{:S(2)}) %collective-permute-start.14) | collective-permute-done | bytes 213024 | tf_op jit(solution)/shard_map/ppermute | solution.py:193
  50.7 1.9 %collective-permute-start.15 = (bf16[416,256]{1,0:T(8,128)(2,1)S(1)}, bf16[416,256]{1,0:T(8,128)(2,1)S(1)}, u32[]{:S(2)}, u32[]{:S(2)}) collective-permute-start(bf16[416,256]{1,0:T(8,128)(2,1)S(1)} %add_convert_fusion.7), channel_id=1, source_target_pairs={{0,2},{2,4},{4,6},{6,7},{7,5},{5,3},{3,1},{1,0},{8,10},{10,12},{12... | collective-permute-start | bytes 638984 | tf_op jit(solution)/shard_map/ppermute | solution.py:193
  52.6 0.6 reduce_sum.36
  54.0 5.9 %collective-permute-done.15.ahead = bf16[416,256]{1,0:T(8,128)(2,1)S(1)} collective-permute-done((bf16[416,256]{1,0:T(8,128)(2,1)S(1)}, bf16[416,256]{1,0:T(8,128)(2,1)S(1)}, u32[]{:S(2)}, u32[]{:S(2)}) %collective-permute-start.15) | collective-permute-done | bytes 213024 | tf_op jit(solution)/shard_map/ppermute | solution.py:193
  60.0 1.9 %collective-permute-start.19 = (bf16[256,256]{1,0:T(8,128)(2,1)S(1)}, bf16[256,256]{1,0:T(8,128)(2,1)S(1)}, u32[]{:S(2)}, u32[]{:S(2)}) collective-permute-start(bf16[256,256]{1,0:T(8,128)(2,1)S(1)} %get-tuple-element.66), channel_id=1, source_target_pairs={{0,16},{8,24},{16,0},{24,8},{32,48},{40,56},{48,32},{56,40},{64,80... | collective-permute-start | bytes 393224 | tf_op jit(solution)/shard_map/ppermute | solution.py:453
  61.9 1.1 %place_staying.1 = bf16[32,16,256]{2,1,0:T(8,128)(2,1)} custom-call(s32[8,512]{1,0:T(8,128)S(1)} %get-tuple-element.54.codes, bf16[400,256]{1,0:T(8,128)(2,1)S(1)} %get-tuple-element.65.first.kept, bf16[144,256]{1,0:T(8,128)(2,1)S(1)} %get-tuple-element.88.second), custom_call_target="tpu_custom_call" | custom-call | flops 8589934592 | bytes 1048576 | tf_op jit(solution)/shard_map/place_staying/pallas_call | solution.py:265
  63.0 11.3 %all-to-all-start = ((bf16[32,16,256]{2,1,0:T(8,128)(2,1)}), bf16[32,16,256]{2,1,0:T(8,128)(2,1)S(1)}, u32[]{:S(2)}, u32[]{:S(2)}) async-start(bf16[32,16,256]{2,1,0:T(8,128)(2,1)} %place_staying.1), calls=%async_computation | async-start | bytes 524288 | tf_op jit(solution)/shard_map/all_to_all | solution.py:468
  74.4 3.7 %collective-permute-done.19.received = bf16[256,256]{1,0:T(8,128)(2,1)S(1)} collective-permute-done((bf16[256,256]{1,0:T(8,128)(2,1)S(1)}, bf16[256,256]{1,0:T(8,128)(2,1)S(1)}, u32[]{:S(2)}, u32[]{:S(2)}) %collective-permute-start.19) | collective-permute-done | bytes 131104 | tf_op jit(solution)/shard_map/ppermute | solution.py:453
  78.1 1.0 place_crossing.1
  79.7 3.6 %all-to-all-done.near = bf16[32,16,256]{2,1,0:T(8,128)(2,1)S(1)} async-done(((bf16[32,16,256]{2,1,0:T(8,128)(2,1)}), bf16[32,16,256]{2,1,0:T(8,128)(2,1)S(1)}, u32[]{:S(2)}, u32[]{:S(2)}) %all-to-all-start) | async-done | bytes 262176 | tf_op jit(solution)/shard_map/all_to_all | solution.py:468
  83.3 6.4 %all-to-all-start.1 = ((bf16[32,16,256]{2,1,0:T(8,128)(2,1)}), bf16[32,16,256]{2,1,0:T(8,128)(2,1)S(1)}, u32[]{:S(2)}, u32[]{:S(2)}) async-start(bf16[32,16,256]{2,1,0:T(8,128)(2,1)} %get-tuple-element.89), calls=%async_computation.1 | async-start | bytes 524288 | tf_op jit(solution)/shard_map/all_to_all | solution.py:468
  90.1 8.7 %all-to-all-done.1.far = bf16[32,16,256]{2,1,0:T(8,128)(2,1)S(1)} async-done(((bf16[32,16,256]{2,1,0:T(8,128)(2,1)}), bf16[32,16,256]{2,1,0:T(8,128)(2,1)S(1)}, u32[]{:S(2)}, u32[]{:S(2)}) %all-to-all-start.1) | async-done | bytes 262176 | tf_op jit(solution)/shard_map/all_to_all | solution.py:468
  98.8 2.5 %rebuild_and_attend.1 = (bf16[256,512]{1,0:T(8,128)(2,1)}, bf16[2,16,1024]{2,1,0:T(8,128)(2,1)}) custom-call(bf16[32,16,256]{2,1,0:T(8,128)(2,1)S(1)} %all-to-all-done.near, bf16[32,16,256]{2,1,0:T(8,128)(2,1)S(1)} %all-to-all-done.1.far, bf16[256,256]{1,0:T(8,128)(2,1)S(1)} %copy-done, s32[1,256]{1,0:T(1,128)S(1)} %reshape.126.resident_valid, ...), custom_call_target="tpu_custom_call" | custom-call | tf_op jit(solution)/shard_map/rebuild_and_attend/pallas_call | solution.py:360
  (35 shorter events, 0.8 us)
Async XLA Ops:
  0.6 0.8 copy-start.1
  1.5 12.0 %copy-start.3 = (bf16[1024,2048]{1,0:T(8,128)(2,1)S(1)}, bf16[1024,2048]{1,0:T(8,128)(2,1)}, u32[]{:S(2)}) copy-start(bf16[1024,2048]{1,0:T(8,128)(2,1)} %weight.3) | copy-start | bytes 12582916
  5.9 46.7 %copy-start.6 = (s32[32]{0:T(128)S(1)}, s32[32]{0:T(128)}, u32[]{:S(2)}) copy-start(s32[32]{0:T(128)} %param.22) | copy-start | bytes 388
  5.9 48.0 %copy-start.4 = (bf16[512,1024]{1,0:T(8,128)(2,1)S(1)}, bf16[512,1024]{1,0:T(8,128)(2,1)}, u32[]{:S(2)}) copy-start(bf16[512,1024]{1,0:T(8,128)(2,1)} %hidden.1) | copy-start | bytes 3145732
  5.9 48.0 %copy-start.5 = (f32[1024]{0:T(1024)S(1)}, f32[1024]{0:T(1024)}, u32[]{:S(2)}) copy-start(f32[1024]{0:T(1024)} %param.17) | copy-start | bytes 12292
  5.9 48.0 %copy-start.7 = (s32[32]{0:T(128)S(1)}, s32[32]{0:T(128)}, u32[]{:S(2)}) copy-start(s32[32]{0:T(128)} %param.21) | copy-start | bytes 388
  5.9 15.7 %collective-permute-start.12 = (bf16[416,256]{1,0:T(8,128)(2,1)S(1)}, bf16[416,256]{1,0:T(8,128)(2,1)S(1)}, u32[]{:S(2)}, u32[]{:S(2)}) collective-permute-start(bf16[416,256]{1,0:T(8,128)(2,1)S(1)} %get-tuple-element.55), channel_id=1, source_target_pairs={{0,2},{2,4},{4,6},{6,7},{7,5},{5,3},{3,1},{1,0},{8,10},{10,12},{12... | collective-permute-start | bytes 638984 | tf_op jit(solution)/shard_map/ppermute | solution.py:193
  11.0 12.6 %collective-permute-start.16 = (bf16[416,256]{1,0:T(8,128)(2,1)S(1)}, bf16[416,256]{1,0:T(8,128)(2,1)S(1)}, u32[]{:S(2)}, u32[]{:S(2)}) collective-permute-start(bf16[416,256]{1,0:T(8,128)(2,1)S(1)} %get-tuple-element.61), channel_id=1, source_target_pairs={{2,0},{4,2},{6,4},{7,6},{5,7},{3,5},{1,3},{0,1},{10,8},{12,10},{14... | collective-permute-start | bytes 638984 | tf_op jit(solution)/shard_map/ppermute | solution.py:193
  21.6 14.4 %collective-permute-start.13 = (bf16[416,256]{1,0:T(8,128)(2,1)S(1)}, bf16[416,256]{1,0:T(8,128)(2,1)S(1)}, u32[]{:S(2)}, u32[]{:S(2)}) collective-permute-start(bf16[416,256]{1,0:T(8,128)(2,1)S(1)} %add_convert_fusion.9), channel_id=1, source_target_pairs={{0,2},{2,4},{4,6},{6,7},{7,5},{5,3},{3,1},{1,0},{8,10},{10,12},{12... | collective-permute-start | bytes 638984 | tf_op jit(solution)/shard_map/ppermute | solution.py:193
  23.7 14.4 %collective-permute-start.17 = (bf16[416,256]{1,0:T(8,128)(2,1)S(1)}, bf16[416,256]{1,0:T(8,128)(2,1)S(1)}, u32[]{:S(2)}, u32[]{:S(2)}) collective-permute-start(bf16[416,256]{1,0:T(8,128)(2,1)S(1)} %add_convert_fusion.6), channel_id=1, source_target_pairs={{2,0},{4,2},{6,4},{7,6},{5,7},{3,5},{1,3},{0,1},{10,8},{12,10},{14... | collective-permute-start | bytes 638984 | tf_op jit(solution)/shard_map/ppermute | solution.py:193
  36.1 14.5 %collective-permute-start.14 = (bf16[416,256]{1,0:T(8,128)(2,1)S(1)}, bf16[416,256]{1,0:T(8,128)(2,1)S(1)}, u32[]{:S(2)}, u32[]{:S(2)}) collective-permute-start(bf16[416,256]{1,0:T(8,128)(2,1)S(1)} %add_convert_fusion.8), channel_id=1, source_target_pairs={{0,2},{2,4},{4,6},{6,7},{7,5},{5,3},{3,1},{1,0},{8,10},{10,12},{12... | collective-permute-start | bytes 638984 | tf_op jit(solution)/shard_map/ppermute | solution.py:193
  38.1 15.8 %collective-permute-start.18 = (bf16[416,256]{1,0:T(8,128)(2,1)S(1)}, bf16[416,256]{1,0:T(8,128)(2,1)S(1)}, u32[]{:S(2)}, u32[]{:S(2)}) collective-permute-start(bf16[416,256]{1,0:T(8,128)(2,1)S(1)} %add_convert_fusion.5), channel_id=1, source_target_pairs={{2,0},{4,2},{6,4},{7,6},{5,7},{3,5},{1,3},{0,1},{10,8},{12,10},{14... | collective-permute-start | bytes 638984 | tf_op jit(solution)/shard_map/ppermute | solution.py:193
  50.7 9.2 %collective-permute-start.15 = (bf16[416,256]{1,0:T(8,128)(2,1)S(1)}, bf16[416,256]{1,0:T(8,128)(2,1)S(1)}, u32[]{:S(2)}, u32[]{:S(2)}) collective-permute-start(bf16[416,256]{1,0:T(8,128)(2,1)S(1)} %add_convert_fusion.7), channel_id=1, source_target_pairs={{0,2},{2,4},{4,6},{6,7},{7,5},{5,3},{3,1},{1,0},{8,10},{10,12},{12... | collective-permute-start | bytes 638984 | tf_op jit(solution)/shard_map/ppermute | solution.py:193
  60.0 18.1 %collective-permute-start.19 = (bf16[256,256]{1,0:T(8,128)(2,1)S(1)}, bf16[256,256]{1,0:T(8,128)(2,1)S(1)}, u32[]{:S(2)}, u32[]{:S(2)}) collective-permute-start(bf16[256,256]{1,0:T(8,128)(2,1)S(1)} %get-tuple-element.66), channel_id=1, source_target_pairs={{0,16},{8,24},{16,0},{24,8},{32,48},{40,56},{48,32},{56,40},{64,80... | collective-permute-start | bytes 393224 | tf_op jit(solution)/shard_map/ppermute | solution.py:453
  63.0 20.3 %all-to-all-start = ((bf16[32,16,256]{2,1,0:T(8,128)(2,1)}), bf16[32,16,256]{2,1,0:T(8,128)(2,1)S(1)}, u32[]{:S(2)}, u32[]{:S(2)}) async-start(bf16[32,16,256]{2,1,0:T(8,128)(2,1)} %place_staying.1), calls=%async_computation | async-start | bytes 524288 | tf_op jit(solution)/shard_map/all_to_all | solution.py:468
  74.3 15.4 %copy-start.8 = (s32[16]{0:T(128)S(1)}, s32[16]{0:T(128)}, u32[]{:S(2)}) copy-start(s32[16]{0:T(128)} %param.24) | copy-start | bytes 196
  74.3 15.6 %copy-start.9 = (s32[16]{0:T(128)S(1)}, s32[16]{0:T(128)}, u32[]{:S(2)}) copy-start(s32[16]{0:T(128)} %param.23) | copy-start | bytes 196
  74.4 24.4 %copy-start = (bf16[256,256]{1,0:T(8,128)(2,1)S(1)}, bf16[256,256]{1,0:T(8,128)(2,1)}, u32[]{:S(2)}) copy-start(bf16[256,256]{1,0:T(8,128)(2,1)} %resident.1) | copy-start | bytes 393220
  74.4 24.4 %copy-start.2 = (bf16[2,16,1024]{2,1,0:T(8,128)(2,1)S(1)}, bf16[2,16,1024]{2,1,0:T(8,128)(2,1)}, u32[]{:S(2)}) copy-start(bf16[2,16,1024]{2,1,0:T(8,128)(2,1)} %queries.1) | copy-start | bytes 196612
  83.3 15.4 %all-to-all-start.1 = ((bf16[32,16,256]{2,1,0:T(8,128)(2,1)}), bf16[32,16,256]{2,1,0:T(8,128)(2,1)S(1)}, u32[]{:S(2)}, u32[]{:S(2)}) async-start(bf16[32,16,256]{2,1,0:T(8,128)(2,1)} %get-tuple-element.89), calls=%async_computation.1 | async-start | bytes 524288 | tf_op jit(solution)/shard_map/all_to_all | solution.py:468

commit v7 on v6

--- a/solution.py
+++ b/solution.py
@@ -51,15 +51,37 @@
     return pltpu.make_async_copy(weight.at[:, columns], blocks.at[place], sems.at[place])
 
 
-def first_chunks(
-    offsets, dest, length, hidden, fresh, gain, weight, out_a, out_b, scaled, extra, codes, blocks, sems
-):
+def pair_of_chunks(capacity, scaled, extra, codes, block, mirrored, out, mirrored_out):
+    rows, lanes = scaled.shape[0], out.shape[1]
+    here = dot(scaled[...], block[...])
+    there = dot(scaled[...], mirrored[...])
+    row = iota((rows, lanes), 0)
+    crosses = (row < codes[1:2, :1]) & (row < capacity)
+    out[:rows, :] = jnp.where(crosses, there, here).astype(BF)
+    mirrored_out[:rows, :] = jnp.where(crosses, here, there).astype(BF)
+    out[rows:, :] = extra[...]
+    mirrored_out[rows:, :] = extra[...]
+
+
+def first_chunks(offsets, *refs):
+    operands, weight = refs[:5], refs[5]
+    outs, (scaled, extra, codes), (blocks, sems) = refs[6:8], refs[8:11], refs[11:13]
+    held, held_sems = refs[13:18], refs[18]
+    fetches = [
+        pltpu.make_async_copy(source, target, held_sems.at[i])
+        for i, (source, target) in enumerate(zip(operands, held))
+    ]
+    for fetch in fetches:
+        fetch.start()
     copies = [weight_copy(weight, blocks, sems, offset, i) for i, offset in enumerate(offsets)]
     for copy in copies:
         copy.start()
+    dest, length, gain, fresh, hidden = held
     requests = dest.shape[1]
     context = hidden.shape[0] // requests
     rows, capacity = scaled.shape[0], scaled.shape[0] - fresh.shape[0]
+    for fetch in fetches[:2]:
+        fetch.wait()
     half = half_of(lax.axis_index("inst"))
 
     def upright(line):
@@ -83,51 +105,61 @@
     code = jnp.sum(code, axis=0, keepdims=True) - 1
     codes[...] = jnp.where(iota(codes.shape, 0) == 0, code, crossing)
     select = jnp.where(target == iota((capacity, hidden.shape[0]), 0), 1.0, 0.0).astype(BF)
+    for fetch in fetches[2:]:
+        fetch.wait()
     wide = jnp.concatenate([dot(select, hidden[...]), fresh[...].astype(F32)], axis=0)
     scaled[...] = (wide * gain[...]).astype(BF)
     square = wide * wide
-    high = square.astype(BF)
-    low = (square - high.astype(F32)).astype(BF)
-    lanes = out_a.shape[1]
-    ones = jnp.ones((EXTRA, wide.shape[1]), BF)
-    total = jnp.zeros((EXTRA, lanes), F32)
-    for index, start in enumerate(range(0, rows, lanes)):
-        stop = min(start + lanes, rows)
-        part = dot(ones, high[start:stop], ((1,), (1,))) + dot(ones, low[start:stop], ((1,), (1,)))
-        if stop - start < lanes:
-            part = jnp.concatenate([part, jnp.zeros((EXTRA, lanes - stop + start), F32)], axis=1)
-        total = jnp.where(iota((EXTRA, lanes), 0) == index, part, total)
-    extra[...] = total.astype(BF)
-    for place_here, out in enumerate((out_a, out_b)):
-        copies[place_here].wait()
-        out[:rows, :] = dot(scaled[...], blocks[place_here]).astype(BF)
-        out[rows:, :] = extra[...]
-
-
-def later_chunks(offsets, scaled, extra, weight, *refs):
+    narrow = sum(square[:, i : i + TILE] for i in range(TILE, square.shape[1], TILE))
+    column = jnp.sum(narrow + square[:, :TILE], axis=1, keepdims=True)
+    lanes = extra.shape[1]
+    totals = [jnp.zeros((EXTRA, TILE), F32) for _ in range(0, lanes, TILE)]
+    for start in range(0, rows, TILE):
+        size = min(TILE, rows - start)
+        diagonal = iota((size, TILE), 0) == iota((size, TILE), 1)
+        line = jnp.where(diagonal, column[start : start + size], 0.0)
+        line = jnp.sum(line, axis=0, keepdims=True)
+        place_here = start % lanes // TILE
+        totals[place_here] = jnp.where(
+            iota((EXTRA, TILE), 0) == start // lanes, line, totals[place_here]
+        )
+    extra[...] = jnp.concatenate(totals, axis=1).astype(BF)
+    for copy in copies:
+        copy.wait()
+    pair_of_chunks(capacity, scaled, extra, codes, blocks.at[0], blocks.at[1], *outs)
+
+
+def later_chunks(offsets, capacity, scaled, extra, codes, weight, *refs):
     outs, (blocks, sems) = refs[:-2], refs[-2:]
     copies = [weight_copy(weight, blocks, sems, offset, i) for i, offset in enumerate(offsets)]
     for copy in copies:
         copy.start()
-    rows = scaled.shape[0]
-    for place_here, out in enumerate(outs):
-        copies[place_here].wait()
-        out[:rows, :] = dot(scaled[...], blocks[place_here]).astype(BF)
-        out[rows:, :] = extra[...]
+    for i in range(0, len(copies), 2):
+        copies[i].wait()
+        copies[i + 1].wait()
+        pair_of_chunks(
+            capacity, scaled, extra, codes, blocks.at[i], blocks.at[i + 1], *outs[i : i + 2]
+        )
 
 
 def project_chunks(hidden, fresh, gain, weight, dest, length, capacity, lanes):
     rows, depth = capacity + fresh.shape[0], hidden.shape[1]
     chunk = jax.ShapeDtypeStruct((rows + EXTRA, lanes), BF)
-    offsets = ring_offsets(lax.axis_size("tensor"))
+    tensors = lax.axis_size("tensor")
+    offsets = ring_offsets(tensors)
+    pairs = []
+    for offset in offsets:
+        if all(offset not in pair for pair in pairs):
+            pairs.append((offset, offset - tensors // 2 if offset > 0 else offset + tensors // 2))
     vmem = pl.BlockSpec(memory_space=pltpu.VMEM)
     hbm = pl.BlockSpec(memory_space=pltpu.HBM)
 
-    def options(count, name):
+    def options(count, name, *more):
         return dict(
             scratch_shapes=[
                 pltpu.VMEM((count, depth, lanes), BF),
                 pltpu.SemaphoreType.DMA((count,)),
+                *more,
             ],
             compiler_params=pltpu.CompilerParams(vmem_limit_bytes=VMEM_BYTES),
             cost_estimate=pl.CostEstimate(
@@ -138,9 +170,10 @@
             name=name,
         )
 
-    out_a, out_b, scaled, extra, codes = pl.pallas_call(
-        functools.partial(first_chunks, offsets[:2]),
-        in_specs=[vmem, vmem, vmem, vmem, vmem, hbm],
+    operands = [dest[None, :], length[None, :], gain, fresh, hidden]
+    *first, scaled, extra, codes = pl.pallas_call(
+        functools.partial(first_chunks, pairs[0]),
+        in_specs=[hbm] * 6,
         out_shape=[
             chunk,
             chunk,
@@ -148,16 +181,24 @@
             jax.ShapeDtypeStruct((EXTRA, lanes), BF),
             jax.ShapeDtypeStruct((8, hidden.shape[0]), jnp.int32),
         ],
-        **options(2, "first_chunks"),
-    )(dest[None, :], length[None, :], hidden, fresh, gain, weight)
-    rest = len(offsets) - 2
-    later = pl.pallas_call(
-        functools.partial(later_chunks, offsets[2:]),
-        in_specs=[vmem, vmem, hbm],
-        out_shape=[chunk] * rest,
-        **options(rest, "later_chunks"),
-    )(scaled, extra, weight)
-    return [out_a, out_b, *later], codes
+        **options(
+            2,
+            "first_chunks",
+            *(pltpu.VMEM(operand.shape, operand.dtype) for operand in operands),
+            pltpu.SemaphoreType.DMA((len(operands),)),
+        ),
+    )(*operands, weight)
+    chunks = dict(zip(pairs[0], first))
+    for group, name in ((pairs[1:2], "second_chunks"), (pairs[2:], "later_chunks")):
+        group = [offset for pair in group for offset in pair]
+        outs = pl.pallas_call(
+            functools.partial(later_chunks, group, capacity),
+            in_specs=[vmem, vmem, vmem, hbm],
+            out_shape=[chunk] * len(group),
+            **options(len(group), name),
+        )(scaled, extra, codes, weight)
+        chunks.update(zip(group, outs))
+    return [chunks[offset] for offset in offsets], codes
 
 
 def ring_offsets(tensors):
@@ -381,8 +422,14 @@
         distance *= 2
     parts = jnp.dot((wide * gain).astype(BF), weight, preferred_element_type=F32).astype(BF)
     order = ring_order(tensors)
+    crosses = capacity + jnp.arange(left, dtype=jnp.int32)[:, None] < codes[1, 0]
+
+    def block_of(owner):
+        return lax.dynamic_slice_in_dim(parts, owner * lanes, lanes, 1)
+
     chunks = [
-        lax.dynamic_slice_in_dim(parts, order[i] * lanes, lanes, 1) for i in range(tensors)
+        jnp.where(crosses, block_of(tensors - 1 - order[i]), block_of(order[i]))
+        for i in range(tensors)
     ]
     ahead, behind, own = ring_sums(chunks)
     total = ahead.astype(F32) + behind.astype(F32) + own.astype(F32)
@@ -447,10 +494,15 @@
         lambda: jnp.zeros((leaving - capacity, owned), BF),
     )
 
-    halves = [(i, i ^ 2) for i in range(instances)]
+    tensors = lax.axis_size("tensor")
+    halves = [
+        (i * tensors + t, (i ^ 2) * tensors + tensors - 1 - t)
+        for i in range(instances)
+        for t in range(tensors)
+    ]
     planes = [[i for i in range(instances) if half_of(i) == half] for half in range(2)]
 
-    received = lax.ppermute(crossing_rows, "inst", halves)
+    received = lax.ppermute(crossing_rows, ("inst", "tensor"), halves)
     blocks_type = jax.ShapeDtypeStruct((plane, context, owned), BF)
     vmem = pl.BlockSpec(memory_space=pltpu.VMEM)
     staying = place(place_staying, blocks_type, vmem, 1 << 33, codes, kept, rest)
@@ -471,8 +523,8 @@
 
     def all_crossing():
         rows = jnp.concatenate([kept[:capacity], rest], axis=0)
-        rows = lax.ppermute(rows, "inst", halves)
-        notes = lax.ppermute(codes, "inst", halves)
+        rows = lax.ppermute(rows, ("inst", "tensor"), halves)
+        notes = lax.ppermute(codes, ("inst", "tensor"), halves)
         lane = jnp.arange(leaving, dtype=jnp.int32)[None, :]
         slot = jnp.arange(plane * context, dtype=jnp.int32)[:, None]
         route = (slot == notes[0:1]) & (lane < notes[1:2])

time: 102 us -> 102 us (level)
  starting transfers between devices: 43.9 us -> 52.6 us
  waiting for transfers between devices: 39.9 us -> 34.6 us
  Pallas kernels: 13 us -> 9.76 us
    all_to_all x2, starting transfers between devices: 17.8 us -> 23.2 us  [over_plane(): lax.all_to_all(rows, 'inst', split_axis=0, concat_axis=0, tiled=True, axi...]
    ppermute x7, waiting for transfers between devices: 23.9 us -> 18.5 us  [ring_sums(): sums[way] = lax.ppermute(chunk, 'tensor', forward if way else backward)]
    ppermute x1, starting transfers between devices: 1.92 us -> 6.38 us  [shards(): received = lax.ppermute(crossing_rows, ('inst', 'tensor'), halves)]
    all_to_all x2, waiting for transfers between devices: 12.3 us -> 16.1 us  [over_plane(): lax.all_to_all(rows, 'inst', split_axis=0, concat_axis=0, tiled=True, axi...]
    ppermute x1, waiting for transfers between devices: 3.72 us -> 0.01 us  [shards(): received = lax.ppermute(crossing_rows, ('inst', 'tensor'), halves)]
    pallas_call x2 -> x3, Pallas kernels: 8.38 us -> 5.1 us  [the longest x1 2.75 us: project_chunks(): pl.pallas_call(functools.partial(first_chunks, pairs[0]), in_specs=[hbm]...]
    ppermute x7, starting transfers between devices: 24.2 us -> 23 us  [ring_sums(): sums[way] = lax.ppermute(chunk, 'tensor', forward if way else backward)]
  transfers between devices with their start and end apart: 10 -> 10, of which waited for: 7 -> 8; matrix products, arithmetic and copies ran while one was open for 1% -> 1% of each run, Pallas kernels for 6% -> 4%
where the time goes in v7:
time: 102 us; the launch traced here: 101 us
  starting transfers between devices  52.6 us (52%)
  waiting for transfers between devices  34.6 us (34%)
  Pallas kernels  9.76 us (10%)
  between operations  2.25 us (2%)
  local copies, waits for them, and re-layouts  1.08 us (1%)
    all_to_all x2, starting transfers between devices, over_plane(): lax.all_to_all(rows, 'inst', split_axis=0, concat_axis=0, tiled=True, axi...  23.2 us
    ppermute x7, starting transfers between devices, ring_sums(): sums[way] = lax.ppermute(chunk, 'tensor', forward if way else backward)  23 us
    ppermute x7, waiting for transfers between devices, ring_sums(): sums[way] = lax.ppermute(chunk, 'tensor', forward if way else backward)  18.5 us
    all_to_all x2, waiting for transfers between devices, over_plane(): lax.all_to_all(rows, 'inst', split_axis=0, concat_axis=0, tiled=True, axi...  16.1 us
    ppermute x1, starting transfers between devices, shards(): received = lax.ppermute(crossing_rows, ('inst', 'tensor'), halves)  6.38 us
    pallas_call x1, Pallas kernels, project_chunks(): pl.pallas_call(functools.partial(first_chunks, pairs[0]), in_specs=[hbm]...  2.75 us
    pallas_call x1, Pallas kernels, rebuild(): pl.pallas_call(rebuild_and_attend, out_shape=[jax.ShapeDtypeStruct((near....  2.48 us
    pallas_call x2, Pallas kernels, project_chunks(): pl.pallas_call(functools.partial(later_chunks, group, capacity), in_specs...  2.35 us
  transfers between devices with their start and end apart: 10, of which 8 were waited for; matrix products, arithmetic and copies ran while one was open for 1% of the time, Pallas kernels for 4%

profile of v7, /device:TPU:129, one launch (start us, length us, event | category | flops | bytes accessed | tf_op | source)
XLA Modules:
  0.0 101.3 jit_solution(14590290017984472406)
XLA Ops:
  0.6 0.8 copy-done.1
  1.5 2.7 %first_chunks.1 = (bf16[416,256]{1,0:T(8,128)(2,1)S(1)}, bf16[416,256]{1,0:T(8,128)(2,1)S(1)}, bf16[400,1024]{1,0:T(8,128)(2,1)S(1)}, bf16[16,256]{1,0:T(8,128)(2,1)S(1)}, s32[8,512]{1,0:T(8,128)S(1)}) custom-call(s32[1,32]{1,0:T(1,128)} %bitcast.35, s32[1,32]{1,0:T(1,128)} %bitcast.34, f32[1,1024]{1,0:T(1,128)} %bitcast.29, bf16[32,1024]{1,0:T(8,128)(2,1)S(1)} %bitcast.28, ...), custom_call_target="tpu_custom_call" | custom-call | flops 419430400 | bytes 2277376 | tf_op jit(solution)/shard_map/first_chunks/pallas_call | solution.py:174
  4.2 4.9 %collective-permute-start.12 = (bf16[416,256]{1,0:T(8,128)(2,1)S(1)}, bf16[416,256]{1,0:T(8,128)(2,1)S(1)}, u32[]{:S(2)}, u32[]{:S(2)}) collective-permute-start(bf16[416,256]{1,0:T(8,128)(2,1)S(1)} %get-tuple-element.58), channel_id=1, source_target_pairs={{0,2},{2,4},{4,6},{6,7},{7,5},{5,3},{3,1},{1,0},{8,10},{10,12},{12... | collective-permute-start | bytes 638984 | tf_op jit(solution)/shard_map/ppermute | solution.py:234
  9.1 0.8 second_chunks.1
  10.0 2.6 %collective-permute-start.16 = (bf16[416,256]{1,0:T(8,128)(2,1)S(1)}, bf16[416,256]{1,0:T(8,128)(2,1)S(1)}, u32[]{:S(2)}, u32[]{:S(2)}) collective-permute-start(bf16[416,256]{1,0:T(8,128)(2,1)S(1)} %get-tuple-element.64), channel_id=1, source_target_pairs={{2,0},{4,2},{6,4},{7,6},{5,7},{3,5},{1,3},{0,1},{10,8},{12,10},{14... | collective-permute-start | bytes 638984 | tf_op jit(solution)/shard_map/ppermute | solution.py:234
  12.6 1.6 %later_chunks.1 = (bf16[416,256]{1,0:T(8,128)(2,1)S(1)}, bf16[416,256]{1,0:T(8,128)(2,1)S(1)}, bf16[416,256]{1,0:T(8,128)(2,1)S(1)}, bf16[416,256]{1,0:T(8,128)(2,1)S(1)}) custom-call(bf16[400,1024]{1,0:T(8,128)(2,1)S(1)} %get-tuple-element.59.scaled, bf16[16,256]{1,0:T(8,128)(2,1)S(1)} %get-tuple-element.60.extra, s32[8,512]{1,0:T(8,128)S(1)} %get-tuple-element.57.codes, ...), custom_call_target="tpu_custom_call" | custom-call | flops 838860800 | bytes 3735552 | tf_op jit(solution)/shard_map/later_chunks/pallas_call | solution.py:194
  14.2 2.1 %collective-permute-done.12 = bf16[416,256]{1,0:T(8,128)(2,1)S(1)} collective-permute-done((bf16[416,256]{1,0:T(8,128)(2,1)S(1)}, bf16[416,256]{1,0:T(8,128)(2,1)S(1)}, u32[]{:S(2)}, u32[]{:S(2)}) %collective-permute-start.12) | collective-permute-done | bytes 213024 | tf_op jit(solution)/shard_map/ppermute | solution.py:234
  16.4 1.9 %collective-permute-start.13 = (bf16[416,256]{1,0:T(8,128)(2,1)S(1)}, bf16[416,256]{1,0:T(8,128)(2,1)S(1)}, u32[]{:S(2)}, u32[]{:S(2)}) collective-permute-start(bf16[416,256]{1,0:T(8,128)(2,1)S(1)} %add_convert_fusion.9), channel_id=1, source_target_pairs={{0,2},{2,4},{4,6},{6,7},{7,5},{5,3},{3,1},{1,0},{8,10},{10,12},{12... | collective-permute-start | bytes 638984 | tf_op jit(solution)/shard_map/ppermute | solution.py:234
  18.3 1.7 %collective-permute-done.16 = bf16[416,256]{1,0:T(8,128)(2,1)S(1)} collective-permute-done((bf16[416,256]{1,0:T(8,128)(2,1)S(1)}, bf16[416,256]{1,0:T(8,128)(2,1)S(1)}, u32[]{:S(2)}, u32[]{:S(2)}) %collective-permute-start.16) | collective-permute-done | bytes 213024 | tf_op jit(solution)/shard_map/ppermute | solution.py:234
  20.1 3.8 %collective-permute-start.17 = (bf16[416,256]{1,0:T(8,128)(2,1)S(1)}, bf16[416,256]{1,0:T(8,128)(2,1)S(1)}, u32[]{:S(2)}, u32[]{:S(2)}) collective-permute-start(bf16[416,256]{1,0:T(8,128)(2,1)S(1)} %add_convert_fusion.6), channel_id=1, source_target_pairs={{2,0},{4,2},{6,4},{7,6},{5,7},{3,5},{1,3},{0,1},{10,8},{12,10},{14... | collective-permute-start | bytes 638984 | tf_op jit(solution)/shard_map/ppermute | solution.py:234
  23.9 1.9 %collective-permute-done.13 = bf16[416,256]{1,0:T(8,128)(2,1)S(1)} collective-permute-done((bf16[416,256]{1,0:T(8,128)(2,1)S(1)}, bf16[416,256]{1,0:T(8,128)(2,1)S(1)}, u32[]{:S(2)}, u32[]{:S(2)}) %collective-permute-start.13) | collective-permute-done | bytes 213024 | tf_op jit(solution)/shard_map/ppermute | solution.py:234
  25.8 1.9 %collective-permute-start.14 = (bf16[416,256]{1,0:T(8,128)(2,1)S(1)}, bf16[416,256]{1,0:T(8,128)(2,1)S(1)}, u32[]{:S(2)}, u32[]{:S(2)}) collective-permute-start(bf16[416,256]{1,0:T(8,128)(2,1)S(1)} %add_convert_fusion.8), channel_id=1, source_target_pairs={{0,2},{2,4},{4,6},{6,7},{7,5},{5,3},{3,1},{1,0},{8,10},{10,12},{12... | collective-permute-start | bytes 638984 | tf_op jit(solution)/shard_map/ppermute | solution.py:234
  27.9 5.4 %collective-permute-start.18 = (bf16[416,256]{1,0:T(8,128)(2,1)S(1)}, bf16[416,256]{1,0:T(8,128)(2,1)S(1)}, u32[]{:S(2)}, u32[]{:S(2)}) collective-permute-start(bf16[416,256]{1,0:T(8,128)(2,1)S(1)} %add_convert_fusion.5), channel_id=1, source_target_pairs={{2,0},{4,2},{6,4},{7,6},{5,7},{3,5},{1,3},{0,1},{10,8},{12,10},{14... | collective-permute-start | bytes 638984 | tf_op jit(solution)/shard_map/ppermute | solution.py:234
  33.3 2.7 %collective-permute-done.14 = bf16[416,256]{1,0:T(8,128)(2,1)S(1)} collective-permute-done((bf16[416,256]{1,0:T(8,128)(2,1)S(1)}, bf16[416,256]{1,0:T(8,128)(2,1)S(1)}, u32[]{:S(2)}, u32[]{:S(2)}) %collective-permute-start.14) | collective-permute-done | bytes 213024 | tf_op jit(solution)/shard_map/ppermute | solution.py:234
  36.1 2.5 %collective-permute-start.15 = (bf16[416,256]{1,0:T(8,128)(2,1)S(1)}, bf16[416,256]{1,0:T(8,128)(2,1)S(1)}, u32[]{:S(2)}, u32[]{:S(2)}) collective-permute-start(bf16[416,256]{1,0:T(8,128)(2,1)S(1)} %add_convert_fusion.7), channel_id=1, source_target_pairs={{0,2},{2,4},{4,6},{6,7},{7,5},{5,3},{3,1},{1,0},{8,10},{10,12},{12... | collective-permute-start | bytes 638984 | tf_op jit(solution)/shard_map/ppermute | solution.py:234
  39.9 9.9 %collective-permute-done.15.ahead = bf16[416,256]{1,0:T(8,128)(2,1)S(1)} collective-permute-done((bf16[416,256]{1,0:T(8,128)(2,1)S(1)}, bf16[416,256]{1,0:T(8,128)(2,1)S(1)}, u32[]{:S(2)}, u32[]{:S(2)}) %collective-permute-start.15) | collective-permute-done | bytes 213024 | tf_op jit(solution)/shard_map/ppermute | solution.py:234
  50.0 6.4 %collective-permute-start.19 = (bf16[256,256]{1,0:T(8,128)(2,1)S(1)}, bf16[256,256]{1,0:T(8,128)(2,1)S(1)}, u32[]{:S(2)}, u32[]{:S(2)}) collective-permute-start(bf16[256,256]{1,0:T(8,128)(2,1)S(1)} %get-tuple-element.69), channel_id=1, source_target_pairs={{0,23},{1,22},{2,21},{3,20},{4,19},{5,18},{6,17},{7,16},{8,31},{9,... | collective-permute-start | bytes 393224 | tf_op jit(solution)/shard_map/ppermute | solution.py:505
  56.4 1.1 %place_staying.1 = bf16[32,16,256]{2,1,0:T(8,128)(2,1)} custom-call(s32[8,512]{1,0:T(8,128)S(1)} %get-tuple-element.57.codes, bf16[400,256]{1,0:T(8,128)(2,1)S(1)} %get-tuple-element.68.first.kept, bf16[144,256]{1,0:T(8,128)(2,1)S(1)} %get-tuple-element.89.second), custom_call_target="tpu_custom_call" | custom-call | flops 8589934592 | bytes 1048576 | tf_op jit(solution)/shard_map/place_staying/pallas_call | solution.py:306
  57.5 19.5 %all-to-all-start = ((bf16[32,16,256]{2,1,0:T(8,128)(2,1)}), bf16[32,16,256]{2,1,0:T(8,128)(2,1)S(1)}, u32[]{:S(2)}, u32[]{:S(2)}) async-start(bf16[32,16,256]{2,1,0:T(8,128)(2,1)} %place_staying.1), calls=%async_computation | async-start | bytes 524288 | tf_op jit(solution)/shard_map/all_to_all | solution.py:520
  77.0 1.0 place_crossing.1
  78.7 7.3 %all-to-all-done.near = bf16[32,16,256]{2,1,0:T(8,128)(2,1)S(1)} async-done(((bf16[32,16,256]{2,1,0:T(8,128)(2,1)}), bf16[32,16,256]{2,1,0:T(8,128)(2,1)S(1)}, u32[]{:S(2)}, u32[]{:S(2)}) %all-to-all-start) | async-done | bytes 262176 | tf_op jit(solution)/shard_map/all_to_all | solution.py:520
  86.0 3.7 %all-to-all-start.1 = ((bf16[32,16,256]{2,1,0:T(8,128)(2,1)}), bf16[32,16,256]{2,1,0:T(8,128)(2,1)S(1)}, u32[]{:S(2)}, u32[]{:S(2)}) async-start(bf16[32,16,256]{2,1,0:T(8,128)(2,1)} %get-tuple-element.90), calls=%async_computation.1 | async-start | bytes 524288 | tf_op jit(solution)/shard_map/all_to_all | solution.py:520
  90.0 8.8 %all-to-all-done.1.far = bf16[32,16,256]{2,1,0:T(8,128)(2,1)S(1)} async-done(((bf16[32,16,256]{2,1,0:T(8,128)(2,1)}), bf16[32,16,256]{2,1,0:T(8,128)(2,1)S(1)}, u32[]{:S(2)}, u32[]{:S(2)}) %all-to-all-start.1) | async-done | bytes 262176 | tf_op jit(solution)/shard_map/all_to_all | solution.py:520
  98.8 2.5 %rebuild_and_attend.1 = (bf16[256,512]{1,0:T(8,128)(2,1)}, bf16[2,16,1024]{2,1,0:T(8,128)(2,1)}) custom-call(bf16[32,16,256]{2,1,0:T(8,128)(2,1)S(1)} %all-to-all-done.near, bf16[32,16,256]{2,1,0:T(8,128)(2,1)S(1)} %all-to-all-done.1.far, bf16[256,256]{1,0:T(8,128)(2,1)S(1)} %copy-done, s32[1,256]{1,0:T(1,128)S(1)} %reshape.161.resident_valid, ...), custom_call_target="tpu_custom_call" | custom-call | tf_op jit(solution)/shard_map/rebuild_and_attend/pallas_call | solution.py:401
  (36 shorter events, 1.5 us)
Async XLA Ops:
  0.6 0.8 copy-start.1
  1.5 7.7 %copy-start.3 = (bf16[1024,2048]{1,0:T(8,128)(2,1)S(1)}, bf16[1024,2048]{1,0:T(8,128)(2,1)}, u32[]{:S(2)}) copy-start(bf16[1024,2048]{1,0:T(8,128)(2,1)} %weight.3) | copy-start | bytes 12582916
  4.2 12.1 %collective-permute-start.12 = (bf16[416,256]{1,0:T(8,128)(2,1)S(1)}, bf16[416,256]{1,0:T(8,128)(2,1)S(1)}, u32[]{:S(2)}, u32[]{:S(2)}) collective-permute-start(bf16[416,256]{1,0:T(8,128)(2,1)S(1)} %get-tuple-element.58), channel_id=1, source_target_pairs={{0,2},{2,4},{4,6},{6,7},{7,5},{5,3},{3,1},{1,0},{8,10},{10,12},{12... | collective-permute-start | bytes 638984 | tf_op jit(solution)/shard_map/ppermute | solution.py:234
  9.9 28.6 %copy-start.6 = (s32[32]{0:T(128)S(1)}, s32[32]{0:T(128)}, u32[]{:S(2)}) copy-start(s32[32]{0:T(128)} %param.22) | copy-start | bytes 388
  10.0 29.9 %copy-start.4 = (bf16[512,1024]{1,0:T(8,128)(2,1)S(1)}, bf16[512,1024]{1,0:T(8,128)(2,1)}, u32[]{:S(2)}) copy-start(bf16[512,1024]{1,0:T(8,128)(2,1)} %refs_4_.1) | copy-start | bytes 3145732
  10.0 29.9 %copy-start.5 = (f32[1024]{0:T(1024)S(1)}, f32[1024]{0:T(1024)}, u32[]{:S(2)}) copy-start(f32[1024]{0:T(1024)} %param.17) | copy-start | bytes 12292
  10.0 29.9 %copy-start.7 = (s32[32]{0:T(128)S(1)}, s32[32]{0:T(128)}, u32[]{:S(2)}) copy-start(s32[32]{0:T(128)} %param.21) | copy-start | bytes 388
  10.0 10.0 %collective-permute-start.16 = (bf16[416,256]{1,0:T(8,128)(2,1)S(1)}, bf16[416,256]{1,0:T(8,128)(2,1)S(1)}, u32[]{:S(2)}, u32[]{:S(2)}) collective-permute-start(bf16[416,256]{1,0:T(8,128)(2,1)S(1)} %get-tuple-element.64), channel_id=1, source_target_pairs={{2,0},{4,2},{6,4},{7,6},{5,7},{3,5},{1,3},{0,1},{10,8},{12,10},{14... | collective-permute-start | bytes 638984 | tf_op jit(solution)/shard_map/ppermute | solution.py:234
  16.4 9.4 %collective-permute-start.13 = (bf16[416,256]{1,0:T(8,128)(2,1)S(1)}, bf16[416,256]{1,0:T(8,128)(2,1)S(1)}, u32[]{:S(2)}, u32[]{:S(2)}) collective-permute-start(bf16[416,256]{1,0:T(8,128)(2,1)S(1)} %add_convert_fusion.9), channel_id=1, source_target_pairs={{0,2},{2,4},{4,6},{6,7},{7,5},{5,3},{3,1},{1,0},{8,10},{10,12},{12... | collective-permute-start | bytes 638984 | tf_op jit(solution)/shard_map/ppermute | solution.py:234
  20.1 7.8 %collective-permute-start.17 = (bf16[416,256]{1,0:T(8,128)(2,1)S(1)}, bf16[416,256]{1,0:T(8,128)(2,1)S(1)}, u32[]{:S(2)}, u32[]{:S(2)}) collective-permute-start(bf16[416,256]{1,0:T(8,128)(2,1)S(1)} %add_convert_fusion.6), channel_id=1, source_target_pairs={{2,0},{4,2},{6,4},{7,6},{5,7},{3,5},{1,3},{0,1},{10,8},{12,10},{14... | collective-permute-start | bytes 638984 | tf_op jit(solution)/shard_map/ppermute | solution.py:234
  25.8 10.2 %collective-permute-start.14 = (bf16[416,256]{1,0:T(8,128)(2,1)S(1)}, bf16[416,256]{1,0:T(8,128)(2,1)S(1)}, u32[]{:S(2)}, u32[]{:S(2)}) collective-permute-start(bf16[416,256]{1,0:T(8,128)(2,1)S(1)} %add_convert_fusion.8), channel_id=1, source_target_pairs={{0,2},{2,4},{4,6},{6,7},{7,5},{5,3},{3,1},{1,0},{8,10},{10,12},{12... | collective-permute-start | bytes 638984 | tf_op jit(solution)/shard_map/ppermute | solution.py:234
  27.9 12.0 %collective-permute-start.18 = (bf16[416,256]{1,0:T(8,128)(2,1)S(1)}, bf16[416,256]{1,0:T(8,128)(2,1)S(1)}, u32[]{:S(2)}, u32[]{:S(2)}) collective-permute-start(bf16[416,256]{1,0:T(8,128)(2,1)S(1)} %add_convert_fusion.5), channel_id=1, source_target_pairs={{2,0},{4,2},{6,4},{7,6},{5,7},{3,5},{1,3},{0,1},{10,8},{12,10},{14... | collective-permute-start | bytes 638984 | tf_op jit(solution)/shard_map/ppermute | solution.py:234
  36.1 13.8 %collective-permute-start.15 = (bf16[416,256]{1,0:T(8,128)(2,1)S(1)}, bf16[416,256]{1,0:T(8,128)(2,1)S(1)}, u32[]{:S(2)}, u32[]{:S(2)}) collective-permute-start(bf16[416,256]{1,0:T(8,128)(2,1)S(1)} %add_convert_fusion.7), channel_id=1, source_target_pairs={{0,2},{2,4},{4,6},{6,7},{7,5},{5,3},{3,1},{1,0},{8,10},{10,12},{12... | collective-permute-start | bytes 638984 | tf_op jit(solution)/shard_map/ppermute | solution.py:234
  50.0 27.0 %collective-permute-start.19 = (bf16[256,256]{1,0:T(8,128)(2,1)S(1)}, bf16[256,256]{1,0:T(8,128)(2,1)S(1)}, u32[]{:S(2)}, u32[]{:S(2)}) collective-permute-start(bf16[256,256]{1,0:T(8,128)(2,1)S(1)} %get-tuple-element.69), channel_id=1, source_target_pairs={{0,23},{1,22},{2,21},{3,20},{4,19},{5,18},{6,17},{7,16},{8,31},{9,... | collective-permute-start | bytes 393224 | tf_op jit(solution)/shard_map/ppermute | solution.py:505
  57.5 28.5 %all-to-all-start = ((bf16[32,16,256]{2,1,0:T(8,128)(2,1)}), bf16[32,16,256]{2,1,0:T(8,128)(2,1)S(1)}, u32[]{:S(2)}, u32[]{:S(2)}) async-start(bf16[32,16,256]{2,1,0:T(8,128)(2,1)} %place_staying.1), calls=%async_computation | async-start | bytes 524288 | tf_op jit(solution)/shard_map/all_to_all | solution.py:520
  77.0 12.7 %copy-start.8 = (s32[16]{0:T(128)S(1)}, s32[16]{0:T(128)}, u32[]{:S(2)}) copy-start(s32[16]{0:T(128)} %param.24) | copy-start | bytes 196
  77.0 12.8 %copy-start.9 = (s32[16]{0:T(128)S(1)}, s32[16]{0:T(128)}, u32[]{:S(2)}) copy-start(s32[16]{0:T(128)} %param.23) | copy-start | bytes 196
  77.0 21.8 %copy-start = (bf16[256,256]{1,0:T(8,128)(2,1)S(1)}, bf16[256,256]{1,0:T(8,128)(2,1)}, u32[]{:S(2)}) copy-start(bf16[256,256]{1,0:T(8,128)(2,1)} %resident.1) | copy-start | bytes 393220
  77.0 21.8 %copy-start.2 = (bf16[2,16,1024]{2,1,0:T(8,128)(2,1)S(1)}, bf16[2,16,1024]{2,1,0:T(8,128)(2,1)}, u32[]{:S(2)}) copy-start(bf16[2,16,1024]{2,1,0:T(8,128)(2,1)} %queries.1) | copy-start | bytes 196612
  86.0 12.8 %all-to-all-start.1 = ((bf16[32,16,256]{2,1,0:T(8,128)(2,1)}), bf16[32,16,256]{2,1,0:T(8,128)(2,1)S(1)}, u32[]{:S(2)}, u32[]{:S(2)}) async-start(bf16[32,16,256]{2,1,0:T(8,128)(2,1)} %get-tuple-element.90), calls=%async_computation.1 | async-start | bytes 524288 | tf_op jit(solution)/shard_map/all_to_all | solution.py:520

commit v8 on v7

--- a/solution.py
+++ b/solution.py
@@ -291,45 +291,45 @@
     out[...] = routed(jnp.where(route, 1.0, 0.0), rows).reshape(out.shape)
 
 
-def place_crossing(received, codes, out, most):
-    slots, context, lanes = out.shape
+def place_crossing(received, codes, near, out, most):
+    slots, context, lanes = near.shape
     sent = received.shape[0] - EXTRA
     notes = received[sent:, :].astype(F32).astype(jnp.int32)
     code = notes[0:1, :sent] * context + notes[1:2, :sent]
     route = iota((slots * context, sent), 0) == code
-    out[...] = routed(jnp.where(route, 1.0, 0.0), received[:sent, :]).reshape(out.shape)
+    out[:, :context, :] = near[...]
+    out[:, context:, :] = routed(jnp.where(route, 1.0, 0.0), received[:sent, :]).reshape(near.shape)
     counts = jnp.maximum(notes[2:3, :sent] * context + notes[3:4, :sent], codes[1:2, :sent])
     most[0] = jnp.max(counts)
 
 
-def place(kernel, out_shape, out_specs, weighs, *operands):
+def place(kernel, out_shape, out_specs, *operands):
     return pl.pallas_call(
         kernel,
         out_shape=out_shape,
         out_specs=out_specs,
         compiler_params=pltpu.CompilerParams(vmem_limit_bytes=VMEM_BYTES),
-        cost_estimate=pl.CostEstimate(flops=weighs, bytes_accessed=1 << 20, transcendentals=0),
         name=kernel.__name__,
     )(*operands)
 
 
 def rebuild_and_attend(
-    near, far, resident, resident_valid, queries, kept, wanted, rebuilt, attended
+    arrived, resident, resident_valid, queries, kept, wanted, rebuilt, attended
 ):
-    plane, context, lanes = near.shape
-    slots = 2 * plane
+    plane, context, lanes = arrived.shape
+    slots, context = 2 * plane, context // 2
     steps, batch, width = queries.shape
     rows = slots * context
     fresh = kept[kept.shape[0] - steps * batch :, :]
     columns = rebuilt.shape[1]
     held = resident.shape[1]
     heads = width // HD
-    blocks = jnp.concatenate([near[...], far[...]], axis=0).reshape(rows, lanes)
+    blocks = arrived[...].reshape(rows, lanes)
     half = half_of(lax.axis_index("inst"))
 
     def instance_of(slot):
-        place = slot % plane
-        there = jnp.where(slot < plane, half, 1 - half)
+        place = slot >> 1
+        there = jnp.where(slot % 2 == 0, half, 1 - half)
         return (place >> 1) * 4 + there * 2 + (place & 1)
 
     valid = blocks[:, :TILE].astype(F32) < ABSENT / 2
@@ -397,16 +397,16 @@
             attended[s, :, h * HD : (h + 1) * HD] = out[start : start + batch]
 
 
-def rebuild(near, far, resident, resident_valid, queries, kept, wanted, columns):
+def rebuild(arrived, resident, resident_valid, queries, kept, wanted, columns):
     return pl.pallas_call(
         rebuild_and_attend,
         out_shape=[
-            jax.ShapeDtypeStruct((near.shape[2], columns), BF),
+            jax.ShapeDtypeStruct((arrived.shape[2], columns), BF),
             jax.ShapeDtypeStruct(queries.shape, BF),
         ],
         compiler_params=pltpu.CompilerParams(vmem_limit_bytes=VMEM_BYTES),
         name="rebuild_and_attend",
-    )(near, far, resident, resident_valid, queries, kept, wanted)
+    )(arrived, resident, resident_valid, queries, kept, wanted)
 
 
 def remaining_rows(hidden, gain, weight, codes, target_of, capacity, lanes):
@@ -505,21 +505,17 @@
     received = lax.ppermute(crossing_rows, ("inst", "tensor"), halves)
     blocks_type = jax.ShapeDtypeStruct((plane, context, owned), BF)
     vmem = pl.BlockSpec(memory_space=pltpu.VMEM)
-    staying = place(place_staying, blocks_type, vmem, 1 << 33, codes, kept, rest)
+    near = place(place_staying, blocks_type, vmem, codes, kept, rest)
+    both_type = jax.ShapeDtypeStruct((plane, 2 * context, owned), BF)
     most_type = jax.ShapeDtypeStruct((1,), jnp.int32)
-    crossing, most = place(
+    outgoing, most = place(
         place_crossing,
-        (blocks_type, most_type),
+        (both_type, most_type),
         (vmem, pl.BlockSpec(memory_space=pltpu.SMEM)),
-        1 << 36,
         received,
         codes,
-    )
-
-    def over_plane(rows):
-        return lax.all_to_all(
-            rows, "inst", split_axis=0, concat_axis=0, tiled=True, axis_index_groups=planes
-        )
+        near,
+    )
 
     def all_crossing():
         rows = jnp.concatenate([kept[:capacity], rest], axis=0)
@@ -528,12 +524,15 @@
         lane = jnp.arange(leaving, dtype=jnp.int32)[None, :]
         slot = jnp.arange(plane * context, dtype=jnp.int32)[:, None]
         route = (slot == notes[0:1]) & (lane < notes[1:2])
-        return routed(route.astype(F32), rows).reshape(crossing.shape)
-
-    near = over_plane(staying)
-    far = over_plane(lax.cond(most[0] > sent, all_crossing, lambda: crossing))
+        far = routed(route.astype(F32), rows).reshape(near.shape)
+        return jnp.concatenate([near, far], axis=1)
+
+    outgoing = lax.cond(most[0] > sent, all_crossing, lambda: outgoing)
+    arrived = lax.all_to_all(
+        outgoing, "inst", split_axis=0, concat_axis=0, tiled=True, axis_index_groups=planes
+    )
     return tuple(
-        rebuild(near, far, resident_cache, resident_valid, queries, kept, wanted, leaving)
+        rebuild(arrived, resident_cache, resident_valid, queries, kept, wanted, leaving)
     )
 
 

time: 102 us -> 98.6 us (0.967)
  the two profiles are of different devices: /device:TPU:129 before, /device:TPU:1 now
where the time goes in v8:
time: 98.6 us; the launch traced here: 98.2 us
  starting transfers between devices  59.5 us (60%)
  waiting for transfers between devices  25.1 us (25%)
  Pallas kernels  9.18 us (9%)
  between operations  2.26 us (2%)
  local copies, waits for them, and re-layouts  1.08 us (1%)
    ppermute x7, starting transfers between devices, ring_sums(): sums[way] = lax.ppermute(chunk, 'tensor', forward if way else backward)  28.4 us
    all_to_all x1, starting transfers between devices, shards(): lax.all_to_all(outgoing, 'inst', split_axis=0, concat_axis=0, tiled=True,...  22.2 us
    ppermute x7, waiting for transfers between devices, ring_sums(): sums[way] = lax.ppermute(chunk, 'tensor', forward if way else backward)  12.3 us
    all_to_all x1, waiting for transfers between devices, shards(): lax.all_to_all(outgoing, 'inst', split_axis=0, concat_axis=0, tiled=True,...  11.3 us
    ppermute x1, starting transfers between devices, shards(): received = lax.ppermute(crossing_rows, ('inst', 'tensor'), halves)  8.94 us
    pallas_call x1, Pallas kernels, project_chunks(): pl.pallas_call(functools.partial(first_chunks, pairs[0]), in_specs=[hbm]...  2.75 us
    pallas_call x1, Pallas kernels, rebuild(): pl.pallas_call(rebuild_and_attend, out_shape=[jax.ShapeDtypeStruct((arriv...  2.49 us
    pallas_call x2, Pallas kernels, project_chunks(): pl.pallas_call(functools.partial(later_chunks, group, capacity), in_specs...  2.35 us
  transfers between devices with their start and end apart: 9, of which 7 were waited for; matrix products, arithmetic and copies ran while one was open for 1% of the time, Pallas kernels for 3%

profile of v8, /device:TPU:1, one launch (start us, length us, event | category | flops | bytes accessed | tf_op | source)
XLA Modules:
  0.0 98.2 jit_solution(15402589499300191185)
XLA Ops:
  0.6 0.8 copy-done.1
  1.5 2.7 %first_chunks.1 = (bf16[416,256]{1,0:T(8,128)(2,1)S(1)}, bf16[416,256]{1,0:T(8,128)(2,1)S(1)}, bf16[400,1024]{1,0:T(8,128)(2,1)S(1)}, bf16[16,256]{1,0:T(8,128)(2,1)S(1)}, s32[8,512]{1,0:T(8,128)S(1)}) custom-call(s32[1,32]{1,0:T(1,128)} %bitcast.36, s32[1,32]{1,0:T(1,128)} %bitcast.35, f32[1,1024]{1,0:T(1,128)} %bitcast.30, bf16[32,1024]{1,0:T(8,128)(2,1)S(1)} %bitcast.28, ...), custom_call_target="tpu_custom_call" | custom-call | flops 419430400 | bytes 2277376 | tf_op jit(solution)/shard_map/first_chunks/pallas_call | solution.py:174
  4.2 5.7 %collective-permute-start.12 = (bf16[416,256]{1,0:T(8,128)(2,1)S(1)}, bf16[416,256]{1,0:T(8,128)(2,1)S(1)}, u32[]{:S(2)}, u32[]{:S(2)}) collective-permute-start(bf16[416,256]{1,0:T(8,128)(2,1)S(1)} %get-tuple-element.61), channel_id=1, source_target_pairs={{0,2},{2,4},{4,6},{6,7},{7,5},{5,3},{3,1},{1,0},{8,10},{10,12},{12... | collective-permute-start | bytes 638984 | tf_op jit(solution)/shard_map/ppermute | solution.py:234
  10.0 0.8 second_chunks.1
  10.8 2.1 %collective-permute-start.16 = (bf16[416,256]{1,0:T(8,128)(2,1)S(1)}, bf16[416,256]{1,0:T(8,128)(2,1)S(1)}, u32[]{:S(2)}, u32[]{:S(2)}) collective-permute-start(bf16[416,256]{1,0:T(8,128)(2,1)S(1)} %get-tuple-element.67), channel_id=1, source_target_pairs={{2,0},{4,2},{6,4},{7,6},{5,7},{3,5},{1,3},{0,1},{10,8},{12,10},{14... | collective-permute-start | bytes 638984 | tf_op jit(solution)/shard_map/ppermute | solution.py:234
  12.9 1.6 %later_chunks.1 = (bf16[416,256]{1,0:T(8,128)(2,1)S(1)}, bf16[416,256]{1,0:T(8,128)(2,1)S(1)}, bf16[416,256]{1,0:T(8,128)(2,1)S(1)}, bf16[416,256]{1,0:T(8,128)(2,1)S(1)}) custom-call(bf16[400,1024]{1,0:T(8,128)(2,1)S(1)} %get-tuple-element.62.scaled, bf16[16,256]{1,0:T(8,128)(2,1)S(1)} %get-tuple-element.63.extra, s32[8,512]{1,0:T(8,128)S(1)} %get-tuple-element.60.codes, ...), custom_call_target="tpu_custom_call" | custom-call | flops 838860800 | bytes 3735552 | tf_op jit(solution)/shard_map/later_chunks/pallas_call | solution.py:194
  14.5 7.2 %collective-permute-start.13 = (bf16[416,256]{1,0:T(8,128)(2,1)S(1)}, bf16[416,256]{1,0:T(8,128)(2,1)S(1)}, u32[]{:S(2)}, u32[]{:S(2)}) collective-permute-start(bf16[416,256]{1,0:T(8,128)(2,1)S(1)} %add_convert_fusion.9), channel_id=1, source_target_pairs={{0,2},{2,4},{4,6},{6,7},{7,5},{5,3},{3,1},{1,0},{8,10},{10,12},{12... | collective-permute-start | bytes 638984 | tf_op jit(solution)/shard_map/ppermute | solution.py:234
  21.8 1.9 %collective-permute-start.17 = (bf16[416,256]{1,0:T(8,128)(2,1)S(1)}, bf16[416,256]{1,0:T(8,128)(2,1)S(1)}, u32[]{:S(2)}, u32[]{:S(2)}) collective-permute-start(bf16[416,256]{1,0:T(8,128)(2,1)S(1)} %add_convert_fusion.6), channel_id=1, source_target_pairs={{2,0},{4,2},{6,4},{7,6},{5,7},{3,5},{1,3},{0,1},{10,8},{12,10},{14... | collective-permute-start | bytes 638984 | tf_op jit(solution)/shard_map/ppermute | solution.py:234
  23.7 1.3 %collective-permute-done.13 = bf16[416,256]{1,0:T(8,128)(2,1)S(1)} collective-permute-done((bf16[416,256]{1,0:T(8,128)(2,1)S(1)}, bf16[416,256]{1,0:T(8,128)(2,1)S(1)}, u32[]{:S(2)}, u32[]{:S(2)}) %collective-permute-start.13) | collective-permute-done | bytes 213024 | tf_op jit(solution)/shard_map/ppermute | solution.py:234
  25.1 6.7 %collective-permute-start.14 = (bf16[416,256]{1,0:T(8,128)(2,1)S(1)}, bf16[416,256]{1,0:T(8,128)(2,1)S(1)}, u32[]{:S(2)}, u32[]{:S(2)}) collective-permute-start(bf16[416,256]{1,0:T(8,128)(2,1)S(1)} %add_convert_fusion.8), channel_id=1, source_target_pairs={{0,2},{2,4},{4,6},{6,7},{7,5},{5,3},{3,1},{1,0},{8,10},{10,12},{12... | collective-permute-start | bytes 638984 | tf_op jit(solution)/shard_map/ppermute | solution.py:234
  31.8 1.0 %collective-permute-done.17 = bf16[416,256]{1,0:T(8,128)(2,1)S(1)} collective-permute-done((bf16[416,256]{1,0:T(8,128)(2,1)S(1)}, bf16[416,256]{1,0:T(8,128)(2,1)S(1)}, u32[]{:S(2)}, u32[]{:S(2)}) %collective-permute-start.17) | collective-permute-done | bytes 213024 | tf_op jit(solution)/shard_map/ppermute | solution.py:234
  32.9 2.9 %collective-permute-start.18 = (bf16[416,256]{1,0:T(8,128)(2,1)S(1)}, bf16[416,256]{1,0:T(8,128)(2,1)S(1)}, u32[]{:S(2)}, u32[]{:S(2)}) collective-permute-start(bf16[416,256]{1,0:T(8,128)(2,1)S(1)} %add_convert_fusion.5), channel_id=1, source_target_pairs={{2,0},{4,2},{6,4},{7,6},{5,7},{3,5},{1,3},{0,1},{10,8},{12,10},{14... | collective-permute-start | bytes 638984 | tf_op jit(solution)/shard_map/ppermute | solution.py:234
  35.8 5.3 %collective-permute-done.14 = bf16[416,256]{1,0:T(8,128)(2,1)S(1)} collective-permute-done((bf16[416,256]{1,0:T(8,128)(2,1)S(1)}, bf16[416,256]{1,0:T(8,128)(2,1)S(1)}, u32[]{:S(2)}, u32[]{:S(2)}) %collective-permute-start.14) | collective-permute-done | bytes 213024 | tf_op jit(solution)/shard_map/ppermute | solution.py:234
  41.1 1.9 %collective-permute-start.15 = (bf16[416,256]{1,0:T(8,128)(2,1)S(1)}, bf16[416,256]{1,0:T(8,128)(2,1)S(1)}, u32[]{:S(2)}, u32[]{:S(2)}) collective-permute-start(bf16[416,256]{1,0:T(8,128)(2,1)S(1)} %add_convert_fusion.7), channel_id=1, source_target_pairs={{0,2},{2,4},{4,6},{6,7},{7,5},{5,3},{3,1},{1,0},{8,10},{10,12},{12... | collective-permute-start | bytes 638984 | tf_op jit(solution)/shard_map/ppermute | solution.py:234
  43.0 0.8 collective-permute-done.18.behind
  43.9 3.8 %collective-permute-done.15.ahead = bf16[416,256]{1,0:T(8,128)(2,1)S(1)} collective-permute-done((bf16[416,256]{1,0:T(8,128)(2,1)S(1)}, bf16[416,256]{1,0:T(8,128)(2,1)S(1)}, u32[]{:S(2)}, u32[]{:S(2)}) %collective-permute-start.15) | collective-permute-done | bytes 213024 | tf_op jit(solution)/shard_map/ppermute | solution.py:234
  47.9 8.9 %collective-permute-start.19 = (bf16[256,256]{1,0:T(8,128)(2,1)S(1)}, bf16[256,256]{1,0:T(8,128)(2,1)S(1)}, u32[]{:S(2)}, u32[]{:S(2)}) collective-permute-start(bf16[256,256]{1,0:T(8,128)(2,1)S(1)} %get-tuple-element.71), channel_id=1, source_target_pairs={{0,23},{1,22},{2,21},{3,20},{4,19},{5,18},{6,17},{7,16},{8,31},{9,... | collective-permute-start | bytes 393224 | tf_op jit(solution)/shard_map/ppermute | solution.py:505
  56.8 0.6 reduce_sum.36
  58.2 0.4 place_staying.1.near
  58.6 1.5 %collective-permute-done.19.received = bf16[256,256]{1,0:T(8,128)(2,1)S(1)} collective-permute-done((bf16[256,256]{1,0:T(8,128)(2,1)S(1)}, bf16[256,256]{1,0:T(8,128)(2,1)S(1)}, u32[]{:S(2)}, u32[]{:S(2)}) %collective-permute-start.19) | collective-permute-done | bytes 131104 | tf_op jit(solution)/shard_map/ppermute | solution.py:505
  60.1 1.1 %place_crossing.1 = (bf16[32,32,256]{2,1,0:T(8,128)(2,1)}, s32[1]{0:T(128)}) custom-call(bf16[256,256]{1,0:T(8,128)(2,1)S(1)} %collective-permute-done.19.received, s32[8,512]{1,0:T(8,128)S(1)} %get-tuple-element.60.codes, bf16[32,16,256]{2,1,0:T(8,128)(2,1)S(1)} %place_staying.1.near), custom_call_target="tpu_custom_call" | custom-call | tf_op jit(solution)/shard_map/place_crossing/pallas_call | solution.py:307
  61.8 22.2 %all-to-all-start = ((bf16[32,32,256]{2,1,0:T(8,128)(2,1)}), bf16[32,32,256]{2,1,0:T(8,128)(2,1)S(1)}, u32[]{:S(2)}, u32[]{:S(2)}) async-start(bf16[32,32,256]{2,1,0:T(8,128)(2,1)} %get-tuple-element.93), calls=%async_computation | async-start | bytes 1048576 | tf_op jit(solution)/shard_map/all_to_all | solution.py:531
  84.3 11.3 %all-to-all-done.arrived = bf16[32,32,256]{2,1,0:T(8,128)(2,1)S(1)} async-done(((bf16[32,32,256]{2,1,0:T(8,128)(2,1)}), bf16[32,32,256]{2,1,0:T(8,128)(2,1)S(1)}, u32[]{:S(2)}, u32[]{:S(2)}) %all-to-all-start) | async-done | bytes 524320 | tf_op jit(solution)/shard_map/all_to_all | solution.py:531
  95.7 2.5 %rebuild_and_attend.1 = (bf16[256,512]{1,0:T(8,128)(2,1)}, bf16[2,16,1024]{2,1,0:T(8,128)(2,1)}) custom-call(bf16[32,32,256]{2,1,0:T(8,128)(2,1)S(1)} %all-to-all-done.arrived, bf16[256,256]{1,0:T(8,128)(2,1)S(1)} %copy-done, s32[1,256]{1,0:T(1,128)S(1)} %reshape.161.resident_valid, bf16[2,16,1024]{2,1,0:T(8,128)(2,1)S(1)} %copy-done.2, ...), custom_call_target="tpu_custom_call" | custom-call | tf_op jit(solution)/shard_map/rebuild_and_attend/pallas_call | solution.py:401
  (34 shorter events, 0.8 us)
Async XLA Ops:
  0.6 0.8 copy-start.1
  1.5 8.5 %copy-start.3 = (bf16[1024,2048]{1,0:T(8,128)(2,1)S(1)}, bf16[1024,2048]{1,0:T(8,128)(2,1)}, u32[]{:S(2)}) copy-start(bf16[1024,2048]{1,0:T(8,128)(2,1)} %weight.3) | copy-start | bytes 12582916
  4.2 10.2 %collective-permute-start.12 = (bf16[416,256]{1,0:T(8,128)(2,1)S(1)}, bf16[416,256]{1,0:T(8,128)(2,1)S(1)}, u32[]{:S(2)}, u32[]{:S(2)}) collective-permute-start(bf16[416,256]{1,0:T(8,128)(2,1)S(1)} %get-tuple-element.61), channel_id=1, source_target_pairs={{0,2},{2,4},{4,6},{6,7},{7,5},{5,3},{3,1},{1,0},{8,10},{10,12},{12... | collective-permute-start | bytes 638984 | tf_op jit(solution)/shard_map/ppermute | solution.py:234
  10.8 46.0 %copy-start.6 = (s32[32]{0:T(128)S(1)}, s32[32]{0:T(128)}, u32[]{:S(2)}) copy-start(s32[32]{0:T(128)} %param.22) | copy-start | bytes 388
  10.8 47.3 %copy-start.4 = (bf16[512,1024]{1,0:T(8,128)(2,1)S(1)}, bf16[512,1024]{1,0:T(8,128)(2,1)}, u32[]{:S(2)}) copy-start(bf16[512,1024]{1,0:T(8,128)(2,1)} %refs_4_.1) | copy-start | bytes 3145732
  10.8 47.3 %copy-start.5 = (f32[1024]{0:T(1024)S(1)}, f32[1024]{0:T(1024)}, u32[]{:S(2)}) copy-start(f32[1024]{0:T(1024)} %param.17) | copy-start | bytes 12292
  10.8 47.3 %copy-start.7 = (s32[32]{0:T(128)S(1)}, s32[32]{0:T(128)}, u32[]{:S(2)}) copy-start(s32[32]{0:T(128)} %param.21) | copy-start | bytes 388
  10.8 10.9 %collective-permute-start.16 = (bf16[416,256]{1,0:T(8,128)(2,1)S(1)}, bf16[416,256]{1,0:T(8,128)(2,1)S(1)}, u32[]{:S(2)}, u32[]{:S(2)}) collective-permute-start(bf16[416,256]{1,0:T(8,128)(2,1)S(1)} %get-tuple-element.67), channel_id=1, source_target_pairs={{2,0},{4,2},{6,4},{7,6},{5,7},{3,5},{1,3},{0,1},{10,8},{12,10},{14... | collective-permute-start | bytes 638984 | tf_op jit(solution)/shard_map/ppermute | solution.py:234
  14.5 10.5 %collective-permute-start.13 = (bf16[416,256]{1,0:T(8,128)(2,1)S(1)}, bf16[416,256]{1,0:T(8,128)(2,1)S(1)}, u32[]{:S(2)}, u32[]{:S(2)}) collective-permute-start(bf16[416,256]{1,0:T(8,128)(2,1)S(1)} %add_convert_fusion.9), channel_id=1, source_target_pairs={{0,2},{2,4},{4,6},{6,7},{7,5},{5,3},{3,1},{1,0},{8,10},{10,12},{12... | collective-permute-start | bytes 638984 | tf_op jit(solution)/shard_map/ppermute | solution.py:234
  21.8 11.0 %collective-permute-start.17 = (bf16[416,256]{1,0:T(8,128)(2,1)S(1)}, bf16[416,256]{1,0:T(8,128)(2,1)S(1)}, u32[]{:S(2)}, u32[]{:S(2)}) collective-permute-start(bf16[416,256]{1,0:T(8,128)(2,1)S(1)} %add_convert_fusion.6), channel_id=1, source_target_pairs={{2,0},{4,2},{6,4},{7,6},{5,7},{3,5},{1,3},{0,1},{10,8},{12,10},{14... | collective-permute-start | bytes 638984 | tf_op jit(solution)/shard_map/ppermute | solution.py:234
  25.1 16.0 %collective-permute-start.14 = (bf16[416,256]{1,0:T(8,128)(2,1)S(1)}, bf16[416,256]{1,0:T(8,128)(2,1)S(1)}, u32[]{:S(2)}, u32[]{:S(2)}) collective-permute-start(bf16[416,256]{1,0:T(8,128)(2,1)S(1)} %add_convert_fusion.8), channel_id=1, source_target_pairs={{0,2},{2,4},{4,6},{6,7},{7,5},{5,3},{3,1},{1,0},{8,10},{10,12},{12... | collective-permute-start | bytes 638984 | tf_op jit(solution)/shard_map/ppermute | solution.py:234
  32.9 11.0 %collective-permute-start.18 = (bf16[416,256]{1,0:T(8,128)(2,1)S(1)}, bf16[416,256]{1,0:T(8,128)(2,1)S(1)}, u32[]{:S(2)}, u32[]{:S(2)}) collective-permute-start(bf16[416,256]{1,0:T(8,128)(2,1)S(1)} %add_convert_fusion.5), channel_id=1, source_target_pairs={{2,0},{4,2},{6,4},{7,6},{5,7},{3,5},{1,3},{0,1},{10,8},{12,10},{14... | collective-permute-start | bytes 638984 | tf_op jit(solution)/shard_map/ppermute | solution.py:234
  41.1 6.6 %collective-permute-start.15 = (bf16[416,256]{1,0:T(8,128)(2,1)S(1)}, bf16[416,256]{1,0:T(8,128)(2,1)S(1)}, u32[]{:S(2)}, u32[]{:S(2)}) collective-permute-start(bf16[416,256]{1,0:T(8,128)(2,1)S(1)} %add_convert_fusion.7), channel_id=1, source_target_pairs={{0,2},{2,4},{4,6},{6,7},{7,5},{5,3},{3,1},{1,0},{8,10},{10,12},{12... | collective-permute-start | bytes 638984 | tf_op jit(solution)/shard_map/ppermute | solution.py:234
  47.9 12.2 %collective-permute-start.19 = (bf16[256,256]{1,0:T(8,128)(2,1)S(1)}, bf16[256,256]{1,0:T(8,128)(2,1)S(1)}, u32[]{:S(2)}, u32[]{:S(2)}) collective-permute-start(bf16[256,256]{1,0:T(8,128)(2,1)S(1)} %get-tuple-element.71), channel_id=1, source_target_pairs={{0,23},{1,22},{2,21},{3,20},{4,19},{5,18},{6,17},{7,16},{8,31},{9,... | collective-permute-start | bytes 393224 | tf_op jit(solution)/shard_map/ppermute | solution.py:505
  58.2 25.9 %copy-start.8 = (s32[16]{0:T(128)S(1)}, s32[16]{0:T(128)}, u32[]{:S(2)}) copy-start(s32[16]{0:T(128)} %param.24) | copy-start | bytes 196
  58.2 26.0 %copy-start.9 = (s32[16]{0:T(128)S(1)}, s32[16]{0:T(128)}, u32[]{:S(2)}) copy-start(s32[16]{0:T(128)} %param.23) | copy-start | bytes 196
  58.2 37.5 %copy-start = (bf16[256,256]{1,0:T(8,128)(2,1)S(1)}, bf16[256,256]{1,0:T(8,128)(2,1)}, u32[]{:S(2)}) copy-start(bf16[256,256]{1,0:T(8,128)(2,1)} %resident.1) | copy-start | bytes 393220
  58.2 37.5 %copy-start.2 = (bf16[2,16,1024]{2,1,0:T(8,128)(2,1)S(1)}, bf16[2,16,1024]{2,1,0:T(8,128)(2,1)}, u32[]{:S(2)}) copy-start(bf16[2,16,1024]{2,1,0:T(8,128)(2,1)} %queries.1) | copy-start | bytes 196612
  61.8 33.8 %all-to-all-start = ((bf16[32,32,256]{2,1,0:T(8,128)(2,1)}), bf16[32,32,256]{2,1,0:T(8,128)(2,1)S(1)}, u32[]{:S(2)}, u32[]{:S(2)}) async-start(bf16[32,32,256]{2,1,0:T(8,128)(2,1)} %get-tuple-element.93), calls=%async_computation | async-start | bytes 1048576 | tf_op jit(solution)/shard_map/all_to_all | solution.py:531

commit v9 on v8

--- a/solution.py
+++ b/solution.py
@@ -37,6 +37,10 @@
     return (instance >> 2) * 2 + (instance & 1)
 
 
+def core_of(instance):
+    return instance & 1
+
+
 def half_of(instance):
     return (instance >> 1) & 1
 
@@ -45,7 +49,8 @@
     tensors, lanes = lax.axis_size("tensor"), blocks.shape[2]
     me = lax.axis_index("tensor")
     at = jnp.where(me % 2 == 0, me // 2, tensors - 1 - me // 2)
-    at = (at + offset + tensors) % tensors
+    sense = 1 - 2 * core_of(lax.axis_index("inst"))
+    at = (at + sense * offset + tensors) % tensors
     owner = jnp.where(at < (tensors + 1) // 2, 2 * at, 2 * (tensors - at) - 1)
     columns = pl.ds(pl.multiple_of(owner * lanes, lanes), lanes)
     return pltpu.make_async_copy(weight.at[:, columns], blocks.at[place], sems.at[place])
@@ -214,24 +219,29 @@
 
 def ring_order(tensors):
     ring = ring_of(tensors)
-    table = [
-        [ring[(ring.index(device) + offset) % tensors] for offset in ring_offsets(tensors)]
-        for device in range(tensors)
-    ]
-    return jnp.array(table, jnp.int32)[lax.axis_index("tensor")]
+    offsets = jnp.array(ring_offsets(tensors), jnp.int32)
+    at = jnp.array([ring.index(i) for i in range(tensors)], jnp.int32)[lax.axis_index("tensor")]
+    sense = 1 - 2 * core_of(lax.axis_index("inst"))
+    return jnp.array(ring, jnp.int32)[(at + sense * offsets + tensors) % tensors]
 
 
 def ring_sums(chunks):
     tensors = lax.axis_size("tensor")
     ring = ring_of(tensors)
-    forward = [(ring[i], ring[(i + 1) % tensors]) for i in range(tensors)]
-    backward = [(b, a) for a, b in forward]
+    links = [(ring[i], ring[(i + 1) % tensors]) for i in range(tensors)]
+    forward, backward = [], []
+    for instance in range(lax.axis_size("inst")):
+        ways = (forward, backward) if core_of(instance) == 0 else (backward, forward)
+        for a, b in links:
+            a, b = instance * tensors + a, instance * tensors + b
+            ways[0].append((a, b))
+            ways[1].append((b, a))
     sums = {True: None, False: None}
     for offset, chunk in zip(ring_offsets(tensors), chunks[:-1]):
         way = offset > 0
         if sums[way] is not None:
             chunk = (sums[way].astype(F32) + chunk.astype(F32)).astype(BF)
-        sums[way] = lax.ppermute(chunk, "tensor", forward if way else backward)
+        sums[way] = lax.ppermute(chunk, ("inst", "tensor"), forward if way else backward)
     return sums[True], sums[False], chunks[-1]
 
 

time: 98.6 us -> 97.3 us (0.987)
  the two profiles are of different devices: /device:TPU:1 before, /device:TPU:129 now
where the time goes in v9:
time: 97.3 us; the launch traced here: 96.8 us
  starting transfers between devices  48.9 us (50%)
  waiting for transfers between devices  34.4 us (35%)
  Pallas kernels  9.19 us (9%)
  between operations  2.25 us (2%)
  local copies, waits for them, and re-layouts  1.08 us (1%)
    ppermute x7, starting transfers between devices, ring_sums(): lax.ppermute(chunk, ('inst', 'tensor'), forward if way else backward)  25 us
    ppermute x7, waiting for transfers between devices, ring_sums(): lax.ppermute(chunk, ('inst', 'tensor'), forward if way else backward)  18.3 us
    all_to_all x1, starting transfers between devices, shards(): lax.all_to_all(outgoing, 'inst', split_axis=0, concat_axis=0, tiled=True,...  17.7 us
    all_to_all x1, waiting for transfers between devices, shards(): lax.all_to_all(outgoing, 'inst', split_axis=0, concat_axis=0, tiled=True,...  11.3 us
    ppermute x1, starting transfers between devices, shards(): received = lax.ppermute(crossing_rows, ('inst', 'tensor'), halves)  6.19 us
    ppermute x1, waiting for transfers between devices, shards(): received = lax.ppermute(crossing_rows, ('inst', 'tensor'), halves)  4.74 us
    pallas_call x1, Pallas kernels, project_chunks(): pl.pallas_call(functools.partial(first_chunks, pairs[0]), in_specs=[hbm]...  2.75 us
    pallas_call x1, Pallas kernels, rebuild(): pl.pallas_call(rebuild_and_attend, out_shape=[jax.ShapeDtypeStruct((arriv...  2.49 us
  transfers between devices with their start and end apart: 9, of which 8 were waited for; matrix products, arithmetic and copies ran while one was open for 1% of the time, Pallas kernels for 3%

profile of v9, /device:TPU:129, one launch (start us, length us, event | category | flops | bytes accessed | tf_op | source)
XLA Modules:
  0.0 96.8 jit_solution(5888266532655392690)
XLA Ops:
  0.6 0.8 copy-done.1
  1.5 2.7 %first_chunks.1 = (bf16[416,256]{1,0:T(8,128)(2,1)S(1)}, bf16[416,256]{1,0:T(8,128)(2,1)S(1)}, bf16[400,1024]{1,0:T(8,128)(2,1)S(1)}, bf16[16,256]{1,0:T(8,128)(2,1)S(1)}, s32[8,512]{1,0:T(8,128)S(1)}) custom-call(s32[1,32]{1,0:T(1,128)} %bitcast.37, s32[1,32]{1,0:T(1,128)} %bitcast.36, f32[1,1024]{1,0:T(1,128)} %bitcast.31, bf16[32,1024]{1,0:T(8,128)(2,1)S(1)} %bitcast.29, ...), custom_call_target="tpu_custom_call" | custom-call | flops 419430400 | bytes 2277376 | tf_op jit(solution)/shard_map/first_chunks/pallas_call | solution.py:179
  4.2 1.9 %collective-permute-start.12 = (bf16[416,256]{1,0:T(8,128)(2,1)S(1)}, bf16[416,256]{1,0:T(8,128)(2,1)S(1)}, u32[]{:S(2)}, u32[]{:S(2)}) collective-permute-start(bf16[416,256]{1,0:T(8,128)(2,1)S(1)} %get-tuple-element.67), channel_id=1, source_target_pairs={{0,2},{2,4},{4,6},{6,7},{7,5},{5,3},{3,1},{1,0},{10,8},{12,10},{14... | collective-permute-start | bytes 638984 | tf_op jit(solution)/shard_map/ppermute | solution.py:244
  6.2 0.8 second_chunks.1
  7.0 5.0 %collective-permute-start.16 = (bf16[416,256]{1,0:T(8,128)(2,1)S(1)}, bf16[416,256]{1,0:T(8,128)(2,1)S(1)}, u32[]{:S(2)}, u32[]{:S(2)}) collective-permute-start(bf16[416,256]{1,0:T(8,128)(2,1)S(1)} %get-tuple-element.73), channel_id=1, source_target_pairs={{2,0},{4,2},{6,4},{7,6},{5,7},{3,5},{1,3},{0,1},{8,10},{10,12},{12... | collective-permute-start | bytes 638984 | tf_op jit(solution)/shard_map/ppermute | solution.py:244
  12.1 1.6 %later_chunks.1 = (bf16[416,256]{1,0:T(8,128)(2,1)S(1)}, bf16[416,256]{1,0:T(8,128)(2,1)S(1)}, bf16[416,256]{1,0:T(8,128)(2,1)S(1)}, bf16[416,256]{1,0:T(8,128)(2,1)S(1)}) custom-call(bf16[400,1024]{1,0:T(8,128)(2,1)S(1)} %get-tuple-element.68.scaled, bf16[16,256]{1,0:T(8,128)(2,1)S(1)} %get-tuple-element.69.extra, s32[8,512]{1,0:T(8,128)S(1)} %get-tuple-element.66.codes, ...), custom_call_target="tpu_custom_call" | custom-call | flops 838860800 | bytes 3735552 | tf_op jit(solution)/shard_map/later_chunks/pallas_call | solution.py:199
  13.7 2.5 %collective-permute-start.13 = (bf16[416,256]{1,0:T(8,128)(2,1)S(1)}, bf16[416,256]{1,0:T(8,128)(2,1)S(1)}, u32[]{:S(2)}, u32[]{:S(2)}) collective-permute-start(bf16[416,256]{1,0:T(8,128)(2,1)S(1)} %add_convert_fusion.9), channel_id=1, source_target_pairs={{0,2},{2,4},{4,6},{6,7},{7,5},{5,3},{3,1},{1,0},{10,8},{12,10},{14... | collective-permute-start | bytes 638984 | tf_op jit(solution)/shard_map/ppermute | solution.py:244
  16.2 2.6 %collective-permute-done.16 = bf16[416,256]{1,0:T(8,128)(2,1)S(1)} collective-permute-done((bf16[416,256]{1,0:T(8,128)(2,1)S(1)}, bf16[416,256]{1,0:T(8,128)(2,1)S(1)}, u32[]{:S(2)}, u32[]{:S(2)}) %collective-permute-start.16) | collective-permute-done | bytes 213024 | tf_op jit(solution)/shard_map/ppermute | solution.py:244
  18.8 5.5 %collective-permute-start.17 = (bf16[416,256]{1,0:T(8,128)(2,1)S(1)}, bf16[416,256]{1,0:T(8,128)(2,1)S(1)}, u32[]{:S(2)}, u32[]{:S(2)}) collective-permute-start(bf16[416,256]{1,0:T(8,128)(2,1)S(1)} %add_convert_fusion.6), channel_id=1, source_target_pairs={{2,0},{4,2},{6,4},{7,6},{5,7},{3,5},{1,3},{0,1},{8,10},{10,12},{12... | collective-permute-start | bytes 638984 | tf_op jit(solution)/shard_map/ppermute | solution.py:244
  24.3 1.5 %collective-permute-done.13 = bf16[416,256]{1,0:T(8,128)(2,1)S(1)} collective-permute-done((bf16[416,256]{1,0:T(8,128)(2,1)S(1)}, bf16[416,256]{1,0:T(8,128)(2,1)S(1)}, u32[]{:S(2)}, u32[]{:S(2)}) %collective-permute-start.13) | collective-permute-done | bytes 213024 | tf_op jit(solution)/shard_map/ppermute | solution.py:244
  25.9 1.9 %collective-permute-start.14 = (bf16[416,256]{1,0:T(8,128)(2,1)S(1)}, bf16[416,256]{1,0:T(8,128)(2,1)S(1)}, u32[]{:S(2)}, u32[]{:S(2)}) collective-permute-start(bf16[416,256]{1,0:T(8,128)(2,1)S(1)} %add_convert_fusion.8), channel_id=1, source_target_pairs={{0,2},{2,4},{4,6},{6,7},{7,5},{5,3},{3,1},{1,0},{10,8},{12,10},{14... | collective-permute-start | bytes 638984 | tf_op jit(solution)/shard_map/ppermute | solution.py:244
  27.8 4.3 %collective-permute-done.17 = bf16[416,256]{1,0:T(8,128)(2,1)S(1)} collective-permute-done((bf16[416,256]{1,0:T(8,128)(2,1)S(1)}, bf16[416,256]{1,0:T(8,128)(2,1)S(1)}, u32[]{:S(2)}, u32[]{:S(2)}) %collective-permute-start.17) | collective-permute-done | bytes 213024 | tf_op jit(solution)/shard_map/ppermute | solution.py:244
  32.2 4.3 %collective-permute-start.18 = (bf16[416,256]{1,0:T(8,128)(2,1)S(1)}, bf16[416,256]{1,0:T(8,128)(2,1)S(1)}, u32[]{:S(2)}, u32[]{:S(2)}) collective-permute-start(bf16[416,256]{1,0:T(8,128)(2,1)S(1)} %add_convert_fusion.5), channel_id=1, source_target_pairs={{2,0},{4,2},{6,4},{7,6},{5,7},{3,5},{1,3},{0,1},{8,10},{10,12},{12... | collective-permute-start | bytes 638984 | tf_op jit(solution)/shard_map/ppermute | solution.py:244
  36.5 2.4 %collective-permute-done.14 = bf16[416,256]{1,0:T(8,128)(2,1)S(1)} collective-permute-done((bf16[416,256]{1,0:T(8,128)(2,1)S(1)}, bf16[416,256]{1,0:T(8,128)(2,1)S(1)}, u32[]{:S(2)}, u32[]{:S(2)}) %collective-permute-start.14) | collective-permute-done | bytes 213024 | tf_op jit(solution)/shard_map/ppermute | solution.py:244
  38.9 3.9 %collective-permute-start.15 = (bf16[416,256]{1,0:T(8,128)(2,1)S(1)}, bf16[416,256]{1,0:T(8,128)(2,1)S(1)}, u32[]{:S(2)}, u32[]{:S(2)}) collective-permute-start(bf16[416,256]{1,0:T(8,128)(2,1)S(1)} %add_convert_fusion.7), channel_id=1, source_target_pairs={{0,2},{2,4},{4,6},{6,7},{7,5},{5,3},{3,1},{1,0},{10,8},{12,10},{14... | collective-permute-start | bytes 638984 | tf_op jit(solution)/shard_map/ppermute | solution.py:244
  42.8 1.8 %collective-permute-done.18.behind = bf16[416,256]{1,0:T(8,128)(2,1)S(1)} collective-permute-done((bf16[416,256]{1,0:T(8,128)(2,1)S(1)}, bf16[416,256]{1,0:T(8,128)(2,1)S(1)}, u32[]{:S(2)}, u32[]{:S(2)}) %collective-permute-start.18) | collective-permute-done | bytes 213024 | tf_op jit(solution)/shard_map/ppermute | solution.py:244
  44.5 5.8 %collective-permute-done.15.ahead = bf16[416,256]{1,0:T(8,128)(2,1)S(1)} collective-permute-done((bf16[416,256]{1,0:T(8,128)(2,1)S(1)}, bf16[416,256]{1,0:T(8,128)(2,1)S(1)}, u32[]{:S(2)}, u32[]{:S(2)}) %collective-permute-start.15) | collective-permute-done | bytes 213024 | tf_op jit(solution)/shard_map/ppermute | solution.py:244
  50.5 6.2 %collective-permute-start.19 = (bf16[256,256]{1,0:T(8,128)(2,1)S(1)}, bf16[256,256]{1,0:T(8,128)(2,1)S(1)}, u32[]{:S(2)}, u32[]{:S(2)}) collective-permute-start(bf16[256,256]{1,0:T(8,128)(2,1)S(1)} %get-tuple-element.77), channel_id=1, source_target_pairs={{0,23},{1,22},{2,21},{3,20},{4,19},{5,18},{6,17},{7,16},{8,31},{9,... | collective-permute-start | bytes 393224 | tf_op jit(solution)/shard_map/ppermute | solution.py:515
  56.7 0.6 reduce_sum.36
  58.5 4.7 %collective-permute-done.19.received = bf16[256,256]{1,0:T(8,128)(2,1)S(1)} collective-permute-done((bf16[256,256]{1,0:T(8,128)(2,1)S(1)}, bf16[256,256]{1,0:T(8,128)(2,1)S(1)}, u32[]{:S(2)}, u32[]{:S(2)}) %collective-permute-start.19) | collective-permute-done | bytes 131104 | tf_op jit(solution)/shard_map/ppermute | solution.py:515
  63.2 1.1 %place_crossing.1 = (bf16[32,32,256]{2,1,0:T(8,128)(2,1)}, s32[1]{0:T(128)}) custom-call(bf16[256,256]{1,0:T(8,128)(2,1)S(1)} %collective-permute-done.19.received, s32[8,512]{1,0:T(8,128)S(1)} %get-tuple-element.66.codes, bf16[32,16,256]{2,1,0:T(8,128)(2,1)S(1)} %place_staying.1.near), custom_call_target="tpu_custom_call" | custom-call | tf_op jit(solution)/shard_map/place_crossing/pallas_call | solution.py:317
  65.0 17.7 %all-to-all-start = ((bf16[32,32,256]{2,1,0:T(8,128)(2,1)}), bf16[32,32,256]{2,1,0:T(8,128)(2,1)S(1)}, u32[]{:S(2)}, u32[]{:S(2)}) async-start(bf16[32,32,256]{2,1,0:T(8,128)(2,1)} %get-tuple-element.103), calls=%async_computation | async-start | bytes 1048576 | tf_op jit(solution)/shard_map/all_to_all | solution.py:541
  83.0 11.3 %all-to-all-done.arrived = bf16[32,32,256]{2,1,0:T(8,128)(2,1)S(1)} async-done(((bf16[32,32,256]{2,1,0:T(8,128)(2,1)}), bf16[32,32,256]{2,1,0:T(8,128)(2,1)S(1)}, u32[]{:S(2)}, u32[]{:S(2)}) %all-to-all-start) | async-done | bytes 524320 | tf_op jit(solution)/shard_map/all_to_all | solution.py:541
  94.3 2.5 %rebuild_and_attend.1 = (bf16[256,512]{1,0:T(8,128)(2,1)}, bf16[2,16,1024]{2,1,0:T(8,128)(2,1)}) custom-call(bf16[32,32,256]{2,1,0:T(8,128)(2,1)S(1)} %all-to-all-done.arrived, bf16[256,256]{1,0:T(8,128)(2,1)S(1)} %copy-done, s32[1,256]{1,0:T(1,128)S(1)} %reshape.145.resident_valid, bf16[2,16,1024]{2,1,0:T(8,128)(2,1)S(1)} %copy-done.2, ...), custom_call_target="tpu_custom_call" | custom-call | tf_op jit(solution)/shard_map/rebuild_and_attend/pallas_call | solution.py:411
  (34 shorter events, 1.1 us)
Async XLA Ops:
  0.6 0.8 copy-start.1
  1.5 4.7 %copy-start.3 = (bf16[1024,2048]{1,0:T(8,128)(2,1)S(1)}, bf16[1024,2048]{1,0:T(8,128)(2,1)}, u32[]{:S(2)}) copy-start(bf16[1024,2048]{1,0:T(8,128)(2,1)} %weight.3) | copy-start | bytes 12582916
  4.2 9.4 %collective-permute-start.12 = (bf16[416,256]{1,0:T(8,128)(2,1)S(1)}, bf16[416,256]{1,0:T(8,128)(2,1)S(1)}, u32[]{:S(2)}, u32[]{:S(2)}) collective-permute-start(bf16[416,256]{1,0:T(8,128)(2,1)S(1)} %get-tuple-element.67), channel_id=1, source_target_pairs={{0,2},{2,4},{4,6},{6,7},{7,5},{5,3},{3,1},{1,0},{10,8},{12,10},{14... | collective-permute-start | bytes 638984 | tf_op jit(solution)/shard_map/ppermute | solution.py:244
  7.0 49.8 %copy-start.6 = (s32[32]{0:T(128)S(1)}, s32[32]{0:T(128)}, u32[]{:S(2)}) copy-start(s32[32]{0:T(128)} %param.24) | copy-start | bytes 388
  7.0 51.0 %copy-start.4 = (bf16[512,1024]{1,0:T(8,128)(2,1)S(1)}, bf16[512,1024]{1,0:T(8,128)(2,1)}, u32[]{:S(2)}) copy-start(bf16[512,1024]{1,0:T(8,128)(2,1)} %refs_4_.1) | copy-start | bytes 3145732
  7.0 51.0 %copy-start.5 = (f32[1024]{0:T(1024)S(1)}, f32[1024]{0:T(1024)}, u32[]{:S(2)}) copy-start(f32[1024]{0:T(1024)} %param.19) | copy-start | bytes 12292
  7.0 51.0 %copy-start.7 = (s32[32]{0:T(128)S(1)}, s32[32]{0:T(128)}, u32[]{:S(2)}) copy-start(s32[32]{0:T(128)} %param.23) | copy-start | bytes 388
  7.0 11.8 %collective-permute-start.16 = (bf16[416,256]{1,0:T(8,128)(2,1)S(1)}, bf16[416,256]{1,0:T(8,128)(2,1)S(1)}, u32[]{:S(2)}, u32[]{:S(2)}) collective-permute-start(bf16[416,256]{1,0:T(8,128)(2,1)S(1)} %get-tuple-element.73), channel_id=1, source_target_pairs={{2,0},{4,2},{6,4},{7,6},{5,7},{3,5},{1,3},{0,1},{8,10},{10,12},{12... | collective-permute-start | bytes 638984 | tf_op jit(solution)/shard_map/ppermute | solution.py:244
  13.7 12.1 %collective-permute-start.13 = (bf16[416,256]{1,0:T(8,128)(2,1)S(1)}, bf16[416,256]{1,0:T(8,128)(2,1)S(1)}, u32[]{:S(2)}, u32[]{:S(2)}) collective-permute-start(bf16[416,256]{1,0:T(8,128)(2,1)S(1)} %add_convert_fusion.9), channel_id=1, source_target_pairs={{0,2},{2,4},{4,6},{6,7},{7,5},{5,3},{3,1},{1,0},{10,8},{12,10},{14... | collective-permute-start | bytes 638984 | tf_op jit(solution)/shard_map/ppermute | solution.py:244
  18.8 13.3 %collective-permute-start.17 = (bf16[416,256]{1,0:T(8,128)(2,1)S(1)}, bf16[416,256]{1,0:T(8,128)(2,1)S(1)}, u32[]{:S(2)}, u32[]{:S(2)}) collective-permute-start(bf16[416,256]{1,0:T(8,128)(2,1)S(1)} %add_convert_fusion.6), channel_id=1, source_target_pairs={{2,0},{4,2},{6,4},{7,6},{5,7},{3,5},{1,3},{0,1},{8,10},{10,12},{12... | collective-permute-start | bytes 638984 | tf_op jit(solution)/shard_map/ppermute | solution.py:244
  25.9 13.0 %collective-permute-start.14 = (bf16[416,256]{1,0:T(8,128)(2,1)S(1)}, bf16[416,256]{1,0:T(8,128)(2,1)S(1)}, u32[]{:S(2)}, u32[]{:S(2)}) collective-permute-start(bf16[416,256]{1,0:T(8,128)(2,1)S(1)} %add_convert_fusion.8), channel_id=1, source_target_pairs={{0,2},{2,4},{4,6},{6,7},{7,5},{5,3},{3,1},{1,0},{10,8},{12,10},{14... | collective-permute-start | bytes 638984 | tf_op jit(solution)/shard_map/ppermute | solution.py:244
  32.2 12.4 %collective-permute-start.18 = (bf16[416,256]{1,0:T(8,128)(2,1)S(1)}, bf16[416,256]{1,0:T(8,128)(2,1)S(1)}, u32[]{:S(2)}, u32[]{:S(2)}) collective-permute-start(bf16[416,256]{1,0:T(8,128)(2,1)S(1)} %add_convert_fusion.5), channel_id=1, source_target_pairs={{2,0},{4,2},{6,4},{7,6},{5,7},{3,5},{1,3},{0,1},{8,10},{10,12},{12... | collective-permute-start | bytes 638984 | tf_op jit(solution)/shard_map/ppermute | solution.py:244
  38.9 11.5 %collective-permute-start.15 = (bf16[416,256]{1,0:T(8,128)(2,1)S(1)}, bf16[416,256]{1,0:T(8,128)(2,1)S(1)}, u32[]{:S(2)}, u32[]{:S(2)}) collective-permute-start(bf16[416,256]{1,0:T(8,128)(2,1)S(1)} %add_convert_fusion.7), channel_id=1, source_target_pairs={{0,2},{2,4},{4,6},{6,7},{7,5},{5,3},{3,1},{1,0},{10,8},{12,10},{14... | collective-permute-start | bytes 638984 | tf_op jit(solution)/shard_map/ppermute | solution.py:244
  50.5 12.7 %collective-permute-start.19 = (bf16[256,256]{1,0:T(8,128)(2,1)S(1)}, bf16[256,256]{1,0:T(8,128)(2,1)S(1)}, u32[]{:S(2)}, u32[]{:S(2)}) collective-permute-start(bf16[256,256]{1,0:T(8,128)(2,1)S(1)} %get-tuple-element.77), channel_id=1, source_target_pairs={{0,23},{1,22},{2,21},{3,20},{4,19},{5,18},{6,17},{7,16},{8,31},{9,... | collective-permute-start | bytes 393224 | tf_op jit(solution)/shard_map/ppermute | solution.py:515
  58.1 24.6 %copy-start.8 = (s32[16]{0:T(128)S(1)}, s32[16]{0:T(128)}, u32[]{:S(2)}) copy-start(s32[16]{0:T(128)} %param.26) | copy-start | bytes 196
  58.1 24.8 %copy-start.9 = (s32[16]{0:T(128)S(1)}, s32[16]{0:T(128)}, u32[]{:S(2)}) copy-start(s32[16]{0:T(128)} %param.25) | copy-start | bytes 196
  58.1 36.2 %copy-start = (bf16[256,256]{1,0:T(8,128)(2,1)S(1)}, bf16[256,256]{1,0:T(8,128)(2,1)}, u32[]{:S(2)}) copy-start(bf16[256,256]{1,0:T(8,128)(2,1)} %resident.1) | copy-start | bytes 393220
  58.1 36.2 %copy-start.2 = (bf16[2,16,1024]{2,1,0:T(8,128)(2,1)S(1)}, bf16[2,16,1024]{2,1,0:T(8,128)(2,1)}, u32[]{:S(2)}) copy-start(bf16[2,16,1024]{2,1,0:T(8,128)(2,1)} %queries.1) | copy-start | bytes 196612
  65.0 29.3 %all-to-all-start = ((bf16[32,32,256]{2,1,0:T(8,128)(2,1)}), bf16[32,32,256]{2,1,0:T(8,128)(2,1)S(1)}, u32[]{:S(2)}, u32[]{:S(2)}) async-start(bf16[32,32,256]{2,1,0:T(8,128)(2,1)} %get-tuple-element.103), calls=%async_computation | async-start | bytes 1048576 | tf_op jit(solution)/shard_map/all_to_all | solution.py:541

commit v10 on v9

--- a/solution.py
+++ b/solution.py
@@ -353,14 +353,14 @@
     target = jnp.where(valid, target, -1)
     routes = jnp.concatenate(
         [
-            jnp.where(target == iota((rows, TILE), 1) + start, 1.0, 0.0).astype(BF)
+            jnp.where(target == iota((rows, TILE), 1) + start, 1.0, 0.0)
             for start in range(0, columns, TILE)
         ],
         axis=1,
     )[:, :columns]
-    moved = dot(blocks, routes, ((0,), (0,))).astype(BF)
+    filled = jnp.sum(routes, axis=0, keepdims=True) > 0.5
+    moved = dot(blocks, routes.astype(BF), ((0,), (0,))).astype(BF)
     rebuilt[...] = moved
-    filled = dot(jnp.ones((EXTRA, rows), BF), routes)[:1] > 0.5
 
     query = jnp.concatenate(
         [queries[s, :, h * HD : (h + 1) * HD] for s in range(steps) for h in range(heads)], axis=0
@@ -396,10 +396,11 @@
         + jnp.sum(exp_moved, axis=1, keepdims=True)
         + jnp.sum(exp_fresh, axis=1, keepdims=True)
     )
+    share = 1.0 / total
     across = ((1,), (1,))
-    out = dot((exp_held / total).astype(BF), resident[HD:, :], across)
-    out = out + dot((exp_moved / total).astype(BF), moved[HD:], across)
-    out = out + dot((exp_fresh / total).astype(BF), fresh[:, HD:])
+    out = dot((exp_held * share).astype(BF), resident[HD:, :], across)
+    out = out + dot((exp_moved * share).astype(BF), moved[HD:], across)
+    out = out + dot((exp_fresh * share).astype(BF), fresh[:, HD:])
     out = out.astype(BF)
     for s in range(steps):
         for h in range(heads):

time: 97.3 us -> 97.3 us (level)
  no operation moved by 1% of the time
where the time goes in v10:
time: 97.3 us; the launch traced here: 96.8 us
  starting transfers between devices  48.9 us (50%)
  waiting for transfers between devices  34.4 us (35%)
  Pallas kernels  9.21 us (9%)
  between operations  2.25 us (2%)
  local copies, waits for them, and re-layouts  1.08 us (1%)
    ppermute x7, starting transfers between devices, ring_sums(): lax.ppermute(chunk, ('inst', 'tensor'), forward if way else backward)  25 us
    ppermute x7, waiting for transfers between devices, ring_sums(): lax.ppermute(chunk, ('inst', 'tensor'), forward if way else backward)  18.3 us
    all_to_all x1, starting transfers between devices, shards(): lax.all_to_all(outgoing, 'inst', split_axis=0, concat_axis=0, tiled=True,...  17.7 us
    all_to_all x1, waiting for transfers between devices, shards(): lax.all_to_all(outgoing, 'inst', split_axis=0, concat_axis=0, tiled=True,...  11.3 us
    ppermute x1, starting transfers between devices, shards(): received = lax.ppermute(crossing_rows, ('inst', 'tensor'), halves)  6.19 us
    ppermute x1, waiting for transfers between devices, shards(): received = lax.ppermute(crossing_rows, ('inst', 'tensor'), halves)  4.74 us
    pallas_call x1, Pallas kernels, project_chunks(): pl.pallas_call(functools.partial(first_chunks, pairs[0]), in_specs=[hbm]...  2.75 us
    pallas_call x1, Pallas kernels, rebuild(): pl.pallas_call(rebuild_and_attend, out_shape=[jax.ShapeDtypeStruct((arriv...  2.5 us
  transfers between devices with their start and end apart: 9, of which 8 were waited for; matrix products, arithmetic and copies ran while one was open for 1% of the time, Pallas kernels for 3%

profile of v10, /device:TPU:129, one launch (start us, length us, event | category | flops | bytes accessed | tf_op | source)
XLA Modules:
  0.0 96.8 jit_solution(3591976535693820479)
XLA Ops:
  0.6 0.8 copy-done.1
  1.5 2.7 %first_chunks.1 = (bf16[416,256]{1,0:T(8,128)(2,1)S(1)}, bf16[416,256]{1,0:T(8,128)(2,1)S(1)}, bf16[400,1024]{1,0:T(8,128)(2,1)S(1)}, bf16[16,256]{1,0:T(8,128)(2,1)S(1)}, s32[8,512]{1,0:T(8,128)S(1)}) custom-call(s32[1,32]{1,0:T(1,128)} %bitcast.37, s32[1,32]{1,0:T(1,128)} %bitcast.36, f32[1,1024]{1,0:T(1,128)} %bitcast.31, bf16[32,1024]{1,0:T(8,128)(2,1)S(1)} %bitcast.29, ...), custom_call_target="tpu_custom_call" | custom-call | flops 419430400 | bytes 2277376 | tf_op jit(solution)/shard_map/first_chunks/pallas_call | solution.py:179
  4.2 1.9 %collective-permute-start.12 = (bf16[416,256]{1,0:T(8,128)(2,1)S(1)}, bf16[416,256]{1,0:T(8,128)(2,1)S(1)}, u32[]{:S(2)}, u32[]{:S(2)}) collective-permute-start(bf16[416,256]{1,0:T(8,128)(2,1)S(1)} %get-tuple-element.67), channel_id=1, source_target_pairs={{0,2},{2,4},{4,6},{6,7},{7,5},{5,3},{3,1},{1,0},{10,8},{12,10},{14... | collective-permute-start | bytes 638984 | tf_op jit(solution)/shard_map/ppermute | solution.py:244
  6.2 0.8 second_chunks.1
  7.0 5.0 %collective-permute-start.16 = (bf16[416,256]{1,0:T(8,128)(2,1)S(1)}, bf16[416,256]{1,0:T(8,128)(2,1)S(1)}, u32[]{:S(2)}, u32[]{:S(2)}) collective-permute-start(bf16[416,256]{1,0:T(8,128)(2,1)S(1)} %get-tuple-element.73), channel_id=1, source_target_pairs={{2,0},{4,2},{6,4},{7,6},{5,7},{3,5},{1,3},{0,1},{8,10},{10,12},{12... | collective-permute-start | bytes 638984 | tf_op jit(solution)/shard_map/ppermute | solution.py:244
  12.1 1.6 %later_chunks.1 = (bf16[416,256]{1,0:T(8,128)(2,1)S(1)}, bf16[416,256]{1,0:T(8,128)(2,1)S(1)}, bf16[416,256]{1,0:T(8,128)(2,1)S(1)}, bf16[416,256]{1,0:T(8,128)(2,1)S(1)}) custom-call(bf16[400,1024]{1,0:T(8,128)(2,1)S(1)} %get-tuple-element.68.scaled, bf16[16,256]{1,0:T(8,128)(2,1)S(1)} %get-tuple-element.69.extra, s32[8,512]{1,0:T(8,128)S(1)} %get-tuple-element.66.codes, ...), custom_call_target="tpu_custom_call" | custom-call | flops 838860800 | bytes 3735552 | tf_op jit(solution)/shard_map/later_chunks/pallas_call | solution.py:199
  13.7 2.5 %collective-permute-start.13 = (bf16[416,256]{1,0:T(8,128)(2,1)S(1)}, bf16[416,256]{1,0:T(8,128)(2,1)S(1)}, u32[]{:S(2)}, u32[]{:S(2)}) collective-permute-start(bf16[416,256]{1,0:T(8,128)(2,1)S(1)} %add_convert_fusion.9), channel_id=1, source_target_pairs={{0,2},{2,4},{4,6},{6,7},{7,5},{5,3},{3,1},{1,0},{10,8},{12,10},{14... | collective-permute-start | bytes 638984 | tf_op jit(solution)/shard_map/ppermute | solution.py:244
  16.2 2.6 %collective-permute-done.16 = bf16[416,256]{1,0:T(8,128)(2,1)S(1)} collective-permute-done((bf16[416,256]{1,0:T(8,128)(2,1)S(1)}, bf16[416,256]{1,0:T(8,128)(2,1)S(1)}, u32[]{:S(2)}, u32[]{:S(2)}) %collective-permute-start.16) | collective-permute-done | bytes 213024 | tf_op jit(solution)/shard_map/ppermute | solution.py:244
  18.8 5.5 %collective-permute-start.17 = (bf16[416,256]{1,0:T(8,128)(2,1)S(1)}, bf16[416,256]{1,0:T(8,128)(2,1)S(1)}, u32[]{:S(2)}, u32[]{:S(2)}) collective-permute-start(bf16[416,256]{1,0:T(8,128)(2,1)S(1)} %add_convert_fusion.6), channel_id=1, source_target_pairs={{2,0},{4,2},{6,4},{7,6},{5,7},{3,5},{1,3},{0,1},{8,10},{10,12},{12... | collective-permute-start | bytes 638984 | tf_op jit(solution)/shard_map/ppermute | solution.py:244
  24.3 1.5 %collective-permute-done.13 = bf16[416,256]{1,0:T(8,128)(2,1)S(1)} collective-permute-done((bf16[416,256]{1,0:T(8,128)(2,1)S(1)}, bf16[416,256]{1,0:T(8,128)(2,1)S(1)}, u32[]{:S(2)}, u32[]{:S(2)}) %collective-permute-start.13) | collective-permute-done | bytes 213024 | tf_op jit(solution)/shard_map/ppermute | solution.py:244
  25.9 1.9 %collective-permute-start.14 = (bf16[416,256]{1,0:T(8,128)(2,1)S(1)}, bf16[416,256]{1,0:T(8,128)(2,1)S(1)}, u32[]{:S(2)}, u32[]{:S(2)}) collective-permute-start(bf16[416,256]{1,0:T(8,128)(2,1)S(1)} %add_convert_fusion.8), channel_id=1, source_target_pairs={{0,2},{2,4},{4,6},{6,7},{7,5},{5,3},{3,1},{1,0},{10,8},{12,10},{14... | collective-permute-start | bytes 638984 | tf_op jit(solution)/shard_map/ppermute | solution.py:244
  27.8 4.3 %collective-permute-done.17 = bf16[416,256]{1,0:T(8,128)(2,1)S(1)} collective-permute-done((bf16[416,256]{1,0:T(8,128)(2,1)S(1)}, bf16[416,256]{1,0:T(8,128)(2,1)S(1)}, u32[]{:S(2)}, u32[]{:S(2)}) %collective-permute-start.17) | collective-permute-done | bytes 213024 | tf_op jit(solution)/shard_map/ppermute | solution.py:244
  32.2 4.3 %collective-permute-start.18 = (bf16[416,256]{1,0:T(8,128)(2,1)S(1)}, bf16[416,256]{1,0:T(8,128)(2,1)S(1)}, u32[]{:S(2)}, u32[]{:S(2)}) collective-permute-start(bf16[416,256]{1,0:T(8,128)(2,1)S(1)} %add_convert_fusion.5), channel_id=1, source_target_pairs={{2,0},{4,2},{6,4},{7,6},{5,7},{3,5},{1,3},{0,1},{8,10},{10,12},{12... | collective-permute-start | bytes 638984 | tf_op jit(solution)/shard_map/ppermute | solution.py:244
  36.5 2.4 %collective-permute-done.14 = bf16[416,256]{1,0:T(8,128)(2,1)S(1)} collective-permute-done((bf16[416,256]{1,0:T(8,128)(2,1)S(1)}, bf16[416,256]{1,0:T(8,128)(2,1)S(1)}, u32[]{:S(2)}, u32[]{:S(2)}) %collective-permute-start.14) | collective-permute-done | bytes 213024 | tf_op jit(solution)/shard_map/ppermute | solution.py:244
  38.9 3.9 %collective-permute-start.15 = (bf16[416,256]{1,0:T(8,128)(2,1)S(1)}, bf16[416,256]{1,0:T(8,128)(2,1)S(1)}, u32[]{:S(2)}, u32[]{:S(2)}) collective-permute-start(bf16[416,256]{1,0:T(8,128)(2,1)S(1)} %add_convert_fusion.7), channel_id=1, source_target_pairs={{0,2},{2,4},{4,6},{6,7},{7,5},{5,3},{3,1},{1,0},{10,8},{12,10},{14... | collective-permute-start | bytes 638984 | tf_op jit(solution)/shard_map/ppermute | solution.py:244
  42.8 1.8 %collective-permute-done.18.behind = bf16[416,256]{1,0:T(8,128)(2,1)S(1)} collective-permute-done((bf16[416,256]{1,0:T(8,128)(2,1)S(1)}, bf16[416,256]{1,0:T(8,128)(2,1)S(1)}, u32[]{:S(2)}, u32[]{:S(2)}) %collective-permute-start.18) | collective-permute-done | bytes 213024 | tf_op jit(solution)/shard_map/ppermute | solution.py:244
  44.5 5.8 %collective-permute-done.15.ahead = bf16[416,256]{1,0:T(8,128)(2,1)S(1)} collective-permute-done((bf16[416,256]{1,0:T(8,128)(2,1)S(1)}, bf16[416,256]{1,0:T(8,128)(2,1)S(1)}, u32[]{:S(2)}, u32[]{:S(2)}) %collective-permute-start.15) | collective-permute-done | bytes 213024 | tf_op jit(solution)/shard_map/ppermute | solution.py:244
  50.5 6.2 %collective-permute-start.19 = (bf16[256,256]{1,0:T(8,128)(2,1)S(1)}, bf16[256,256]{1,0:T(8,128)(2,1)S(1)}, u32[]{:S(2)}, u32[]{:S(2)}) collective-permute-start(bf16[256,256]{1,0:T(8,128)(2,1)S(1)} %get-tuple-element.77), channel_id=1, source_target_pairs={{0,23},{1,22},{2,21},{3,20},{4,19},{5,18},{6,17},{7,16},{8,31},{9,... | collective-permute-start | bytes 393224 | tf_op jit(solution)/shard_map/ppermute | solution.py:516
  56.7 0.6 reduce_sum.36
  58.5 4.7 %collective-permute-done.19.received = bf16[256,256]{1,0:T(8,128)(2,1)S(1)} collective-permute-done((bf16[256,256]{1,0:T(8,128)(2,1)S(1)}, bf16[256,256]{1,0:T(8,128)(2,1)S(1)}, u32[]{:S(2)}, u32[]{:S(2)}) %collective-permute-start.19) | collective-permute-done | bytes 131104 | tf_op jit(solution)/shard_map/ppermute | solution.py:516
  63.2 1.1 %place_crossing.1 = (bf16[32,32,256]{2,1,0:T(8,128)(2,1)}, s32[1]{0:T(128)}) custom-call(bf16[256,256]{1,0:T(8,128)(2,1)S(1)} %collective-permute-done.19.received, s32[8,512]{1,0:T(8,128)S(1)} %get-tuple-element.66.codes, bf16[32,16,256]{2,1,0:T(8,128)(2,1)S(1)} %place_staying.1.near), custom_call_target="tpu_custom_call" | custom-call | tf_op jit(solution)/shard_map/place_crossing/pallas_call | solution.py:317
  65.0 17.7 %all-to-all-start = ((bf16[32,32,256]{2,1,0:T(8,128)(2,1)}), bf16[32,32,256]{2,1,0:T(8,128)(2,1)S(1)}, u32[]{:S(2)}, u32[]{:S(2)}) async-start(bf16[32,32,256]{2,1,0:T(8,128)(2,1)} %get-tuple-element.103), calls=%async_computation | async-start | bytes 1048576 | tf_op jit(solution)/shard_map/all_to_all | solution.py:542
  83.0 11.3 %all-to-all-done.arrived = bf16[32,32,256]{2,1,0:T(8,128)(2,1)S(1)} async-done(((bf16[32,32,256]{2,1,0:T(8,128)(2,1)}), bf16[32,32,256]{2,1,0:T(8,128)(2,1)S(1)}, u32[]{:S(2)}, u32[]{:S(2)}) %all-to-all-start) | async-done | bytes 524320 | tf_op jit(solution)/shard_map/all_to_all | solution.py:542
  94.3 2.5 %rebuild_and_attend.1 = (bf16[256,512]{1,0:T(8,128)(2,1)}, bf16[2,16,1024]{2,1,0:T(8,128)(2,1)}) custom-call(bf16[32,32,256]{2,1,0:T(8,128)(2,1)S(1)} %all-to-all-done.arrived, bf16[256,256]{1,0:T(8,128)(2,1)S(1)} %copy-done, s32[1,256]{1,0:T(1,128)S(1)} %reshape.145.resident_valid, bf16[2,16,1024]{2,1,0:T(8,128)(2,1)S(1)} %copy-done.2, ...), custom_call_target="tpu_custom_call" | custom-call | tf_op jit(solution)/shard_map/rebuild_and_attend/pallas_call | solution.py:412
  (34 shorter events, 1.1 us)
Async XLA Ops:
  0.6 0.8 copy-start.1
  1.5 4.7 %copy-start.3 = (bf16[1024,2048]{1,0:T(8,128)(2,1)S(1)}, bf16[1024,2048]{1,0:T(8,128)(2,1)}, u32[]{:S(2)}) copy-start(bf16[1024,2048]{1,0:T(8,128)(2,1)} %weight.3) | copy-start | bytes 12582916
  4.2 9.4 %collective-permute-start.12 = (bf16[416,256]{1,0:T(8,128)(2,1)S(1)}, bf16[416,256]{1,0:T(8,128)(2,1)S(1)}, u32[]{:S(2)}, u32[]{:S(2)}) collective-permute-start(bf16[416,256]{1,0:T(8,128)(2,1)S(1)} %get-tuple-element.67), channel_id=1, source_target_pairs={{0,2},{2,4},{4,6},{6,7},{7,5},{5,3},{3,1},{1,0},{10,8},{12,10},{14... | collective-permute-start | bytes 638984 | tf_op jit(solution)/shard_map/ppermute | solution.py:244
  7.0 49.8 %copy-start.6 = (s32[32]{0:T(128)S(1)}, s32[32]{0:T(128)}, u32[]{:S(2)}) copy-start(s32[32]{0:T(128)} %param.24) | copy-start | bytes 388
  7.0 51.0 %copy-start.4 = (bf16[512,1024]{1,0:T(8,128)(2,1)S(1)}, bf16[512,1024]{1,0:T(8,128)(2,1)}, u32[]{:S(2)}) copy-start(bf16[512,1024]{1,0:T(8,128)(2,1)} %refs_4_.1) | copy-start | bytes 3145732
  7.0 51.0 %copy-start.5 = (f32[1024]{0:T(1024)S(1)}, f32[1024]{0:T(1024)}, u32[]{:S(2)}) copy-start(f32[1024]{0:T(1024)} %param.19) | copy-start | bytes 12292
  7.0 51.0 %copy-start.7 = (s32[32]{0:T(128)S(1)}, s32[32]{0:T(128)}, u32[]{:S(2)}) copy-start(s32[32]{0:T(128)} %param.23) | copy-start | bytes 388
  7.0 11.8 %collective-permute-start.16 = (bf16[416,256]{1,0:T(8,128)(2,1)S(1)}, bf16[416,256]{1,0:T(8,128)(2,1)S(1)}, u32[]{:S(2)}, u32[]{:S(2)}) collective-permute-start(bf16[416,256]{1,0:T(8,128)(2,1)S(1)} %get-tuple-element.73), channel_id=1, source_target_pairs={{2,0},{4,2},{6,4},{7,6},{5,7},{3,5},{1,3},{0,1},{8,10},{10,12},{12... | collective-permute-start | bytes 638984 | tf_op jit(solution)/shard_map/ppermute | solution.py:244
  13.7 12.1 %collective-permute-start.13 = (bf16[416,256]{1,0:T(8,128)(2,1)S(1)}, bf16[416,256]{1,0:T(8,128)(2,1)S(1)}, u32[]{:S(2)}, u32[]{:S(2)}) collective-permute-start(bf16[416,256]{1,0:T(8,128)(2,1)S(1)} %add_convert_fusion.9), channel_id=1, source_target_pairs={{0,2},{2,4},{4,6},{6,7},{7,5},{5,3},{3,1},{1,0},{10,8},{12,10},{14... | collective-permute-start | bytes 638984 | tf_op jit(solution)/shard_map/ppermute | solution.py:244
  18.8 13.3 %collective-permute-start.17 = (bf16[416,256]{1,0:T(8,128)(2,1)S(1)}, bf16[416,256]{1,0:T(8,128)(2,1)S(1)}, u32[]{:S(2)}, u32[]{:S(2)}) collective-permute-start(bf16[416,256]{1,0:T(8,128)(2,1)S(1)} %add_convert_fusion.6), channel_id=1, source_target_pairs={{2,0},{4,2},{6,4},{7,6},{5,7},{3,5},{1,3},{0,1},{8,10},{10,12},{12... | collective-permute-start | bytes 638984 | tf_op jit(solution)/shard_map/ppermute | solution.py:244
  25.9 13.0 %collective-permute-start.14 = (bf16[416,256]{1,0:T(8,128)(2,1)S(1)}, bf16[416,256]{1,0:T(8,128)(2,1)S(1)}, u32[]{:S(2)}, u32[]{:S(2)}) collective-permute-start(bf16[416,256]{1,0:T(8,128)(2,1)S(1)} %add_convert_fusion.8), channel_id=1, source_target_pairs={{0,2},{2,4},{4,6},{6,7},{7,5},{5,3},{3,1},{1,0},{10,8},{12,10},{14... | collective-permute-start | bytes 638984 | tf_op jit(solution)/shard_map/ppermute | solution.py:244
  32.2 12.4 %collective-permute-start.18 = (bf16[416,256]{1,0:T(8,128)(2,1)S(1)}, bf16[416,256]{1,0:T(8,128)(2,1)S(1)}, u32[]{:S(2)}, u32[]{:S(2)}) collective-permute-start(bf16[416,256]{1,0:T(8,128)(2,1)S(1)} %add_convert_fusion.5), channel_id=1, source_target_pairs={{2,0},{4,2},{6,4},{7,6},{5,7},{3,5},{1,3},{0,1},{8,10},{10,12},{12... | collective-permute-start | bytes 638984 | tf_op jit(solution)/shard_map/ppermute | solution.py:244
  38.9 11.5 %collective-permute-start.15 = (bf16[416,256]{1,0:T(8,128)(2,1)S(1)}, bf16[416,256]{1,0:T(8,128)(2,1)S(1)}, u32[]{:S(2)}, u32[]{:S(2)}) collective-permute-start(bf16[416,256]{1,0:T(8,128)(2,1)S(1)} %add_convert_fusion.7), channel_id=1, source_target_pairs={{0,2},{2,4},{4,6},{6,7},{7,5},{5,3},{3,1},{1,0},{10,8},{12,10},{14... | collective-permute-start | bytes 638984 | tf_op jit(solution)/shard_map/ppermute | solution.py:244
  50.5 12.7 %collective-permute-start.19 = (bf16[256,256]{1,0:T(8,128)(2,1)S(1)}, bf16[256,256]{1,0:T(8,128)(2,1)S(1)}, u32[]{:S(2)}, u32[]{:S(2)}) collective-permute-start(bf16[256,256]{1,0:T(8,128)(2,1)S(1)} %get-tuple-element.77), channel_id=1, source_target_pairs={{0,23},{1,22},{2,21},{3,20},{4,19},{5,18},{6,17},{7,16},{8,31},{9,... | collective-permute-start | bytes 393224 | tf_op jit(solution)/shard_map/ppermute | solution.py:516
  58.1 24.6 %copy-start.8 = (s32[16]{0:T(128)S(1)}, s32[16]{0:T(128)}, u32[]{:S(2)}) copy-start(s32[16]{0:T(128)} %param.26) | copy-start | bytes 196
  58.1 24.8 %copy-start.9 = (s32[16]{0:T(128)S(1)}, s32[16]{0:T(128)}, u32[]{:S(2)}) copy-start(s32[16]{0:T(128)} %param.25) | copy-start | bytes 196
  58.1 36.2 %copy-start = (bf16[256,256]{1,0:T(8,128)(2,1)S(1)}, bf16[256,256]{1,0:T(8,128)(2,1)}, u32[]{:S(2)}) copy-start(bf16[256,256]{1,0:T(8,128)(2,1)} %resident.1) | copy-start | bytes 393220
  58.1 36.2 %copy-start.2 = (bf16[2,16,1024]{2,1,0:T(8,128)(2,1)S(1)}, bf16[2,16,1024]{2,1,0:T(8,128)(2,1)}, u32[]{:S(2)}) copy-start(bf16[2,16,1024]{2,1,0:T(8,128)(2,1)} %queries.1) | copy-start | bytes 196612
  65.0 29.3 %all-to-all-start = ((bf16[32,32,256]{2,1,0:T(8,128)(2,1)}), bf16[32,32,256]{2,1,0:T(8,128)(2,1)S(1)}, u32[]{:S(2)}, u32[]{:S(2)}) async-start(bf16[32,32,256]{2,1,0:T(8,128)(2,1)} %get-tuple-element.103), calls=%async_computation | async-start | bytes 1048576 | tf_op jit(solution)/shard_map/all_to_all | solution.py:542

commit v11 on v10

--- a/solution.py
+++ b/solution.py
@@ -287,8 +287,9 @@
 
 
 def routed(route, rows):
-    found = jnp.sum(route, axis=1, keepdims=True) > 0.5
-    return jnp.where(found, dot(route.astype(BF), rows), ABSENT).astype(BF)
+    narrow = route.astype(BF)
+    found = dot(narrow, jnp.ones((route.shape[1], rows.shape[1]), BF))
+    return jnp.where(found > 0.5, dot(narrow, rows), ABSENT).astype(BF)
 
 
 def place_staying(codes, first, second, out):

time: 97.3 us -> 97.4 us (level)
  no operation moved by 1% of the time
where the time goes in v11:
time: 97.4 us; the launch traced here: 96.9 us
  starting transfers between devices  48.9 us (50%)
  waiting for transfers between devices  34.4 us (35%)
  Pallas kernels  9.29 us (10%)
  between operations  2.25 us (2%)
  local copies, waits for them, and re-layouts  1.08 us (1%)
  other arithmetic  0.98 us (1%)
    ppermute x7, starting transfers between devices, ring_sums(): lax.ppermute(chunk, ('inst', 'tensor'), forward if way else backward)  25 us
    ppermute x7, waiting for transfers between devices, ring_sums(): lax.ppermute(chunk, ('inst', 'tensor'), forward if way else backward)  18.4 us
    all_to_all x1, starting transfers between devices, shards(): lax.all_to_all(outgoing, 'inst', split_axis=0, concat_axis=0, tiled=True,...  17.7 us
    all_to_all x1, waiting for transfers between devices, shards(): lax.all_to_all(outgoing, 'inst', split_axis=0, concat_axis=0, tiled=True,...  11.3 us
    ppermute x1, starting transfers between devices, shards(): received = lax.ppermute(crossing_rows, ('inst', 'tensor'), halves)  6.17 us
    ppermute x1, waiting for transfers between devices, shards(): received = lax.ppermute(crossing_rows, ('inst', 'tensor'), halves)  4.7 us
    pallas_call x1, Pallas kernels, project_chunks(): pl.pallas_call(functools.partial(first_chunks, pairs[0]), in_specs=[hbm]...  2.75 us
    pallas_call x1, Pallas kernels, rebuild(): pl.pallas_call(rebuild_and_attend, out_shape=[jax.ShapeDtypeStruct((arriv...  2.5 us
  transfers between devices with their start and end apart: 9, of which 8 were waited for; matrix products, arithmetic and copies ran while one was open for 1% of the time, Pallas kernels for 3%

profile of v11, /device:TPU:129, one launch (start us, length us, event | category | flops | bytes accessed | tf_op | source)
XLA Modules:
  0.0 96.9 jit_solution(11849075447972408152)
XLA Ops:
  0.6 0.8 copy-done.1
  1.5 2.7 %first_chunks.1 = (bf16[416,256]{1,0:T(8,128)(2,1)S(1)}, bf16[416,256]{1,0:T(8,128)(2,1)S(1)}, bf16[400,1024]{1,0:T(8,128)(2,1)S(1)}, bf16[16,256]{1,0:T(8,128)(2,1)S(1)}, s32[8,512]{1,0:T(8,128)S(1)}) custom-call(s32[1,32]{1,0:T(1,128)} %bitcast.37, s32[1,32]{1,0:T(1,128)} %bitcast.34, f32[1,1024]{1,0:T(1,128)} %bitcast.31, bf16[32,1024]{1,0:T(8,128)(2,1)S(1)} %bitcast.29, ...), custom_call_target="tpu_custom_call" | custom-call | flops 419430400 | bytes 2277376 | tf_op jit(solution)/shard_map/first_chunks/pallas_call | solution.py:179
  4.2 1.9 %collective-permute-start.12 = (bf16[416,256]{1,0:T(8,128)(2,1)S(1)}, bf16[416,256]{1,0:T(8,128)(2,1)S(1)}, u32[]{:S(2)}, u32[]{:S(2)}) collective-permute-start(bf16[416,256]{1,0:T(8,128)(2,1)S(1)} %get-tuple-element.67), channel_id=1, source_target_pairs={{0,2},{2,4},{4,6},{6,7},{7,5},{5,3},{3,1},{1,0},{10,8},{12,10},{14... | collective-permute-start | bytes 638984 | tf_op jit(solution)/shard_map/ppermute | solution.py:244
  6.2 0.8 second_chunks.1
  7.0 5.0 %collective-permute-start.16 = (bf16[416,256]{1,0:T(8,128)(2,1)S(1)}, bf16[416,256]{1,0:T(8,128)(2,1)S(1)}, u32[]{:S(2)}, u32[]{:S(2)}) collective-permute-start(bf16[416,256]{1,0:T(8,128)(2,1)S(1)} %get-tuple-element.73), channel_id=1, source_target_pairs={{2,0},{4,2},{6,4},{7,6},{5,7},{3,5},{1,3},{0,1},{8,10},{10,12},{12... | collective-permute-start | bytes 638984 | tf_op jit(solution)/shard_map/ppermute | solution.py:244
  12.1 1.6 %later_chunks.1 = (bf16[416,256]{1,0:T(8,128)(2,1)S(1)}, bf16[416,256]{1,0:T(8,128)(2,1)S(1)}, bf16[416,256]{1,0:T(8,128)(2,1)S(1)}, bf16[416,256]{1,0:T(8,128)(2,1)S(1)}) custom-call(bf16[400,1024]{1,0:T(8,128)(2,1)S(1)} %get-tuple-element.68.scaled, bf16[16,256]{1,0:T(8,128)(2,1)S(1)} %get-tuple-element.69.extra, s32[8,512]{1,0:T(8,128)S(1)} %get-tuple-element.66.codes, ...), custom_call_target="tpu_custom_call" | custom-call | flops 838860800 | bytes 3735552 | tf_op jit(solution)/shard_map/later_chunks/pallas_call | solution.py:199
  13.7 2.5 %collective-permute-start.13 = (bf16[416,256]{1,0:T(8,128)(2,1)S(1)}, bf16[416,256]{1,0:T(8,128)(2,1)S(1)}, u32[]{:S(2)}, u32[]{:S(2)}) collective-permute-start(bf16[416,256]{1,0:T(8,128)(2,1)S(1)} %add_convert_fusion.9), channel_id=1, source_target_pairs={{0,2},{2,4},{4,6},{6,7},{7,5},{5,3},{3,1},{1,0},{10,8},{12,10},{14... | collective-permute-start | bytes 638984 | tf_op jit(solution)/shard_map/ppermute | solution.py:244
  16.2 2.6 %collective-permute-done.16 = bf16[416,256]{1,0:T(8,128)(2,1)S(1)} collective-permute-done((bf16[416,256]{1,0:T(8,128)(2,1)S(1)}, bf16[416,256]{1,0:T(8,128)(2,1)S(1)}, u32[]{:S(2)}, u32[]{:S(2)}) %collective-permute-start.16) | collective-permute-done | bytes 213024 | tf_op jit(solution)/shard_map/ppermute | solution.py:244
  18.8 5.5 %collective-permute-start.17 = (bf16[416,256]{1,0:T(8,128)(2,1)S(1)}, bf16[416,256]{1,0:T(8,128)(2,1)S(1)}, u32[]{:S(2)}, u32[]{:S(2)}) collective-permute-start(bf16[416,256]{1,0:T(8,128)(2,1)S(1)} %add_convert_fusion.6), channel_id=1, source_target_pairs={{2,0},{4,2},{6,4},{7,6},{5,7},{3,5},{1,3},{0,1},{8,10},{10,12},{12... | collective-permute-start | bytes 638984 | tf_op jit(solution)/shard_map/ppermute | solution.py:244
  24.3 1.5 %collective-permute-done.13 = bf16[416,256]{1,0:T(8,128)(2,1)S(1)} collective-permute-done((bf16[416,256]{1,0:T(8,128)(2,1)S(1)}, bf16[416,256]{1,0:T(8,128)(2,1)S(1)}, u32[]{:S(2)}, u32[]{:S(2)}) %collective-permute-start.13) | collective-permute-done | bytes 213024 | tf_op jit(solution)/shard_map/ppermute | solution.py:244
  25.9 1.9 %collective-permute-start.14 = (bf16[416,256]{1,0:T(8,128)(2,1)S(1)}, bf16[416,256]{1,0:T(8,128)(2,1)S(1)}, u32[]{:S(2)}, u32[]{:S(2)}) collective-permute-start(bf16[416,256]{1,0:T(8,128)(2,1)S(1)} %add_convert_fusion.8), channel_id=1, source_target_pairs={{0,2},{2,4},{4,6},{6,7},{7,5},{5,3},{3,1},{1,0},{10,8},{12,10},{14... | collective-permute-start | bytes 638984 | tf_op jit(solution)/shard_map/ppermute | solution.py:244
  27.8 4.3 %collective-permute-done.17 = bf16[416,256]{1,0:T(8,128)(2,1)S(1)} collective-permute-done((bf16[416,256]{1,0:T(8,128)(2,1)S(1)}, bf16[416,256]{1,0:T(8,128)(2,1)S(1)}, u32[]{:S(2)}, u32[]{:S(2)}) %collective-permute-start.17) | collective-permute-done | bytes 213024 | tf_op jit(solution)/shard_map/ppermute | solution.py:244
  32.2 4.3 %collective-permute-start.18 = (bf16[416,256]{1,0:T(8,128)(2,1)S(1)}, bf16[416,256]{1,0:T(8,128)(2,1)S(1)}, u32[]{:S(2)}, u32[]{:S(2)}) collective-permute-start(bf16[416,256]{1,0:T(8,128)(2,1)S(1)} %add_convert_fusion.5), channel_id=1, source_target_pairs={{2,0},{4,2},{6,4},{7,6},{5,7},{3,5},{1,3},{0,1},{8,10},{10,12},{12... | collective-permute-start | bytes 638984 | tf_op jit(solution)/shard_map/ppermute | solution.py:244
  36.5 2.4 %collective-permute-done.14 = bf16[416,256]{1,0:T(8,128)(2,1)S(1)} collective-permute-done((bf16[416,256]{1,0:T(8,128)(2,1)S(1)}, bf16[416,256]{1,0:T(8,128)(2,1)S(1)}, u32[]{:S(2)}, u32[]{:S(2)}) %collective-permute-start.14) | collective-permute-done | bytes 213024 | tf_op jit(solution)/shard_map/ppermute | solution.py:244
  38.9 3.8 %collective-permute-start.15 = (bf16[416,256]{1,0:T(8,128)(2,1)S(1)}, bf16[416,256]{1,0:T(8,128)(2,1)S(1)}, u32[]{:S(2)}, u32[]{:S(2)}) collective-permute-start(bf16[416,256]{1,0:T(8,128)(2,1)S(1)} %add_convert_fusion.7), channel_id=1, source_target_pairs={{0,2},{2,4},{4,6},{6,7},{7,5},{5,3},{3,1},{1,0},{10,8},{12,10},{14... | collective-permute-start | bytes 638984 | tf_op jit(solution)/shard_map/ppermute | solution.py:244
  42.8 1.8 %collective-permute-done.18.behind = bf16[416,256]{1,0:T(8,128)(2,1)S(1)} collective-permute-done((bf16[416,256]{1,0:T(8,128)(2,1)S(1)}, bf16[416,256]{1,0:T(8,128)(2,1)S(1)}, u32[]{:S(2)}, u32[]{:S(2)}) %collective-permute-start.18) | collective-permute-done | bytes 213024 | tf_op jit(solution)/shard_map/ppermute | solution.py:244
  44.5 5.8 %collective-permute-done.15.ahead = bf16[416,256]{1,0:T(8,128)(2,1)S(1)} collective-permute-done((bf16[416,256]{1,0:T(8,128)(2,1)S(1)}, bf16[416,256]{1,0:T(8,128)(2,1)S(1)}, u32[]{:S(2)}, u32[]{:S(2)}) %collective-permute-start.15) | collective-permute-done | bytes 213024 | tf_op jit(solution)/shard_map/ppermute | solution.py:244
  50.5 6.2 %collective-permute-start.19 = (bf16[256,256]{1,0:T(8,128)(2,1)S(1)}, bf16[256,256]{1,0:T(8,128)(2,1)S(1)}, u32[]{:S(2)}, u32[]{:S(2)}) collective-permute-start(bf16[256,256]{1,0:T(8,128)(2,1)S(1)} %get-tuple-element.77), channel_id=1, source_target_pairs={{0,23},{1,22},{2,21},{3,20},{4,19},{5,18},{6,17},{7,16},{8,31},{9,... | collective-permute-start | bytes 393224 | tf_op jit(solution)/shard_map/ppermute | solution.py:517
  56.7 0.6 reduce_sum.27
  58.6 4.7 %collective-permute-done.19.received = bf16[256,256]{1,0:T(8,128)(2,1)S(1)} collective-permute-done((bf16[256,256]{1,0:T(8,128)(2,1)S(1)}, bf16[256,256]{1,0:T(8,128)(2,1)S(1)}, u32[]{:S(2)}, u32[]{:S(2)}) %collective-permute-start.19) | collective-permute-done | bytes 131104 | tf_op jit(solution)/shard_map/ppermute | solution.py:517
  63.3 1.1 %place_crossing.1 = (bf16[32,32,256]{2,1,0:T(8,128)(2,1)}, s32[1]{0:T(128)}) custom-call(bf16[256,256]{1,0:T(8,128)(2,1)S(1)} %collective-permute-done.19.received, s32[8,512]{1,0:T(8,128)S(1)} %get-tuple-element.66.codes, bf16[32,16,256]{2,1,0:T(8,128)(2,1)S(1)} %place_staying.1.near), custom_call_target="tpu_custom_call" | custom-call | tf_op jit(solution)/shard_map/place_crossing/pallas_call | solution.py:318
  65.0 17.7 %all-to-all-start = ((bf16[32,32,256]{2,1,0:T(8,128)(2,1)}), bf16[32,32,256]{2,1,0:T(8,128)(2,1)S(1)}, u32[]{:S(2)}, u32[]{:S(2)}) async-start(bf16[32,32,256]{2,1,0:T(8,128)(2,1)} %get-tuple-element.103), calls=%async_computation | async-start | bytes 1048576 | tf_op jit(solution)/shard_map/all_to_all | solution.py:543
  83.0 11.3 %all-to-all-done.arrived = bf16[32,32,256]{2,1,0:T(8,128)(2,1)S(1)} async-done(((bf16[32,32,256]{2,1,0:T(8,128)(2,1)}), bf16[32,32,256]{2,1,0:T(8,128)(2,1)S(1)}, u32[]{:S(2)}, u32[]{:S(2)}) %all-to-all-start) | async-done | bytes 524320 | tf_op jit(solution)/shard_map/all_to_all | solution.py:543
  94.4 2.5 %rebuild_and_attend.1 = (bf16[256,512]{1,0:T(8,128)(2,1)}, bf16[2,16,1024]{2,1,0:T(8,128)(2,1)}) custom-call(bf16[32,32,256]{2,1,0:T(8,128)(2,1)S(1)} %all-to-all-done.arrived, bf16[256,256]{1,0:T(8,128)(2,1)S(1)} %copy-done, s32[1,256]{1,0:T(1,128)S(1)} %reshape.141.resident_valid, bf16[2,16,1024]{2,1,0:T(8,128)(2,1)S(1)} %copy-done.2, ...), custom_call_target="tpu_custom_call" | custom-call | tf_op jit(solution)/shard_map/rebuild_and_attend/pallas_call | solution.py:413
  (34 shorter events, 1.2 us)
Async XLA Ops:
  0.6 0.8 copy-start.1
  1.5 4.7 %copy-start.3 = (bf16[1024,2048]{1,0:T(8,128)(2,1)S(1)}, bf16[1024,2048]{1,0:T(8,128)(2,1)}, u32[]{:S(2)}) copy-start(bf16[1024,2048]{1,0:T(8,128)(2,1)} %weight.3) | copy-start | bytes 12582916
  4.2 9.4 %collective-permute-start.12 = (bf16[416,256]{1,0:T(8,128)(2,1)S(1)}, bf16[416,256]{1,0:T(8,128)(2,1)S(1)}, u32[]{:S(2)}, u32[]{:S(2)}) collective-permute-start(bf16[416,256]{1,0:T(8,128)(2,1)S(1)} %get-tuple-element.67), channel_id=1, source_target_pairs={{0,2},{2,4},{4,6},{6,7},{7,5},{5,3},{3,1},{1,0},{10,8},{12,10},{14... | collective-permute-start | bytes 638984 | tf_op jit(solution)/shard_map/ppermute | solution.py:244
  7.0 49.7 %copy-start.6 = (s32[32]{0:T(128)S(1)}, s32[32]{0:T(128)}, u32[]{:S(2)}) copy-start(s32[32]{0:T(128)} %param.24) | copy-start | bytes 388
  7.0 51.0 %copy-start.4 = (bf16[512,1024]{1,0:T(8,128)(2,1)S(1)}, bf16[512,1024]{1,0:T(8,128)(2,1)}, u32[]{:S(2)}) copy-start(bf16[512,1024]{1,0:T(8,128)(2,1)} %refs_4_.1) | copy-start | bytes 3145732
  7.0 51.0 %copy-start.5 = (f32[1024]{0:T(1024)S(1)}, f32[1024]{0:T(1024)}, u32[]{:S(2)}) copy-start(f32[1024]{0:T(1024)} %param.19) | copy-start | bytes 12292
  7.0 51.0 %copy-start.7 = (s32[32]{0:T(128)S(1)}, s32[32]{0:T(128)}, u32[]{:S(2)}) copy-start(s32[32]{0:T(128)} %param.23) | copy-start | bytes 388
  7.0 11.8 %collective-permute-start.16 = (bf16[416,256]{1,0:T(8,128)(2,1)S(1)}, bf16[416,256]{1,0:T(8,128)(2,1)S(1)}, u32[]{:S(2)}, u32[]{:S(2)}) collective-permute-start(bf16[416,256]{1,0:T(8,128)(2,1)S(1)} %get-tuple-element.73), channel_id=1, source_target_pairs={{2,0},{4,2},{6,4},{7,6},{5,7},{3,5},{1,3},{0,1},{8,10},{10,12},{12... | collective-permute-start | bytes 638984 | tf_op jit(solution)/shard_map/ppermute | solution.py:244
  13.7 12.1 %collective-permute-start.13 = (bf16[416,256]{1,0:T(8,128)(2,1)S(1)}, bf16[416,256]{1,0:T(8,128)(2,1)S(1)}, u32[]{:S(2)}, u32[]{:S(2)}) collective-permute-start(bf16[416,256]{1,0:T(8,128)(2,1)S(1)} %add_convert_fusion.9), channel_id=1, source_target_pairs={{0,2},{2,4},{4,6},{6,7},{7,5},{5,3},{3,1},{1,0},{10,8},{12,10},{14... | collective-permute-start | bytes 638984 | tf_op jit(solution)/shard_map/ppermute | solution.py:244
  18.8 13.3 %collective-permute-start.17 = (bf16[416,256]{1,0:T(8,128)(2,1)S(1)}, bf16[416,256]{1,0:T(8,128)(2,1)S(1)}, u32[]{:S(2)}, u32[]{:S(2)}) collective-permute-start(bf16[416,256]{1,0:T(8,128)(2,1)S(1)} %add_convert_fusion.6), channel_id=1, source_target_pairs={{2,0},{4,2},{6,4},{7,6},{5,7},{3,5},{1,3},{0,1},{8,10},{10,12},{12... | collective-permute-start | bytes 638984 | tf_op jit(solution)/shard_map/ppermute | solution.py:244
  25.9 13.0 %collective-permute-start.14 = (bf16[416,256]{1,0:T(8,128)(2,1)S(1)}, bf16[416,256]{1,0:T(8,128)(2,1)S(1)}, u32[]{:S(2)}, u32[]{:S(2)}) collective-permute-start(bf16[416,256]{1,0:T(8,128)(2,1)S(1)} %add_convert_fusion.8), channel_id=1, source_target_pairs={{0,2},{2,4},{4,6},{6,7},{7,5},{5,3},{3,1},{1,0},{10,8},{12,10},{14... | collective-permute-start | bytes 638984 | tf_op jit(solution)/shard_map/ppermute | solution.py:244
  32.2 12.4 %collective-permute-start.18 = (bf16[416,256]{1,0:T(8,128)(2,1)S(1)}, bf16[416,256]{1,0:T(8,128)(2,1)S(1)}, u32[]{:S(2)}, u32[]{:S(2)}) collective-permute-start(bf16[416,256]{1,0:T(8,128)(2,1)S(1)} %add_convert_fusion.5), channel_id=1, source_target_pairs={{2,0},{4,2},{6,4},{7,6},{5,7},{3,5},{1,3},{0,1},{8,10},{10,12},{12... | collective-permute-start | bytes 638984 | tf_op jit(solution)/shard_map/ppermute | solution.py:244
  38.9 11.5 %collective-permute-start.15 = (bf16[416,256]{1,0:T(8,128)(2,1)S(1)}, bf16[416,256]{1,0:T(8,128)(2,1)S(1)}, u32[]{:S(2)}, u32[]{:S(2)}) collective-permute-start(bf16[416,256]{1,0:T(8,128)(2,1)S(1)} %add_convert_fusion.7), channel_id=1, source_target_pairs={{0,2},{2,4},{4,6},{6,7},{7,5},{5,3},{3,1},{1,0},{10,8},{12,10},{14... | collective-permute-start | bytes 638984 | tf_op jit(solution)/shard_map/ppermute | solution.py:244
  50.5 12.7 %collective-permute-start.19 = (bf16[256,256]{1,0:T(8,128)(2,1)S(1)}, bf16[256,256]{1,0:T(8,128)(2,1)S(1)}, u32[]{:S(2)}, u32[]{:S(2)}) collective-permute-start(bf16[256,256]{1,0:T(8,128)(2,1)S(1)} %get-tuple-element.77), channel_id=1, source_target_pairs={{0,23},{1,22},{2,21},{3,20},{4,19},{5,18},{6,17},{7,16},{8,31},{9,... | collective-permute-start | bytes 393224 | tf_op jit(solution)/shard_map/ppermute | solution.py:517
  58.1 24.7 %copy-start.8 = (s32[16]{0:T(128)S(1)}, s32[16]{0:T(128)}, u32[]{:S(2)}) copy-start(s32[16]{0:T(128)} %param.26) | copy-start | bytes 196
  58.1 24.8 %copy-start.9 = (s32[16]{0:T(128)S(1)}, s32[16]{0:T(128)}, u32[]{:S(2)}) copy-start(s32[16]{0:T(128)} %param.25) | copy-start | bytes 196
  58.1 36.3 %copy-start = (bf16[256,256]{1,0:T(8,128)(2,1)S(1)}, bf16[256,256]{1,0:T(8,128)(2,1)}, u32[]{:S(2)}) copy-start(bf16[256,256]{1,0:T(8,128)(2,1)} %resident.1) | copy-start | bytes 393220
  58.1 36.3 %copy-start.2 = (bf16[2,16,1024]{2,1,0:T(8,128)(2,1)S(1)}, bf16[2,16,1024]{2,1,0:T(8,128)(2,1)}, u32[]{:S(2)}) copy-start(bf16[2,16,1024]{2,1,0:T(8,128)(2,1)} %queries.1) | copy-start | bytes 196612
  65.0 29.3 %all-to-all-start = ((bf16[32,32,256]{2,1,0:T(8,128)(2,1)}), bf16[32,32,256]{2,1,0:T(8,128)(2,1)S(1)}, u32[]{:S(2)}, u32[]{:S(2)}) async-start(bf16[32,32,256]{2,1,0:T(8,128)(2,1)} %get-tuple-element.103), calls=%async_computation | async-start | bytes 1048576 | tf_op jit(solution)/shard_map/all_to_all | solution.py:543
